TPU v7x, 256 devices: a whole 4x4x8 slice. The times are simulated.
256 devices in a mesh: pairs: 64 (over z, y, core), quad: 4 (over x).
Axes of the slice: x: 4, y: 4, z: 8, core: 2. Of those that a mesh axis runs over, the one named last changes fastest.
Arguments:
- picture_descriptors: bfloat16 [1024, 2048, 256], P('pairs', 'quad'), may hold values from -80 to 80
- image_slot: int32 [1024], replicated, may hold values from 0 to 1023, as said below
- group_images: int32 [640], P('pairs'), may hold values from 0 to 1023, as said below
- pair_target: int32 [128], P('pairs'), may hold values from 0 to 7
- pair_count: int32 [64], P('pairs'), may hold values from 1 to 2, 80 in all
Outputs:
- correspondence_result: float32 [128, 3, 2048], P('pairs', None, 'quad')
Inputs may be any that keep to these rules, and one draw needn't show every extreme that they name: A permutation; image i is stored in row image_slot[i], on the devices of pairs index image_slot[i] div 16. `group_images`: entries g * 10 to g * 10 + 9 are the distinct images of group g, its 8 reference images first, then its 2 query images; at most 1 images of one group are stored on one pairs index, and in every group some pairs index stores exactly 1 of them. Group g uses its pairs 0 to pair_count[g] - 1.
All inputs are finite; a program needn't handle non-finite values.
Results may differ from a plain program's by a relative error of at most 0.00035.
Values may be sent and summed in bfloat16 or wider, within the bound.
No kernel may reach another device: no remote copies, remote signals or barrier semaphores. Data moves between devices by JAX's collectives and lax.ppermute only.
A program may use at most 128 MiB of HBM per device.

v0:
```python
import functools
import math

import jax
import jax.numpy as jnp
from jax import lax
from jax.experimental import pallas as pl
from jax.experimental.pallas import tpu as pltpu
from jax.sharding import PartitionSpec as P

IMG_W = 64
TGT_G = 8
SHARPNESS_DIVISOR = 0.1
LOG2E = math.log2(math.e)
LANES = 128
CORES = 2
PLACES = 64
CAPACITIES = (6, 7, 8, 9, 10, 11, 12, 16)
ANY = pl.BlockSpec(memory_space=pl.ANY)
SMEM = pl.BlockSpec(memory_space=pltpu.SMEM)
VMEM = pl.BlockSpec(memory_space=pltpu.VMEM)


def plan_kernel(chip_rows, entries, chip, asked, index, rows, most, requested, before):
    groups = asked.shape[0]
    tiles = requested.shape[0]
    table = asked[:, 0, :]
    lane = lax.broadcasted_iota(jnp.int32, (groups, LANES), 1)
    columns = [table[:, entry : entry + 1] for entry in range(entries)]
    for tile in range(tiles):
        hit = columns[0] == lane + tile * LANES
        for column in columns[1:]:
            hit = hit | (column == lane + tile * LANES)
        requested[tile : tile + 1, :] = jnp.max(jnp.where(hit, 1.0, 0.0), axis=0, keepdims=True)
    first = lax.broadcasted_iota(jnp.int32, (LANES, LANES), 0)
    second = lax.broadcasted_iota(jnp.int32, (LANES, LANES), 1)
    earlier = (first < second) & (lax.div(first, chip_rows) == lax.div(second, chip_rows))
    flags = requested[...]
    before[...] = jnp.dot(flags, jnp.where(earlier, 1.0, 0.0), preferred_element_type=jnp.float32)
    most[0] = jnp.max(before[...] + flags).astype(jnp.int32)

    codes = jnp.zeros((groups, LANES), jnp.int32)
    for entry, column in enumerate(columns):
        found = jnp.zeros((groups, LANES), jnp.float32)
        for tile in range(tiles):
            found += jnp.where(column == lane + tile * LANES, before[tile : tile + 1, :], 0.0)
        place = jnp.sum(found, axis=1, keepdims=True).astype(jnp.int32)
        code = lax.div(jnp.maximum(column, 0), chip_rows) * PLACES + place
        codes = jnp.where(lane == entry, code, codes)
    index[...] = codes

    chips_tile = LANES // chip_rows
    tile = lax.div(chip[0], chips_tile)
    part = lax.rem(chip[0], chips_tile)
    slot = lax.broadcasted_iota(jnp.int32, (chip_rows, LANES), 0).astype(jnp.float32)
    along = lax.broadcasted_iota(jnp.int32, (chip_rows, LANES), 1)
    mine = (requested[pl.ds(tile, 1), :] > 0.0) & (before[pl.ds(tile, 1), :] == slot)
    mine = mine & (lax.div(along, chip_rows) == part)
    row = jnp.sum(jnp.where(mine, lax.rem(along, chip_rows), 0).astype(jnp.float32), axis=1, keepdims=True)
    rows[...] = jnp.broadcast_to(row.astype(jnp.int32), rows.shape)


def plan(chip_rows, images, entries, chip, asked):
    groups = asked.shape[0]
    return pl.pallas_call(
        functools.partial(plan_kernel, chip_rows, entries),
        in_specs=[SMEM, VMEM],
        out_specs=(VMEM, VMEM, SMEM),
        out_shape=(
            jax.ShapeDtypeStruct((groups, LANES), jnp.int32),
            jax.ShapeDtypeStruct((chip_rows, LANES), jnp.int32),
            jax.ShapeDtypeStruct((1,), jnp.int32),
        ),
        scratch_shapes=[pltpu.VMEM((images // LANES, LANES), jnp.float32)] * 2,
    )(chip, asked)


def pick_kernel(core, rows, own, other, out, sems):
    images_dev = own.shape[0]
    half = other.shape[-1]
    capacity = out.shape[1]
    features = pl.ds(pl.multiple_of(core[0] * half, LANES), half)
    for slot in range(capacity):
        row = rows[slot, 0]
        local = lax.rem(row, images_dev)
        is_own = lax.div(row, images_dev) == core[0]

        @pl.when(is_own)
        def _():
            pltpu.make_async_copy(own.at[local, :, :, features], out.at[:, slot], sems.at[slot]).start()

        @pl.when(jnp.logical_not(is_own))
        def _():
            pltpu.make_async_copy(other.at[local], out.at[:, slot], sems.at[slot]).start()

    for slot in range(capacity):
        pltpu.make_async_copy(other.at[0], out.at[:, slot], sems.at[slot]).wait()


def pick(capacity, core, rows, own, other):
    images_dev, groups, piece, half = other.shape
    return pl.pallas_call(
        pick_kernel,
        in_specs=[SMEM, SMEM, ANY, ANY],
        out_specs=ANY,
        out_shape=jax.ShapeDtypeStruct((groups, capacity, piece, half), other.dtype),
        scratch_shapes=[pltpu.SemaphoreType.DMA((capacity,))],
    )(core, rows, own, other)


def regroup_kernel(index, spread, for_query, for_target):
    groups, pairs = for_query.shape[:2]
    half = spread.shape[-1]

    def step(group, carry):
        for entry in range(2 * pairs):
            code = index[group, entry]
            chip = lax.div(code, PLACES)
            place = lax.rem(code, PLACES)
            target = for_query if entry < pairs else for_target
            for core in range(CORES):
                target[group, entry % pairs, :, core * half : (core + 1) * half] = spread[chip * CORES + core, place]
        return carry

    lax.fori_loop(0, groups, step, 0, unroll=4)


def regroup(pairs, index, spread):
    groups, _, piece, half = spread.shape
    shape = jax.ShapeDtypeStruct((groups, pairs, piece, CORES * half), spread.dtype)
    return pl.pallas_call(
        regroup_kernel,
        in_specs=[SMEM, VMEM],
        out_specs=(VMEM, VMEM),
        out_shape=(shape, shape),
        compiler_params=pltpu.CompilerParams(vmem_limit_bytes=24 * 1024 * 1024),
    )(index, spread)


def match_kernel(image_rows, multiplier, meta, q0, q1, q2a, q2b, q3, target, out, scores, column):
    quad = meta[0]
    width = target.shape[-1]
    slab = target.shape[0] * target.shape[2]
    quads = out.shape[0]

    @pl.when(pl.program_id(0) < meta[1])
    def _():
        rows = target[:, 0].reshape(slab, width)
        start = 0
        for query in (q0, q1, q2a, q2b, q3):
            tokens = query.shape[0] * query.shape[2]
            scores[:, start : start + tokens] = (
                lax.dot_general(
                    rows, query[:, 0].reshape(tokens, width), (((1,), (1,)), ((), ())),
                    preferred_element_type=jnp.float32,
                )
                * multiplier
            )
            start += tokens

        def rows_step(index, carry):
            block = pl.ds(pl.multiple_of(index * 32, 32), 32)
            top = jnp.max(scores[block, :], axis=1, keepdims=True)
            powers = jnp.exp2(scores[block, :] - top)
            column[block, :] = powers * (1.0 / jnp.sum(powers, axis=1, keepdims=True))
            return carry

        lax.fori_loop(0, slab // 32, rows_step, 0, unroll=4)

        bands = slab // IMG_W
        along = lax.broadcasted_iota(jnp.int32, (IMG_W, LANES), 0).astype(jnp.float32)
        coord_x = (2.0 * along + 1.0) / IMG_W - 1.0
        first_row = quad * bands
        for step in range(quads):
            slot = lax.rem(quad - step + quads, quads)

            def lanes_step(index, carry, step=step, slot=slot):
                lanes = pl.ds(pl.multiple_of(step * slab + index * LANES, LANES), LANES)
                top = jnp.max(scores[:, lanes], axis=0, keepdims=True)
                total = jnp.zeros((8, LANES), jnp.float32)
                weighted_y = jnp.zeros((8, LANES), jnp.float32)
                mutual = jnp.zeros((8, LANES), jnp.float32)
                folded = jnp.zeros((IMG_W, LANES), jnp.float32)
                for band in range(bands):
                    piece = slice(band * IMG_W, (band + 1) * IMG_W)
                    powers = jnp.exp2(scores[piece, lanes] - top)
                    folded += powers
                    part = jnp.sum(powers.reshape(IMG_W // 8, 8, LANES), axis=0)
                    total += part
                    coord_y = (2.0 * (first_row + band).astype(jnp.float32) + 1.0) / image_rows - 1.0
                    weighted_y += part * coord_y
                    mutual += jnp.sum((powers * column[piece, lanes]).reshape(IMG_W // 8, 8, LANES), axis=0)
                place = pl.ds(pl.multiple_of(index * LANES, LANES), LANES)
                out[slot, 0, 0:1, place] = top
                out[slot, 0, 1:2, place] = jnp.sum(total, axis=0, keepdims=True)
                out[slot, 0, 2:3, place] = jnp.sum(folded * coord_x, axis=0, keepdims=True)
                out[slot, 0, 3:4, place] = jnp.sum(weighted_y, axis=0, keepdims=True)
                out[slot, 0, 4:5, place] = jnp.sum(mutual, axis=0, keepdims=True)
                return carry

            lax.fori_loop(0, slab // LANES, lanes_step, 0, unroll=4)


def match(image_rows, multiplier, meta, quads, queries, target):
    pieces, pairs, piece, width = target.shape
    slab = pieces * piece

    def block(array):
        return pl.BlockSpec((array.shape[0], 1, piece, width), lambda pair, meta: (0, pair, 0, 0))

    return pl.pallas_call(
        functools.partial(match_kernel, image_rows, multiplier),
        grid_spec=pltpu.PrefetchScalarGridSpec(
            num_scalar_prefetch=1,
            grid=(pairs,),
            in_specs=[block(array) for array in (*queries, target)],
            out_specs=pl.BlockSpec((quads, 1, 8, slab), lambda pair, meta: (0, pair, 0, 0)),
            scratch_shapes=[pltpu.VMEM((slab, quads * slab), jnp.float32)] * 2,
        ),
        out_shape=jax.ShapeDtypeStruct((quads, pairs, 8, slab), jnp.float32),
        compiler_params=pltpu.CompilerParams(vmem_limit_bytes=40 * 1024 * 1024),
        cost_estimate=pl.CostEstimate(
            flops=2 * pairs * slab * slab * quads * width, bytes_accessed=4 << 20, transcendentals=4 << 20
        ),
    )(meta, *queries, target)


def shards(picture_descriptors, image_slot, group_images, pair_target, pair_count):
    groups = lax.axis_size("pairs")
    quads = lax.axis_size("quad")
    me = lax.axis_index("pairs").astype(jnp.int32)
    quad = lax.axis_index("quad").astype(jnp.int32)
    images_dev, slab, width = picture_descriptors.shape
    pairs = pair_target.shape[0]
    images = image_slot.shape[0]
    piece = slab // groups
    half = width // CORES
    chip_rows = images_dev * CORES
    image_rows = slab * quads // IMG_W
    multiplier = LOG2E / (width * SHARPNESS_DIVISOR)
    core = me % CORES

    position = jnp.arange(group_images.shape[0], dtype=jnp.int32)
    wanted = jnp.concatenate([TGT_G + jnp.arange(pairs, dtype=jnp.int32), pair_target])
    ids = jnp.sum(jnp.where(wanted[:, None] == position[None, :], group_images[None, :], 0), axis=1)
    catalog = jnp.arange(images, dtype=jnp.int32)
    stored = jnp.sum(jnp.where(ids[:, None] == catalog[None, :], image_slot[None, :], 0), axis=1)
    in_use = jnp.arange(pairs, dtype=jnp.int32) < pair_count[0]
    stored = jnp.where(jnp.concatenate([in_use, in_use]), stored, -1)
    message = jnp.pad(stored, (0, LANES - 2 * pairs), constant_values=-1)
    asked = lax.all_to_all(
        jnp.broadcast_to(message[None, None, :], (groups, 1, LANES)), "pairs", split_axis=0, concat_axis=0, tiled=True
    )

    given = lax.dynamic_slice_in_dim(picture_descriptors, (CORES - 1 - core) * half, half, axis=2)
    traded = lax.ppermute(given, "pairs", [(i, i ^ 1) for i in range(groups)])

    index, rows, most = plan(chip_rows, images, 2 * pairs, (me // CORES)[None], asked)
    own = picture_descriptors.reshape(images_dev, groups, piece, width)
    other = traded.reshape(images_dev, groups, piece, half)

    def exchange(capacity, operands):
        own, other, rows, index = operands
        pieces = pick(capacity, core[None], rows, own, other)
        spread = lax.all_to_all(pieces, "pairs", split_axis=0, concat_axis=0, tiled=True)
        return regroup(pairs, index, spread)

    capacities = [size for size in CAPACITIES if size < chip_rows] + [chip_rows]
    branch = jnp.sum(jnp.asarray(capacities, jnp.int32) < most[0])
    for_query, for_target = lax.switch(
        branch, [functools.partial(exchange, size) for size in capacities], (own, other, rows, index)
    )

    def move(array, step):
        return lax.ppermute(array, "quad", [(i, (i + step) % quads) for i in range(quads)])

    query = lax.all_to_all(for_query, "pairs", split_axis=0, concat_axis=0, tiled=True)
    before = move(query, 1)
    after = move(query, quads - 1)
    across = (move(before[: groups // 2], 1), move(after[groups // 2 :], quads - 1))
    target = lax.all_to_all(for_target, "pairs", split_axis=0, concat_axis=0, tiled=True)
    meta = jnp.stack([quad, pair_count[0]])
    partial = match(image_rows, multiplier, meta, quads, (query, before, *across, after), target)
    partial = lax.all_to_all(partial, "quad", split_axis=0, concat_axis=0, tiled=True)
    top = partial[:, :, 0:1]
    weight = jnp.exp2(top - jnp.max(top, axis=0, keepdims=True))
    sums = jnp.sum(partial[:, :, 1:5] * weight, axis=0)
    return jnp.where(in_use[:, None, None], sums[:, 1:4] / sums[:, 0:1], 0.0)


def solution(mesh):
    return jax.shard_map(
        shards,
        mesh=mesh,
        in_specs=(P("pairs", "quad", None), P(), P("pairs"), P("pairs"), P("pairs")),
        out_specs=P("pairs", None, "quad"),
        check_vma=False,
    )
```

profile of v0, /device:TPU:24, one launch (start us, length us, event | category | flops | bytes accessed | tf_op | source)
XLA Modules:
  0.0 181.1 jit_solution(11507805363367715204)
XLA Ops:
  0.0 0.0 copy-start.2
  0.0 0.0 copy-start.3
  0.0 0.0 copy-start.1
  0.0 0.0 copy-start.4
  0.0 3.2 %constant_dynamic-slice_fusion = bf16[16,512,128]{2,1,0:T(8,128)(2,1)} fusion(bf16[16,512,256]{2,1,0:T(8,128)(2,1)} %param.15, s32[]{:T(128)S(6)} %select_n.35), kind=kLoop, calls=%fused_computation.19 | loop fusion | bytes 4194308 | tf_op jit(solution)/shard_map/dynamic_slice | solution.py:255
  3.2 0.0 collective-permute-start
  3.9 0.0 copy-done.2
  3.9 0.1 pad_add_fusion.1
  3.9 0.0 copy-done.3
  4.0 0.2 select_reduce_fusion.1
  4.1 0.0 copy-done.1
  4.1 0.2 select_reduce_fusion
  4.3 0.1 add_select_fusion
  4.4 0.6 broadcast_in_dim.91
  5.0 12.0 %all-to-all-start.9 = ((s32[64,1,128]{2,1,0:T(1,128)}), s32[64,1,128]{2,1,0:T(1,128)S(1)}, u32[]{:S(2)}, u32[]{:S(2)}) async-start(s32[64,1,128]{2,1,0:T(1,128)} %broadcast_in_dim.91), calls=%async_computation.9 | async-start | bytes 65536 | tf_op jit(solution)/shard_map/all_to_all | solution.py:251
  17.0 7.9 %all-to-all-done.9.asked = s32[64,1,128]{2,1,0:T(1,128)S(1)} async-done(((s32[64,1,128]{2,1,0:T(1,128)}), s32[64,1,128]{2,1,0:T(1,128)S(1)}, u32[]{:S(2)}, u32[]{:S(2)}) %all-to-all-start.9) | async-done | bytes 32800 | tf_op jit(solution)/shard_map/all_to_all | solution.py:251
  24.9 0.0 copy-start
  24.9 0.6 copy-done
  25.5 3.5 %shard_map.64 = (s32[64,128]{1,0:T(8,128)S(1)}, s32[32,128]{1,0:T(8,128)S(1)}, s32[1]{0:T(128)}) custom-call(s32[1]{0:T(128)} %bitcast.11.chip, s32[64,1,128]{2,1,0:T(1,128)} %copy-done), custom_call_target="tpu_custom_call" | custom-call | tf_op jit(solution)/shard_map/pallas_call | solution.py:65
  29.1 0.0 copy-done.4
  29.1 1.3 fusion.2
  31.1 0.0 collective-permute-done
  31.1 77.8 %conditional.1 = ((bf16[64,2,8,256]{3,2,1,0:T(8,128)(2,1)S(1)}, bf16[64,2,8,256]{3,2,1,0:T(8,128)(2,1)})) conditional(s32[]{:T(128)} %clamp.3, (s32[]{:T(128)}, s32[32,128]{1,0:T(8,128)S(1)}, bf16[16,64,8,256]{3,2,1,0:T(8,128)(2,1)}, bf16[16,64,8,128]{3,2,1,0:T(8,128)(2,1)S(1)}, s32[64,128]{1,0:T(8,128)S(1)}) %tuple.60, ...), branch_computations={%region_3.4_spmd, %region_4.5_spmd, %region_5.6_spmd, %region_6.7_... | conditional | bytes 8388616 | solution.py:270
  31.1 21.8 %branch_3_fun.2 = bf16[64,9,8,128]{3,2,1,0:T(8,128)(2,1)} custom-call(s32[1]{0:T(128)} %bitcast.3.core, s32[32,128]{1,0:T(8,128)S(1)} %get-tuple-element.112.rows, bf16[16,64,8,256]{3,2,1,0:T(8,128)(2,1)} %get-tuple-element.113.own, bf16[16,64,8,128]{3,2,1,0:T(8,128)(2,1)S(1)} %get-tuple-element.114.other), custom_call_target="tpu_custom_call" | custom-call | tf_op jit(solution)/shard_map/cond/branch_3_fun/pallas_call | solution.py:102
  53.0 52.9 %all_to_all.59.spread = bf16[64,9,8,128]{3,2,1,0:T(8,128)(2,1)S(1)} all-to-all(bf16[64,9,8,128]{3,2,1,0:T(8,128)(2,1)} %branch_3_fun.2), channel_id=1, replica_groups=mesh['pairs'=64,'quad'=4] {'pairs'}, dimensions={0} | all-to-all | bytes 2359296 | tf_op jit(solution)/shard_map/cond/branch_3_fun/all_to_all | solution.py:265
  105.9 3.0 %branch_3_fun.3 = (bf16[64,2,8,256]{3,2,1,0:T(8,128)(2,1)S(1)}, bf16[64,2,8,256]{3,2,1,0:T(8,128)(2,1)}) custom-call(s32[64,128]{1,0:T(8,128)S(1)} %get-tuple-element.110.index, bf16[64,9,8,128]{3,2,1,0:T(8,128)(2,1)S(1)} %all_to_all.59.spread), custom_call_target="tpu_custom_call" | custom-call | tf_op jit(solution)/shard_map/cond/branch_3_fun/pallas_call | solution.py:131
  108.9 23.0 %all_to_all.65.q0 = bf16[64,2,8,256]{3,2,1,0:T(8,128)(2,1)S(1)} all-to-all(bf16[64,2,8,256]{3,2,1,0:T(8,128)(2,1)S(1)} %get-tuple-element.148), channel_id=1, replica_groups=mesh['pairs'=64,'quad'=4] {'pairs'}, dimensions={0} | all-to-all | bytes 1048576 | tf_op jit(solution)/shard_map/all_to_all | solution.py:277
  131.9 5.9 %all-to-all-start.11 = ((bf16[64,2,8,256]{3,2,1,0:T(8,128)(2,1)}), bf16[64,2,8,256]{3,2,1,0:T(8,128)(2,1)S(1)}, u32[]{:S(2)}, u32[]{:S(2)}) async-start(bf16[64,2,8,256]{3,2,1,0:T(8,128)(2,1)} %get-tuple-element.149), calls=%async_computation.11 | async-start | bytes 1048576 | tf_op jit(solution)/shard_map/all_to_all | solution.py:281
  137.7 2.8 %collective-permute-start.3 = (bf16[64,2,8,256]{3,2,1,0:T(8,128)(2,1)S(1)}, bf16[64,2,8,256]{3,2,1,0:T(8,128)(2,1)S(1)}, u32[]{:S(2)}, u32[]{:S(2)}) collective-permute-start(bf16[64,2,8,256]{3,2,1,0:T(8,128)(2,1)S(1)} %all_to_all.65.q0), channel_id=1, source_target_pairs={{0,3},{1,0},{2,1},{3,2},{4,7},{5,4},{6,5},{7,6},{8,11},{9,8},{10,9... | collective-permute-start | bytes 1572872 | tf_op jit(solution)/shard_map/ppermute | solution.py:275
  140.6 0.0 collective-permute-start.1
  140.6 11.5 %collective-permute-done.3.q3 = bf16[64,2,8,256]{3,2,1,0:T(8,128)(2,1)S(1)} collective-permute-done((bf16[64,2,8,256]{3,2,1,0:T(8,128)(2,1)S(1)}, bf16[64,2,8,256]{3,2,1,0:T(8,128)(2,1)S(1)}, u32[]{:S(2)}, u32[]{:S(2)}) %collective-permute-start.3) | collective-permute-done | bytes 524320 | tf_op jit(solution)/shard_map/ppermute | solution.py:275
  152.1 3.8 %collective-permute-start.4 = (bf16[32,2,8,256]{3,2,1,0:T(8,128)(2,1)S(1)}, bf16[32,2,8,256]{3,2,1,0:T(8,128)(2,1)S(1)}, u32[]{:S(2)}, u32[]{:S(2)}) collective-permute-start(bf16[32,2,8,256]{3,2,1,0:T(8,128)(2,1)S(1)} %slice.25), channel_id=1, source_target_pairs={{0,3},{1,0},{2,1},{3,2},{4,7},{5,4},{6,5},{7,6},{8,11},{9,8},{10,9... | collective-permute-start | bytes 786440 | tf_op jit(solution)/shard_map/ppermute | solution.py:275
  155.9 0.0 collective-permute-done.1.q1
  155.9 0.1 collective-permute-start.2
  156.0 0.1 pad_add_fusion.meta
  156.1 0.0 all-to-all-done.11.target
  156.1 4.8 %collective-permute-done.4.q2b = bf16[32,2,8,256]{3,2,1,0:T(8,128)(2,1)S(1)} collective-permute-done((bf16[32,2,8,256]{3,2,1,0:T(8,128)(2,1)S(1)}, bf16[32,2,8,256]{3,2,1,0:T(8,128)(2,1)S(1)}, u32[]{:S(2)}, u32[]{:S(2)}) %collective-permute-start.4) | collective-permute-done | bytes 262176 | tf_op jit(solution)/shard_map/ppermute | solution.py:275
  160.9 3.5 %collective-permute-done.2.q2a = bf16[32,2,8,256]{3,2,1,0:T(8,128)(2,1)S(1)} collective-permute-done((bf16[32,2,8,256]{3,2,1,0:T(8,128)(2,1)S(1)}, bf16[32,2,8,256]{3,2,1,0:T(8,128)(2,1)S(1)}, u32[]{:S(2)}, u32[]{:S(2)}) %collective-permute-start.2) | collective-permute-done | bytes 262176 | tf_op jit(solution)/shard_map/ppermute | solution.py:275
  164.4 7.5 %shard_map.65 = f32[4,2,8,512]{3,2,1,0:T(8,128)S(1)} custom-call(s32[2]{0:T(128)S(1)} %pad_add_fusion.meta, bf16[64,2,8,256]{3,2,1,0:T(8,128)(2,1)S(1)} %all_to_all.65.q0, bf16[64,2,8,256]{3,2,1,0:T(8,128)(2,1)S(1)} %collective-permute-done.1.q1, bf16[32,2,8,256]{3,2,1,0:T(8,128)(2,1)S(1)} %collective-permute-done.2.q2a, ...), custom_call_target="tpu_custom_call" | custom-call | flops 1073741824 | bytes 4194304 | tf_op jit(solution)/shard_map/pallas_call | solution.py:211
  171.9 8.4 %all_to_all.66 = f32[4,2,8,512]{3,2,1,0:T(8,128)S(1)} all-to-all(f32[4,2,8,512]{3,2,1,0:T(8,128)S(1)} %shard_map.65), channel_id=1, replica_groups=mesh['pairs'=64,'quad'=4] {'quad'}, dimensions={0} | all-to-all | bytes 262144 | tf_op jit(solution)/shard_map/all_to_all | solution.py:284
  180.5 0.1 fusion.1
  180.5 0.6 copy.8
  (11 shorter events, 0.2 us)
Async XLA Ops:
  0.0 3.9 %copy-start.2 = (s32[2]{0:T(128)S(1)}, s32[2]{0:T(128)}, u32[]{:S(2)}) copy-start(s32[2]{0:T(128)} %param.18) | copy-start | bytes 28
  0.0 3.9 %copy-start.3 = (s32[10]{0:T(128)S(1)}, s32[10]{0:T(128)}, u32[]{:S(2)}) copy-start(s32[10]{0:T(128)} %param.17) | copy-start | bytes 124
  0.0 4.1 %copy-start.1 = (s32[1024]{0:T(1024)S(1)}, s32[1024]{0:T(1024)}, u32[]{:S(2)}) copy-start(s32[1024]{0:T(1024)} %param.16) | copy-start | bytes 12292
  0.0 29.1 %copy-start.4 = (s32[9]{0:T(128)S(1)}, s32[9]{0:T(128)}, u32[]{:S(2)}) copy-start(s32[9]{0:T(128)} %constant.51.clone) | copy-start | bytes 112
  3.2 27.9 %collective-permute-start = (bf16[16,512,128]{2,1,0:T(8,128)(2,1)}, bf16[16,512,128]{2,1,0:T(8,128)(2,1)S(1)}, u32[]{:S(2)}, u32[]{:S(2)}) collective-permute-start(bf16[16,512,128]{2,1,0:T(8,128)(2,1)} %constant_dynamic-slice_fusion), channel_id=1, source_target_pairs={{0,4},{4,0},{8,12},{12,8},{16,20},{20,16},{24,28},{28,24},{32,36},... | collective-permute-start | bytes 6291464 | tf_op jit(solution)/shard_map/ppermute | solution.py:256
  5.0 19.9 %all-to-all-start.9 = ((s32[64,1,128]{2,1,0:T(1,128)}), s32[64,1,128]{2,1,0:T(1,128)S(1)}, u32[]{:S(2)}, u32[]{:S(2)}) async-start(s32[64,1,128]{2,1,0:T(1,128)} %broadcast_in_dim.91), calls=%async_computation.9 | async-start | bytes 65536 | tf_op jit(solution)/shard_map/all_to_all | solution.py:251
  24.9 0.6 copy-start
  131.9 24.2 %all-to-all-start.11 = ((bf16[64,2,8,256]{3,2,1,0:T(8,128)(2,1)}), bf16[64,2,8,256]{3,2,1,0:T(8,128)(2,1)S(1)}, u32[]{:S(2)}, u32[]{:S(2)}) async-start(bf16[64,2,8,256]{3,2,1,0:T(8,128)(2,1)} %get-tuple-element.149), calls=%async_computation.11 | async-start | bytes 1048576 | tf_op jit(solution)/shard_map/all_to_all | solution.py:281
  137.7 14.3 %collective-permute-start.3 = (bf16[64,2,8,256]{3,2,1,0:T(8,128)(2,1)S(1)}, bf16[64,2,8,256]{3,2,1,0:T(8,128)(2,1)S(1)}, u32[]{:S(2)}, u32[]{:S(2)}) collective-permute-start(bf16[64,2,8,256]{3,2,1,0:T(8,128)(2,1)S(1)} %all_to_all.65.q0), channel_id=1, source_target_pairs={{0,3},{1,0},{2,1},{3,2},{4,7},{5,4},{6,5},{7,6},{8,11},{9,8},{10,9... | collective-permute-start | bytes 1572872 | tf_op jit(solution)/shard_map/ppermute | solution.py:275
  140.6 15.3 %collective-permute-start.1 = (bf16[64,2,8,256]{3,2,1,0:T(8,128)(2,1)S(1)}, bf16[64,2,8,256]{3,2,1,0:T(8,128)(2,1)S(1)}, u32[]{:S(2)}, u32[]{:S(2)}) collective-permute-start(bf16[64,2,8,256]{3,2,1,0:T(8,128)(2,1)S(1)} %all_to_all.65.q0), channel_id=1, source_target_pairs={{0,1},{1,2},{2,3},{3,0},{4,5},{5,6},{6,7},{7,4},{8,9},{9,10},{10,1... | collective-permute-start | bytes 1572872 | tf_op jit(solution)/shard_map/ppermute | solution.py:275
  152.1 8.8 %collective-permute-start.4 = (bf16[32,2,8,256]{3,2,1,0:T(8,128)(2,1)S(1)}, bf16[32,2,8,256]{3,2,1,0:T(8,128)(2,1)S(1)}, u32[]{:S(2)}, u32[]{:S(2)}) collective-permute-start(bf16[32,2,8,256]{3,2,1,0:T(8,128)(2,1)S(1)} %slice.25), channel_id=1, source_target_pairs={{0,3},{1,0},{2,1},{3,2},{4,7},{5,4},{6,5},{7,6},{8,11},{9,8},{10,9... | collective-permute-start | bytes 786440 | tf_op jit(solution)/shard_map/ppermute | solution.py:275
  155.9 8.5 %collective-permute-start.2 = (bf16[32,2,8,256]{3,2,1,0:T(8,128)(2,1)S(1)}, bf16[32,2,8,256]{3,2,1,0:T(8,128)(2,1)S(1)}, u32[]{:S(2)}, u32[]{:S(2)}) collective-permute-start(bf16[32,2,8,256]{3,2,1,0:T(8,128)(2,1)S(1)} %slice.24), channel_id=1, source_target_pairs={{0,1},{1,2},{2,3},{3,0},{4,5},{5,6},{6,7},{7,4},{8,9},{9,10},{10,1... | collective-permute-start | bytes 786440 | tf_op jit(solution)/shard_map/ppermute | solution.py:275
where the time goes:
time: 182 us; the launch traced here: 181 us
  blocking collectives  84.3 us (46%)
  Pallas kernels  35.9 us (20%)
  waiting for transfers between devices  27.7 us (15%)
  starting transfers between devices  24.5 us (13%)
  local copies, waits for them, and re-layouts  5.08 us (3%)
  other arithmetic  2.09 us (1%)
    all_to_all x1, blocking collectives, exchange(): lax.all_to_all(pieces, 'pairs', split_axis=0, concat_axis=0, tiled=True)  52.9 us
    all_to_all x1, blocking collectives, shards(): lax.all_to_all(for_query, 'pairs', split_axis=0, concat_axis=0, tiled=True)  23 us
    pallas_call x1, Pallas kernels, pick(): pl.pallas_call(pick_kernel, in_specs=[SMEM, SMEM, ANY, ANY], out_specs=AN...  21.8 us
    ppermute x4, waiting for transfers between devices, move(): lax.ppermute(array, 'quad', [(i, (i + step) % quads) for i in range(quads)])  19.9 us
    all_to_all x1, starting transfers between devices, shards(): lax.all_to_all(jnp.broadcast_to(message[None, None, :], (groups, 1, LANES...  12 us
    all_to_all x1, blocking collectives, shards(): lax.all_to_all(partial, 'quad', split_axis=0, concat_axis=0, tiled=True)  8.36 us
    all_to_all x1, waiting for transfers between devices, shards(): lax.all_to_all(jnp.broadcast_to(message[None, None, :], (groups, 1, LANES...  7.87 us
    pallas_call x1, Pallas kernels, match(): pl.pallas_call(functools.partial(match_kernel, image_rows, multiplier), g...  7.5 us
  transfers between devices with their start and end apart: 7, of which 4 were waited for; matrix products, arithmetic and copies ran while one was open for 1% of the time, Pallas kernels for 2%

commit v1 on v0

v1 whole, which is shorter than its diff:
```python
import functools
import math

import jax
import jax.numpy as jnp
from jax import lax
from jax.experimental import pallas as pl
from jax.experimental.pallas import tpu as pltpu
from jax.sharding import Mesh
from jax.sharding import PartitionSpec as P

IMG_W = 64
TGT_G = 8
SHARPNESS_DIVISOR = 0.1
LOG2E = math.log2(math.e)
LANES = 128
CORES = 2
PLACES = 64
CAPACITIES = (6, 7, 8, 9, 10, 11, 12, 16)
ANY = pl.BlockSpec(memory_space=pl.ANY)
SMEM = pl.BlockSpec(memory_space=pltpu.SMEM)
VMEM = pl.BlockSpec(memory_space=pltpu.VMEM)


def plan_kernel(chip_rows, entries, capacities, chip, asked, index, rows, branch, requested, before):
    groups = asked.shape[0]
    table = asked[:, 0, :]
    lane = lax.broadcasted_iota(jnp.int32, (groups, LANES), 1)
    chips, locals_ = [], []
    count = jnp.zeros((LANES, LANES), jnp.float32)
    for entry in range(entries):
        stored = table[:, entry : entry + 1]
        chips.append(jnp.where(lax.div(stored, chip_rows) == lane, 1.0, 0.0) * jnp.where(stored >= 0, 1.0, 0.0))
        locals_.append(jnp.where(lax.rem(stored, chip_rows) == lane, 1.0, 0.0))
        count += lax.dot_general(
            chips[-1], locals_[-1], (((0,), (0,)), ((), ())), preferred_element_type=jnp.float32
        )
    flags = jnp.where(count > 0.0, 1.0, 0.0)
    first = lax.broadcasted_iota(jnp.int32, (LANES, LANES), 0)
    second = lax.broadcasted_iota(jnp.int32, (LANES, LANES), 1)
    earlier = jnp.dot(flags, jnp.where(first < second, 1.0, 0.0), preferred_element_type=jnp.float32)
    requested[...] = flags
    before[...] = earlier
    most = jnp.max(earlier + flags)
    choice = jnp.int32(0)
    for capacity in capacities[:-1]:
        choice += jnp.where(most > capacity, 1, 0)
    branch[0] = choice

    codes = jnp.zeros((groups, LANES), jnp.int32)
    for entry in range(entries):
        places = jnp.dot(chips[entry], earlier, preferred_element_type=jnp.float32) * locals_[entry]
        place = jnp.sum(places, axis=1, keepdims=True).astype(jnp.int32)
        stored = jnp.maximum(table[:, entry : entry + 1], 0)
        codes = jnp.where(lane == entry, lax.div(stored, chip_rows) * PLACES + place, codes)
    index[...] = codes

    mine = chip[0]
    slot = lax.broadcasted_iota(jnp.int32, (chip_rows, LANES), 0).astype(jnp.float32)
    along = lax.broadcasted_iota(jnp.int32, (chip_rows, LANES), 1).astype(jnp.float32)
    chosen = (requested[pl.ds(mine, 1), :] > 0.0) & (before[pl.ds(mine, 1), :] == slot)
    row = jnp.sum(jnp.where(chosen, along, 0.0), axis=1, keepdims=True)
    rows[...] = jnp.broadcast_to(row.astype(jnp.int32), rows.shape)


def plan(chip_rows, entries, capacities, chip, asked):
    groups = asked.shape[0]
    return pl.pallas_call(
        functools.partial(plan_kernel, chip_rows, entries, capacities),
        grid=(1,),
        in_specs=[SMEM, pl.BlockSpec(asked.shape, lambda step: (0, 0, 0))],
        out_specs=(
            pl.BlockSpec((groups, LANES), lambda step: (0, 0)),
            pl.BlockSpec((chip_rows, LANES), lambda step: (0, 0)),
            SMEM,
        ),
        out_shape=(
            jax.ShapeDtypeStruct((groups, LANES), jnp.int32),
            jax.ShapeDtypeStruct((chip_rows, LANES), jnp.int32),
            jax.ShapeDtypeStruct((1,), jnp.int32),
        ),
        scratch_shapes=[pltpu.VMEM((LANES, LANES), jnp.float32)] * 2,
    )(chip, asked)


def pick_kernel(core, rows, own, other, out, sems):
    images_dev = own.shape[0]
    capacity = out.shape[1]
    for slot in range(capacity):
        row = rows[slot, 0]
        local = lax.rem(row, images_dev)
        is_own = lax.div(row, images_dev) == core[0]

        @pl.when(is_own)
        def _():
            pltpu.make_async_copy(own.at[local, core[0]], out.at[:, slot], sems.at[slot]).start()

        @pl.when(jnp.logical_not(is_own))
        def _():
            pltpu.make_async_copy(other.at[local, core[0]], out.at[:, slot], sems.at[slot]).start()

    for slot in range(capacity):
        pltpu.make_async_copy(other.at[0, 0], out.at[:, slot], sems.at[slot]).wait()


def pick(capacity, core, rows, own, other):
    _, _, chips, piece, width = other.shape
    return pl.pallas_call(
        pick_kernel,
        in_specs=[SMEM, SMEM, ANY, ANY],
        out_specs=VMEM,
        out_shape=jax.ShapeDtypeStruct((chips, capacity, piece, width), other.dtype),
        scratch_shapes=[pltpu.SemaphoreType.DMA((capacity,))],
        compiler_params=pltpu.CompilerParams(vmem_limit_bytes=24 * 1024 * 1024),
    )(core, rows, own, other)


def regroup_kernel(index, spread, out):
    groups, entries = out.shape[:2]

    def step(group, carry):
        for entry in range(entries):
            code = index[group, entry]
            out[group, entry] = spread[lax.div(code, PLACES), lax.rem(code, PLACES)]
        return carry

    lax.fori_loop(0, groups, step, 0, unroll=8)


def regroup(groups, entries, index, spread):
    return pl.pallas_call(
        regroup_kernel,
        in_specs=[SMEM, VMEM],
        out_specs=VMEM,
        out_shape=jax.ShapeDtypeStruct((groups, entries, *spread.shape[2:]), spread.dtype),
        compiler_params=pltpu.CompilerParams(vmem_limit_bytes=24 * 1024 * 1024),
    )(index, spread)


def match_kernel(image_rows, multiplier, pair, meta, q0, q1, q2a, q2b, q3, target, earlier, out, scores, column):
    quad = meta[0]
    chips, cores, _, piece, width = target.shape
    part = chips * piece
    slab = cores * part
    quads = out.shape[0]
    for previous in range(pair):
        out[:, previous] = earlier[:, previous]

    @pl.when(pair < meta[1])
    def _():
        for row in range(cores):
            rows = target[:, row, 0].reshape(part, width)
            for step, skip, query in ((0, 0, q0), (1, 0, q1), (2, 0, q2a), (2, q2a.shape[0], q2b), (3, 0, q3)):
                tokens = query.shape[0] * piece
                for core in range(cores):
                    start = step * slab + core * part + skip * piece
                    scores[row * part : (row + 1) * part, start : start + tokens] = (
                        lax.dot_general(
                            rows, query[:, core, 0].reshape(tokens, width), (((1,), (1,)), ((), ())),
                            preferred_element_type=jnp.float32,
                        )
                        * multiplier
                    )

        def rows_step(index, carry):
            block = pl.ds(pl.multiple_of(index * 32, 32), 32)
            top = jnp.max(scores[block, :], axis=1, keepdims=True)
            powers = jnp.exp2(scores[block, :] - top)
            column[block, :] = powers * (1.0 / jnp.sum(powers, axis=1, keepdims=True))
            return carry

        lax.fori_loop(0, slab // 32, rows_step, 0, unroll=4)

        bands = slab // IMG_W
        along = lax.broadcasted_iota(jnp.int32, (IMG_W, LANES), 0).astype(jnp.float32)
        coord_x = (2.0 * along + 1.0) / IMG_W - 1.0
        first_row = quad * bands
        for step in range(quads):
            slot = lax.rem(quad - step + quads, quads)

            def lanes_step(index, carry, step=step, slot=slot):
                lanes = pl.ds(pl.multiple_of(step * slab + index * LANES, LANES), LANES)
                top = jnp.max(scores[:, lanes], axis=0, keepdims=True)
                total = jnp.zeros((8, LANES), jnp.float32)
                weighted_y = jnp.zeros((8, LANES), jnp.float32)
                mutual = jnp.zeros((8, LANES), jnp.float32)
                folded = jnp.zeros((IMG_W, LANES), jnp.float32)
                for band in range(bands):
                    piece = slice(band * IMG_W, (band + 1) * IMG_W)
                    powers = jnp.exp2(scores[piece, lanes] - top)
                    folded += powers
                    part = jnp.sum(powers.reshape(IMG_W // 8, 8, LANES), axis=0)
                    total += part
                    coord_y = (2.0 * (first_row + band).astype(jnp.float32) + 1.0) / image_rows - 1.0
                    weighted_y += part * coord_y
                    mutual += jnp.sum((powers * column[piece, lanes]).reshape(IMG_W // 8, 8, LANES), axis=0)
                place = pl.ds(pl.multiple_of(index * LANES, LANES), LANES)
                out[slot, pair, 0:1, place] = top
                out[slot, pair, 1:2, place] = jnp.sum(total, axis=0, keepdims=True)
                out[slot, pair, 2:3, place] = jnp.sum(folded * coord_x, axis=0, keepdims=True)
                out[slot, pair, 3:4, place] = jnp.sum(weighted_y, axis=0, keepdims=True)
                out[slot, pair, 4:5, place] = jnp.sum(mutual, axis=0, keepdims=True)
                return carry

            lax.fori_loop(0, slab // LANES, lanes_step, 0, unroll=4)


def match(image_rows, multiplier, pair, meta, queries, maps, earlier):
    chips, cores, entries, piece, width = maps.shape
    quads = len(queries)
    pairs = entries // 2
    slab = chips * cores * piece

    def block(array, entry=0):
        return pl.BlockSpec((array.shape[0], cores, 1, piece, width), lambda step, meta: (0, 0, entry, 0, 0))

    partials = (quads, pairs, 8, slab)
    done = pl.BlockSpec((quads, max(pair, 1), 8, slab), lambda step, meta: (0, 0, 0, 0))
    return pl.pallas_call(
        functools.partial(match_kernel, image_rows, multiplier, pair),
        grid_spec=pltpu.PrefetchScalarGridSpec(
            num_scalar_prefetch=1,
            grid=(1,),
            in_specs=[block(maps, pair)] + [block(array) for array in queries] + [block(maps, pairs + pair), done],
            out_specs=pl.BlockSpec((quads, pair + 1, 8, slab), lambda step, meta: (0, 0, 0, 0)),
            scratch_shapes=[pltpu.VMEM((slab, quads * slab), jnp.float32)] * 2,
        ),
        out_shape=jax.ShapeDtypeStruct((quads, pair + 1, 8, slab), jnp.float32),
        compiler_params=pltpu.CompilerParams(vmem_limit_bytes=40 * 1024 * 1024),
        cost_estimate=pl.CostEstimate(
            flops=2 * slab * slab * quads * width, bytes_accessed=2 << 20, transcendentals=2 << 20
        ),
    )(meta, maps, *queries, maps, earlier)


def shards(picture_descriptors, image_slot, group_images, pair_target, pair_count):
    chips = lax.axis_size("chip")
    cores = lax.axis_size("core")
    quads = lax.axis_size("quad")
    groups = chips * cores
    chip = lax.axis_index("chip").astype(jnp.int32)
    core = lax.axis_index("core").astype(jnp.int32)
    quad = lax.axis_index("quad").astype(jnp.int32)
    images_dev, slab, width = picture_descriptors.shape
    pairs = pair_target.shape[0]
    images = image_slot.shape[0]
    chip_rows = images_dev * cores
    image_rows = slab * quads // IMG_W
    multiplier = LOG2E / (width * SHARPNESS_DIVISOR)

    def all_pairs(array):
        return lax.all_to_all(array, ("chip", "core"), split_axis=0, concat_axis=0, tiled=True)

    traded = lax.ppermute(picture_descriptors, "core", [(i, (i + 1) % cores) for i in range(cores)])

    position = jnp.arange(group_images.shape[0], dtype=jnp.int32)
    wanted = jnp.concatenate([TGT_G + jnp.arange(pairs, dtype=jnp.int32), pair_target])
    ids = jnp.sum(jnp.where(wanted[:, None] == position[None, :], group_images[None, :], 0), axis=1)
    catalog = jnp.arange(images, dtype=jnp.int32)
    stored = jnp.sum(jnp.where(ids[:, None] == catalog[None, :], image_slot[None, :], 0), axis=1)
    in_use = jnp.arange(pairs, dtype=jnp.int32) < pair_count[0]
    stored = jnp.where(jnp.concatenate([in_use, in_use]), stored, -1)
    message = jnp.pad(stored, (0, LANES - 2 * pairs), constant_values=-1)
    asked = all_pairs(jnp.broadcast_to(message[None, None, :], (groups, 1, LANES)))

    capacities = [size for size in CAPACITIES if size < chip_rows] + [chip_rows]
    index, rows, branch = plan(chip_rows, 2 * pairs, capacities, chip[None], asked)
    halves = (images_dev, cores, chips, slab // groups, width)

    def exchange(capacity, operands):
        own, other, rows, index = operands
        pieces = pick(capacity, core[None], rows, own, other)
        spread = lax.all_to_all(pieces, "chip", split_axis=0, concat_axis=0, tiled=True)
        return regroup(groups, 2 * pairs, index, spread)

    pieces = lax.switch(
        branch[0],
        [functools.partial(exchange, size) for size in capacities],
        (picture_descriptors.reshape(halves), traded.reshape(halves), rows, index),
    )
    maps = all_pairs(pieces).reshape(chips, cores, *pieces.shape[1:])

    def move(array, step):
        return lax.ppermute(array, "quad", [(i, (i + step) % quads) for i in range(quads)])

    meta = jnp.stack([quad, pair_count[0]])
    partial = jnp.zeros((quads, 1, 8, slab), jnp.float32)
    for pair in range(pairs):
        query = maps[:, :, pair : pair + 1]
        before = move(query, 1)
        after = move(query, quads - 1)
        across = (move(before[: chips // 2], 1), move(after[chips // 2 :], quads - 1))
        partial = match(image_rows, multiplier, pair, meta, (before, *across, after), maps, partial)
    partial = lax.all_to_all(partial, "quad", split_axis=0, concat_axis=0, tiled=True)
    top = partial[:, :, 0]
    weight = jnp.exp2(top - jnp.max(top, axis=0, keepdims=True))
    total = jnp.sum(partial[:, :, 1] * weight, axis=0)
    fields = [jnp.sum(partial[:, :, 2 + field] * weight, axis=0) / total for field in range(3)]
    return jnp.where(in_use[None, :, None], jnp.stack(fields), 0.0).transpose(1, 0, 2)


def solution(mesh):
    pair_axis = ("chip", "core")
    split = Mesh(mesh.devices.reshape(-1, CORES, mesh.devices.shape[-1]), (*pair_axis, "quad"))
    return jax.shard_map(
        shards,
        mesh=split,
        in_specs=(P(pair_axis, "quad", None), P(), P(pair_axis), P(pair_axis), P(pair_axis)),
        out_specs=P(pair_axis, None, "quad"),
        check_vma=False,
    )
```

time: 182 us -> 139 us (0.76)
  the two profiles are of different devices: /device:TPU:24 before, /device:TPU:48 now
where the time goes in v1:
time: 139 us
  blocking collectives  79.8 us (57%)
  starting transfers between devices  25 us (18%)
  Pallas kernels  15.2 us (11%)
  waiting for transfers between devices  13 us (9%)
  other arithmetic  3.43 us (2%)
  between operations  1.45 us (1%)
    all_to_all x1, blocking collectives, exchange(): lax.all_to_all(pieces, 'chip', split_axis=0, concat_axis=0, tiled=True)  36.2 us
    all_to_all x1, blocking collectives, all_pairs(): lax.all_to_all(array, ('chip', 'core'), split_axis=0, concat_axis=0, tile...  34.5 us
    ppermute x8, starting transfers between devices, move(): lax.ppermute(array, 'quad', [(i, (i + step) % quads) for i in range(quads)])  13.3 us
    all_to_all x1, starting transfers between devices, all_pairs(): lax.all_to_all(array, ('chip', 'core'), split_axis=0, concat_axis=0, tile...  11.6 us
    all_to_all x1, blocking collectives, shards(): lax.all_to_all(partial, 'quad', split_axis=0, concat_axis=0, tiled=True)  9.04 us
    pallas_call x2, Pallas kernels, match(): pl.pallas_call(functools.partial(match_kernel, image_rows, multiplier, pa...  8.24 us
    all_to_all x1, waiting for transfers between devices, all_pairs(): lax.all_to_all(array, ('chip', 'core'), split_axis=0, concat_axis=0, tile...  6.91 us
    ppermute x8, waiting for transfers between devices, move(): lax.ppermute(array, 'quad', [(i, (i + step) % quads) for i in range(quads)])  6.09 us
  transfers between devices with their start and end apart: 10, of which 3 were waited for; matrix products, arithmetic and copies ran while one was open for 2% of the time, Pallas kernels for 5%

profile of v1, /device:TPU:48, one launch (start us, length us, event | category | flops | bytes accessed | tf_op | source)
XLA Modules:
  0.0 139.3 jit_solution(3115619795325205185)
XLA Ops:
  0.0 0.0 collective-permute-start
  0.7 0.7 pad_add_fusion.1
  1.4 0.8 select_reduce_fusion.1
  2.2 0.9 select_reduce_fusion
  3.1 0.1 add_select_fusion
  3.2 0.6 broadcast_in_dim.94
  3.8 11.6 %all-to-all-start.9 = ((s32[64,1,128]{2,1,0:T(1,128)}), s32[64,1,128]{2,1,0:T(1,128)S(1)}, u32[]{:S(2)}, u32[]{:S(2)}) async-start(s32[64,1,128]{2,1,0:T(1,128)} %broadcast_in_dim.94), calls=%async_computation.9 | async-start | bytes 65536 | tf_op jit(solution)/shard_map/all_to_all | solution.py:252
  15.5 6.9 %all-to-all-done.9.asked = s32[64,1,128]{2,1,0:T(1,128)S(1)} async-done(((s32[64,1,128]{2,1,0:T(1,128)}), s32[64,1,128]{2,1,0:T(1,128)S(1)}, u32[]{:S(2)}, u32[]{:S(2)}) %all-to-all-start.9) | async-done | bytes 32800 | tf_op jit(solution)/shard_map/all_to_all | solution.py:252
  22.4 0.0 copy-start
  22.4 0.6 copy-done
  23.0 2.6 %shard_map.55 = (s32[64,128]{1,0:T(8,128)S(1)}, s32[32,128]{1,0:T(8,128)S(1)}, s32[1]{0:T(128)}) custom-call(s32[1]{0:T(128)} %bitcast.11.chip, s32[64,1,128]{2,1,0:T(1,128)} %copy-done), custom_call_target="tpu_custom_call" | custom-call | tf_op jit(solution)/shard_map/pallas_call | solution.py:68
  26.3 0.0 collective-permute-done
  26.3 40.7 %conditional.1 = (bf16[64,4,8,256]{3,2,1,0:T(8,128)(2,1)S(1)}) conditional(s32[]{:T(128)} %bitcast.12, (s32[]{:T(128)}, s32[32,128]{1,0:T(8,128)S(1)}, bf16[16,2,32,8,256]{4,3,2,1,0:T(8,128)(2,1)}, bf16[16,2,32,8,256]{4,3,2,1,0:T(8,128)(2,1)}, s32[64,128]{1,0:T(8,128)S(1)}) %tuple.53, (s32[]{:T(128)}, ...), branch_computations={%region_2.3_spmd, %region_3.4_spmd, %region_4.5_spmd, %region_5.6_... | conditional | bytes 8388616 | solution.py:276
  26.3 2.2 %branch_3_fun.2 = bf16[32,9,8,256]{3,2,1,0:T(8,128)(2,1)S(1)} custom-call(s32[1]{0:T(128)} %bitcast.3.core, s32[32,128]{1,0:T(8,128)S(1)} %get-tuple-element.122.rows, bf16[16,2,32,8,256]{4,3,2,1,0:T(8,128)(2,1)} %get-tuple-element.123.own, bf16[16,2,32,8,256]{4,3,2,1,0:T(8,128)(2,1)} %get-tuple-element.124.other), custom_call_target="tpu_custom_call" | custom-call | tf_op jit(solution)/shard_map/cond/branch_3_fun/pallas_call | solution.py:108
  28.6 36.2 %all_to_all.54.spread = bf16[32,9,8,256]{3,2,1,0:T(8,128)(2,1)S(1)} all-to-all(bf16[32,9,8,256]{3,2,1,0:T(8,128)(2,1)S(1)} %branch_3_fun.2), channel_id=1, replica_groups=mesh['chip'=32,'core'=2,'quad'=4] {'chip'}, dimensions={0} | all-to-all | bytes 2359296 | tf_op jit(solution)/shard_map/cond/branch_3_fun/all_to_all | solution.py:273
  64.8 2.2 %branch_3_fun.3 = bf16[64,4,8,256]{3,2,1,0:T(8,128)(2,1)S(1)} custom-call(s32[64,128]{1,0:T(8,128)S(1)} %get-tuple-element.120.index, bf16[32,9,8,256]{3,2,1,0:T(8,128)(2,1)S(1)} %all_to_all.54.spread), custom_call_target="tpu_custom_call" | custom-call | tf_op jit(solution)/shard_map/cond/branch_3_fun/pallas_call | solution.py:131
  67.0 34.5 %all_to_all.60 = bf16[64,4,8,256]{3,2,1,0:T(8,128)(2,1)S(1)} all-to-all(bf16[64,4,8,256]{3,2,1,0:T(8,128)(2,1)S(1)} %get-tuple-element.171), channel_id=1, replica_groups=mesh['chip'=32,'core'=2,'quad'=4] {'chip','core'}, dimensions={0} | all-to-all | bytes 2097152 | tf_op jit(solution)/shard_map/all_to_all | solution.py:252
  101.6 1.6 %collective-permute-start.5 = (bf16[32,2,1,8,256]{4,3,2,1,0:T(8,128)(2,1)S(1)}, bf16[32,2,1,8,256]{4,3,2,1,0:T(8,128)(2,1)S(1)}, u32[]{:S(2)}, u32[]{:S(2)}) collective-permute-start(bf16[32,2,1,8,256]{4,3,2,1,0:T(8,128)(2,1)S(1)} %get-tuple-element.160), channel_id=1, source_target_pairs={{0,1},{1,2},{2,3},{3,0},{4,5},{5,6},{6,7},{7,4},{8,9},{9,10},{10,1... | collective-permute-start | bytes 786440 | tf_op jit(solution)/shard_map/ppermute | solution.py:284
  103.1 1.7 %collective-permute-start.7 = (bf16[32,2,1,8,256]{4,3,2,1,0:T(8,128)(2,1)S(1)}, bf16[32,2,1,8,256]{4,3,2,1,0:T(8,128)(2,1)S(1)}, u32[]{:S(2)}, u32[]{:S(2)}) collective-permute-start(bf16[32,2,1,8,256]{4,3,2,1,0:T(8,128)(2,1)S(1)} %get-tuple-element.160), channel_id=1, source_target_pairs={{0,3},{1,0},{2,1},{3,2},{4,7},{5,4},{6,5},{7,6},{8,11},{9,8},{10,9... | collective-permute-start | bytes 786440 | tf_op jit(solution)/shard_map/ppermute | solution.py:284
  104.9 0.3 collective-permute-start.1
  105.2 3.0 %collective-permute-start.3 = (bf16[32,2,1,8,256]{4,3,2,1,0:T(8,128)(2,1)S(1)}, bf16[32,2,1,8,256]{4,3,2,1,0:T(8,128)(2,1)S(1)}, u32[]{:S(2)}, u32[]{:S(2)}) collective-permute-start(bf16[32,2,1,8,256]{4,3,2,1,0:T(8,128)(2,1)S(1)} %get-tuple-element.161), channel_id=1, source_target_pairs={{0,3},{1,0},{2,1},{3,2},{4,7},{5,4},{6,5},{7,6},{8,11},{9,8},{10,9... | collective-permute-start | bytes 786440 | tf_op jit(solution)/shard_map/ppermute | solution.py:284
  108.1 4.0 %collective-permute-done.5.q1 = bf16[32,2,1,8,256]{4,3,2,1,0:T(8,128)(2,1)S(1)} collective-permute-done((bf16[32,2,1,8,256]{4,3,2,1,0:T(8,128)(2,1)S(1)}, bf16[32,2,1,8,256]{4,3,2,1,0:T(8,128)(2,1)S(1)}, u32[]{:S(2)}, u32[]{:S(2)}) %collective-permute-start.5) | collective-permute-done | bytes 262176 | tf_op jit(solution)/shard_map/ppermute | solution.py:284
  112.1 0.4 collective-permute-start.6
  112.5 0.0 collective-permute-done.7.q3
  112.5 3.0 %collective-permute-start.8 = (bf16[16,2,1,8,256]{4,3,2,1,0:T(8,128)(2,1)S(1)}, bf16[16,2,1,8,256]{4,3,2,1,0:T(8,128)(2,1)S(1)}, u32[]{:S(2)}, u32[]{:S(2)}) collective-permute-start(bf16[16,2,1,8,256]{4,3,2,1,0:T(8,128)(2,1)S(1)} %slice.49), channel_id=1, source_target_pairs={{0,3},{1,0},{2,1},{3,2},{4,7},{5,4},{6,5},{7,6},{8,11},{9,8},{10,9... | collective-permute-start | bytes 393224 | tf_op jit(solution)/shard_map/ppermute | solution.py:284
  115.5 2.1 %collective-permute-done.1.q1 = bf16[32,2,1,8,256]{4,3,2,1,0:T(8,128)(2,1)S(1)} collective-permute-done((bf16[32,2,1,8,256]{4,3,2,1,0:T(8,128)(2,1)S(1)}, bf16[32,2,1,8,256]{4,3,2,1,0:T(8,128)(2,1)S(1)}, u32[]{:S(2)}, u32[]{:S(2)}) %collective-permute-start.1) | collective-permute-done | bytes 262176 | tf_op jit(solution)/shard_map/ppermute | solution.py:284
  117.6 0.5 collective-permute-start.2
  118.1 0.0 collective-permute-done.3.q3
  118.1 2.9 %collective-permute-start.4 = (bf16[16,2,1,8,256]{4,3,2,1,0:T(8,128)(2,1)S(1)}, bf16[16,2,1,8,256]{4,3,2,1,0:T(8,128)(2,1)S(1)}, u32[]{:S(2)}, u32[]{:S(2)}) collective-permute-start(bf16[16,2,1,8,256]{4,3,2,1,0:T(8,128)(2,1)S(1)} %slice.46), channel_id=1, source_target_pairs={{0,3},{1,0},{2,1},{3,2},{4,7},{5,4},{6,5},{7,6},{8,11},{9,8},{10,9... | collective-permute-start | bytes 393224 | tf_op jit(solution)/shard_map/ppermute | solution.py:284
  121.0 0.1 pad_add_fusion.meta
  121.1 0.0 collective-permute-done.6.q2a
  121.1 0.0 collective-permute-done.8.q2b
  121.1 4.1 %shard_map.56.earlier = f32[4,1,8,512]{3,2,1,0:T(8,128)S(1)} custom-call(s32[2]{0:T(128)S(1)} %pad_add_fusion.meta, bf16[32,2,4,8,256]{4,3,2,1,0:T(8,128)(2,1)S(1)} %bitcast.64, bf16[32,2,1,8,256]{4,3,2,1,0:T(8,128)(2,1)S(1)} %collective-permute-done.5.q1, bf16[16,2,1,8,256]{4,3,2,1,0:T(8,128)(2,1)S(1)} %collective-permute-done.6.q2a, ...), custom_call_target="tpu_custom_call" | custom-call | flops 536870912 | bytes 2097152 | tf_op jit(solution)/shard_map/pallas_call | solution.py:219
  125.2 0.0 collective-permute-done.2.q2a
  125.3 0.0 collective-permute-done.4.q2b
  125.3 4.1 %shard_map.57 = f32[4,2,8,512]{3,2,1,0:T(8,128)S(1)} custom-call(s32[2]{0:T(128)S(1)} %pad_add_fusion.meta, bf16[32,2,4,8,256]{4,3,2,1,0:T(8,128)(2,1)S(1)} %bitcast.66, bf16[32,2,1,8,256]{4,3,2,1,0:T(8,128)(2,1)S(1)} %collective-permute-done.1.q1, bf16[16,2,1,8,256]{4,3,2,1,0:T(8,128)(2,1)S(1)} %collective-permute-done.2.q2a, ...), custom_call_target="tpu_custom_call" | custom-call | flops 536870912 | bytes 2097152 | tf_op jit(solution)/shard_map/pallas_call | solution.py:219
  129.4 9.0 %all_to_all.61 = f32[4,2,8,512]{3,2,1,0:T(8,128)S(1)} all-to-all(f32[4,2,8,512]{3,2,1,0:T(8,128)S(1)} %shard_map.57), channel_id=1, replica_groups=mesh['chip'=32,'core'=2,'quad'=4] {'quad'}, dimensions={0} | all-to-all | bytes 262144 | tf_op jit(solution)/shard_map/all_to_all | solution.py:294
  138.4 0.1 fusion.12
  138.5 0.1 fusion.8
  138.6 0.7 fusion.10
  (10 shorter events, 0.1 us)
Async XLA Ops:
  0.0 26.3 %collective-permute-start = (bf16[16,512,256]{2,1,0:T(8,128)(2,1)}, bf16[16,512,256]{2,1,0:T(8,128)(2,1)}, u32[]{:S(2)}, u32[]{:S(2)}) collective-permute-start(bf16[16,512,256]{2,1,0:T(8,128)(2,1)} %param.14), channel_id=1, source_target_pairs={{0,4},{4,0},{1,5},{5,1},{2,6},{6,2},{3,7},{7,3},{8,12},{12,8},{9,1... | collective-permute-start | bytes 12582920 | tf_op jit(solution)/shard_map/ppermute | solution.py:254
  3.8 18.6 %all-to-all-start.9 = ((s32[64,1,128]{2,1,0:T(1,128)}), s32[64,1,128]{2,1,0:T(1,128)S(1)}, u32[]{:S(2)}, u32[]{:S(2)}) async-start(s32[64,1,128]{2,1,0:T(1,128)} %broadcast_in_dim.94), calls=%async_computation.9 | async-start | bytes 65536 | tf_op jit(solution)/shard_map/all_to_all | solution.py:252
  22.4 0.6 copy-start
  101.6 10.5 %collective-permute-start.5 = (bf16[32,2,1,8,256]{4,3,2,1,0:T(8,128)(2,1)S(1)}, bf16[32,2,1,8,256]{4,3,2,1,0:T(8,128)(2,1)S(1)}, u32[]{:S(2)}, u32[]{:S(2)}) collective-permute-start(bf16[32,2,1,8,256]{4,3,2,1,0:T(8,128)(2,1)S(1)} %get-tuple-element.160), channel_id=1, source_target_pairs={{0,1},{1,2},{2,3},{3,0},{4,5},{5,6},{6,7},{7,4},{8,9},{9,10},{10,1... | collective-permute-start | bytes 786440 | tf_op jit(solution)/shard_map/ppermute | solution.py:284
  103.1 9.3 %collective-permute-start.7 = (bf16[32,2,1,8,256]{4,3,2,1,0:T(8,128)(2,1)S(1)}, bf16[32,2,1,8,256]{4,3,2,1,0:T(8,128)(2,1)S(1)}, u32[]{:S(2)}, u32[]{:S(2)}) collective-permute-start(bf16[32,2,1,8,256]{4,3,2,1,0:T(8,128)(2,1)S(1)} %get-tuple-element.160), channel_id=1, source_target_pairs={{0,3},{1,0},{2,1},{3,2},{4,7},{5,4},{6,5},{7,6},{8,11},{9,8},{10,9... | collective-permute-start | bytes 786440 | tf_op jit(solution)/shard_map/ppermute | solution.py:284
  104.9 12.7 %collective-permute-start.1 = (bf16[32,2,1,8,256]{4,3,2,1,0:T(8,128)(2,1)S(1)}, bf16[32,2,1,8,256]{4,3,2,1,0:T(8,128)(2,1)S(1)}, u32[]{:S(2)}, u32[]{:S(2)}) collective-permute-start(bf16[32,2,1,8,256]{4,3,2,1,0:T(8,128)(2,1)S(1)} %get-tuple-element.161), channel_id=1, source_target_pairs={{0,1},{1,2},{2,3},{3,0},{4,5},{5,6},{6,7},{7,4},{8,9},{9,10},{10,1... | collective-permute-start | bytes 786440 | tf_op jit(solution)/shard_map/ppermute | solution.py:284
  105.2 12.9 %collective-permute-start.3 = (bf16[32,2,1,8,256]{4,3,2,1,0:T(8,128)(2,1)S(1)}, bf16[32,2,1,8,256]{4,3,2,1,0:T(8,128)(2,1)S(1)}, u32[]{:S(2)}, u32[]{:S(2)}) collective-permute-start(bf16[32,2,1,8,256]{4,3,2,1,0:T(8,128)(2,1)S(1)} %get-tuple-element.161), channel_id=1, source_target_pairs={{0,3},{1,0},{2,1},{3,2},{4,7},{5,4},{6,5},{7,6},{8,11},{9,8},{10,9... | collective-permute-start | bytes 786440 | tf_op jit(solution)/shard_map/ppermute | solution.py:284
  112.1 9.0 %collective-permute-start.6 = (bf16[16,2,1,8,256]{4,3,2,1,0:T(8,128)(2,1)S(1)}, bf16[16,2,1,8,256]{4,3,2,1,0:T(8,128)(2,1)S(1)}, u32[]{:S(2)}, u32[]{:S(2)}) collective-permute-start(bf16[16,2,1,8,256]{4,3,2,1,0:T(8,128)(2,1)S(1)} %slice.48), channel_id=1, source_target_pairs={{0,1},{1,2},{2,3},{3,0},{4,5},{5,6},{6,7},{7,4},{8,9},{9,10},{10,1... | collective-permute-start | bytes 393224 | tf_op jit(solution)/shard_map/ppermute | solution.py:284
  112.5 8.6 %collective-permute-start.8 = (bf16[16,2,1,8,256]{4,3,2,1,0:T(8,128)(2,1)S(1)}, bf16[16,2,1,8,256]{4,3,2,1,0:T(8,128)(2,1)S(1)}, u32[]{:S(2)}, u32[]{:S(2)}) collective-permute-start(bf16[16,2,1,8,256]{4,3,2,1,0:T(8,128)(2,1)S(1)} %slice.49), channel_id=1, source_target_pairs={{0,3},{1,0},{2,1},{3,2},{4,7},{5,4},{6,5},{7,6},{8,11},{9,8},{10,9... | collective-permute-start | bytes 393224 | tf_op jit(solution)/shard_map/ppermute | solution.py:284
  117.6 7.6 %collective-permute-start.2 = (bf16[16,2,1,8,256]{4,3,2,1,0:T(8,128)(2,1)S(1)}, bf16[16,2,1,8,256]{4,3,2,1,0:T(8,128)(2,1)S(1)}, u32[]{:S(2)}, u32[]{:S(2)}) collective-permute-start(bf16[16,2,1,8,256]{4,3,2,1,0:T(8,128)(2,1)S(1)} %slice.45), channel_id=1, source_target_pairs={{0,1},{1,2},{2,3},{3,0},{4,5},{5,6},{6,7},{7,4},{8,9},{9,10},{10,1... | collective-permute-start | bytes 393224 | tf_op jit(solution)/shard_map/ppermute | solution.py:284
  118.1 7.2 %collective-permute-start.4 = (bf16[16,2,1,8,256]{4,3,2,1,0:T(8,128)(2,1)S(1)}, bf16[16,2,1,8,256]{4,3,2,1,0:T(8,128)(2,1)S(1)}, u32[]{:S(2)}, u32[]{:S(2)}) collective-permute-start(bf16[16,2,1,8,256]{4,3,2,1,0:T(8,128)(2,1)S(1)} %slice.46), channel_id=1, source_target_pairs={{0,3},{1,0},{2,1},{3,2},{4,7},{5,4},{6,5},{7,6},{8,11},{9,8},{10,9... | collective-permute-start | bytes 393224 | tf_op jit(solution)/shard_map/ppermute | solution.py:284

commit v2 on v1

--- a/solution.py
+++ b/solution.py
@@ -15,11 +15,32 @@
 LOG2E = math.log2(math.e)
 LANES = 128
 CORES = 2
-PLACES = 64
+PLACE_BITS = 6
+PLACES = 1 << PLACE_BITS
 CAPACITIES = (6, 7, 8, 9, 10, 11, 12, 16)
 ANY = pl.BlockSpec(memory_space=pl.ANY)
 SMEM = pl.BlockSpec(memory_space=pltpu.SMEM)
 VMEM = pl.BlockSpec(memory_space=pltpu.VMEM)
+
+
+def announce_kernel(pairs, image_slot, group_images, pair_target, pair_count, out):
+    lane = lax.broadcasted_iota(jnp.int32, out.shape, 2)
+    message = jnp.full(out.shape, -1, jnp.int32)
+    for entry in range(2 * pairs):
+        pair = entry % pairs
+        member = TGT_G + pair if entry < pairs else pair_target[pair]
+        stored = jnp.where(pair < pair_count[0], image_slot[group_images[member]], -1)
+        message = jnp.where(lane == entry, stored, message)
+    out[...] = message
+
+
+def announce(groups, image_slot, group_images, pair_target, pair_count):
+    return pl.pallas_call(
+        functools.partial(announce_kernel, pair_target.shape[0]),
+        in_specs=[SMEM] * 4,
+        out_specs=VMEM,
+        out_shape=jax.ShapeDtypeStruct((groups, 1, LANES), jnp.int32),
+    )(image_slot, group_images, pair_target, pair_count)
 
 
 def plan_kernel(chip_rows, entries, capacities, chip, asked, index, rows, branch, requested, before):
@@ -121,7 +142,7 @@
     def step(group, carry):
         for entry in range(entries):
             code = index[group, entry]
-            out[group, entry] = spread[lax.div(code, PLACES), lax.rem(code, PLACES)]
+            out[group, entry] = spread[code >> PLACE_BITS, code & (PLACES - 1)]
         return carry
 
     lax.fori_loop(0, groups, step, 0, unroll=8)
@@ -137,26 +158,30 @@
     )(index, spread)
 
 
-def match_kernel(image_rows, multiplier, pair, meta, q0, q1, q2a, q2b, q3, target, earlier, out, scores, column):
+def match_kernel(image_rows, multiplier, pair, meta, maps, q1, q2a, q2b, q3, *refs):
+    *earlier, out0, out1, out2, out3, scores, column = refs
+    outs = (out0, out1, out2, out3)
     quad = meta[0]
-    chips, cores, _, piece, width = target.shape
+    chips, cores, entries, piece, width = maps.shape
+    target_entry = entries // 2 + pair
     part = chips * piece
     slab = cores * part
-    quads = out.shape[0]
-    for previous in range(pair):
-        out[:, previous] = earlier[:, previous]
+    quads = len(outs)
+    for old, new in zip(earlier, outs):
+        new[0:pair] = old[...]
 
     @pl.when(pair < meta[1])
     def _():
         for row in range(cores):
-            rows = target[:, row, 0].reshape(part, width)
-            for step, skip, query in ((0, 0, q0), (1, 0, q1), (2, 0, q2a), (2, q2a.shape[0], q2b), (3, 0, q3)):
+            rows = maps[:, row, target_entry].reshape(part, width)
+            blocks = ((0, 0, maps, pair), (1, 0, q1, 0), (2, 0, q2a, 0), (2, q2a.shape[0], q2b, 0), (3, 0, q3, 0))
+            for step, skip, query, entry in blocks:
                 tokens = query.shape[0] * piece
                 for core in range(cores):
                     start = step * slab + core * part + skip * piece
                     scores[row * part : (row + 1) * part, start : start + tokens] = (
                         lax.dot_general(
-                            rows, query[:, core, 0].reshape(tokens, width), (((1,), (1,)), ((), ())),
+                            rows, query[:, core, entry].reshape(tokens, width), (((1,), (1,)), ((), ())),
                             preferred_element_type=jnp.float32,
                         )
                         * multiplier
@@ -176,9 +201,9 @@
         coord_x = (2.0 * along + 1.0) / IMG_W - 1.0
         first_row = quad * bands
         for step in range(quads):
-            slot = lax.rem(quad - step + quads, quads)
-
-            def lanes_step(index, carry, step=step, slot=slot):
+            out = outs[step]
+
+            def lanes_step(index, carry, step=step, out=out):
                 lanes = pl.ds(pl.multiple_of(step * slab + index * LANES, LANES), LANES)
                 top = jnp.max(scores[:, lanes], axis=0, keepdims=True)
                 total = jnp.zeros((8, LANES), jnp.float32)
@@ -195,42 +220,31 @@
                     weighted_y += part * coord_y
                     mutual += jnp.sum((powers * column[piece, lanes]).reshape(IMG_W // 8, 8, LANES), axis=0)
                 place = pl.ds(pl.multiple_of(index * LANES, LANES), LANES)
-                out[slot, pair, 0:1, place] = top
-                out[slot, pair, 1:2, place] = jnp.sum(total, axis=0, keepdims=True)
-                out[slot, pair, 2:3, place] = jnp.sum(folded * coord_x, axis=0, keepdims=True)
-                out[slot, pair, 3:4, place] = jnp.sum(weighted_y, axis=0, keepdims=True)
-                out[slot, pair, 4:5, place] = jnp.sum(mutual, axis=0, keepdims=True)
+                out[pair, 0:1, place] = top
+                out[pair, 1:2, place] = jnp.sum(total, axis=0, keepdims=True)
+                out[pair, 2:3, place] = jnp.sum(folded * coord_x, axis=0, keepdims=True)
+                out[pair, 3:4, place] = jnp.sum(weighted_y, axis=0, keepdims=True)
+                out[pair, 4:5, place] = jnp.sum(mutual, axis=0, keepdims=True)
                 return carry
 
             lax.fori_loop(0, slab // LANES, lanes_step, 0, unroll=4)
 
 
 def match(image_rows, multiplier, pair, meta, queries, maps, earlier):
-    chips, cores, entries, piece, width = maps.shape
+    chips, cores, _, piece, width = maps.shape
     quads = len(queries)
-    pairs = entries // 2
     slab = chips * cores * piece
-
-    def block(array, entry=0):
-        return pl.BlockSpec((array.shape[0], cores, 1, piece, width), lambda step, meta: (0, 0, entry, 0, 0))
-
-    partials = (quads, pairs, 8, slab)
-    done = pl.BlockSpec((quads, max(pair, 1), 8, slab), lambda step, meta: (0, 0, 0, 0))
     return pl.pallas_call(
         functools.partial(match_kernel, image_rows, multiplier, pair),
-        grid_spec=pltpu.PrefetchScalarGridSpec(
-            num_scalar_prefetch=1,
-            grid=(1,),
-            in_specs=[block(maps, pair)] + [block(array) for array in queries] + [block(maps, pairs + pair), done],
-            out_specs=pl.BlockSpec((quads, pair + 1, 8, slab), lambda step, meta: (0, 0, 0, 0)),
-            scratch_shapes=[pltpu.VMEM((slab, quads * slab), jnp.float32)] * 2,
-        ),
-        out_shape=jax.ShapeDtypeStruct((quads, pair + 1, 8, slab), jnp.float32),
-        compiler_params=pltpu.CompilerParams(vmem_limit_bytes=40 * 1024 * 1024),
+        in_specs=[SMEM] + [VMEM] * (1 + len(queries) + len(earlier)),
+        out_specs=[VMEM] * quads,
+        out_shape=[jax.ShapeDtypeStruct((pair + 1, 8, slab), jnp.float32)] * quads,
+        scratch_shapes=[pltpu.VMEM((slab, quads * slab), jnp.float32)] * 2,
+        compiler_params=pltpu.CompilerParams(vmem_limit_bytes=32 * 1024 * 1024),
         cost_estimate=pl.CostEstimate(
             flops=2 * slab * slab * quads * width, bytes_accessed=2 << 20, transcendentals=2 << 20
         ),
-    )(meta, maps, *queries, maps, earlier)
+    )(meta, maps, *queries, *earlier)
 
 
 def shards(picture_descriptors, image_slot, group_images, pair_target, pair_count):
@@ -243,7 +257,6 @@
     quad = lax.axis_index("quad").astype(jnp.int32)
     images_dev, slab, width = picture_descriptors.shape
     pairs = pair_target.shape[0]
-    images = image_slot.shape[0]
     chip_rows = images_dev * cores
     image_rows = slab * quads // IMG_W
     multiplier = LOG2E / (width * SHARPNESS_DIVISOR)
@@ -253,15 +266,7 @@
 
     traded = lax.ppermute(picture_descriptors, "core", [(i, (i + 1) % cores) for i in range(cores)])
 
-    position = jnp.arange(group_images.shape[0], dtype=jnp.int32)
-    wanted = jnp.concatenate([TGT_G + jnp.arange(pairs, dtype=jnp.int32), pair_target])
-    ids = jnp.sum(jnp.where(wanted[:, None] == position[None, :], group_images[None, :], 0), axis=1)
-    catalog = jnp.arange(images, dtype=jnp.int32)
-    stored = jnp.sum(jnp.where(ids[:, None] == catalog[None, :], image_slot[None, :], 0), axis=1)
-    in_use = jnp.arange(pairs, dtype=jnp.int32) < pair_count[0]
-    stored = jnp.where(jnp.concatenate([in_use, in_use]), stored, -1)
-    message = jnp.pad(stored, (0, LANES - 2 * pairs), constant_values=-1)
-    asked = all_pairs(jnp.broadcast_to(message[None, None, :], (groups, 1, LANES)))
+    asked = all_pairs(announce(groups, image_slot, group_images, pair_target, pair_count))
 
     capacities = [size for size in CAPACITIES if size < chip_rows] + [chip_rows]
     index, rows, branch = plan(chip_rows, 2 * pairs, capacities, chip[None], asked)
@@ -284,18 +289,19 @@
         return lax.ppermute(array, "quad", [(i, (i + step) % quads) for i in range(quads)])
 
     meta = jnp.stack([quad, pair_count[0]])
-    partial = jnp.zeros((quads, 1, 8, slab), jnp.float32)
+    partials = []
     for pair in range(pairs):
         query = maps[:, :, pair : pair + 1]
         before = move(query, 1)
         after = move(query, quads - 1)
         across = (move(before[: chips // 2], 1), move(after[chips // 2 :], quads - 1))
-        partial = match(image_rows, multiplier, pair, meta, (before, *across, after), maps, partial)
-    partial = lax.all_to_all(partial, "quad", split_axis=0, concat_axis=0, tiled=True)
+        partials = match(image_rows, multiplier, pair, meta, (before, *across, after), maps, partials)
+    partial = jnp.stack([partials[0]] + [move(partials[step], quads - step) for step in range(1, quads)])
     top = partial[:, :, 0]
     weight = jnp.exp2(top - jnp.max(top, axis=0, keepdims=True))
     total = jnp.sum(partial[:, :, 1] * weight, axis=0)
     fields = [jnp.sum(partial[:, :, 2 + field] * weight, axis=0) / total for field in range(3)]
+    in_use = jnp.arange(pairs, dtype=jnp.int32) < pair_count[0]
     return jnp.where(in_use[None, :, None], jnp.stack(fields), 0.0).transpose(1, 0, 2)
 
 

time: 139 us -> 136 us (0.978)
  the two profiles are of different devices: /device:TPU:48 before, /device:TPU:32 now
where the time goes in v2:
time: 136 us; the launch traced here: 137 us
  blocking collectives  69.2 us (51%)
  starting transfers between devices  28 us (21%)
  waiting for transfers between devices  20.4 us (15%)
  Pallas kernels  16.2 us (12%)
  between operations  1.45 us (1%)
    all_to_all x1, blocking collectives, exchange(): lax.all_to_all(pieces, 'chip', split_axis=0, concat_axis=0, tiled=True)  36.6 us
    all_to_all x1, blocking collectives, all_pairs(): lax.all_to_all(array, ('chip', 'core'), split_axis=0, concat_axis=0, tile...  32.6 us
    ppermute x11, starting transfers between devices, move(): lax.ppermute(array, 'quad', [(i, (i + step) % quads) for i in range(quads)])  16.1 us
    all_to_all x1, starting transfers between devices, all_pairs(): lax.all_to_all(array, ('chip', 'core'), split_axis=0, concat_axis=0, tile...  11.9 us
    ppermute x11, waiting for transfers between devices, move(): lax.ppermute(array, 'quad', [(i, (i + step) % quads) for i in range(quads)])  11.8 us
    all_to_all x1, waiting for transfers between devices, all_pairs(): lax.all_to_all(array, ('chip', 'core'), split_axis=0, concat_axis=0, tile...  8.61 us
    pallas_call x2, Pallas kernels, match(): pl.pallas_call(functools.partial(match_kernel, image_rows, multiplier, pa...  8.19 us
  transfers between devices with their start and end apart: 13, of which 8 were waited for; matrix products, arithmetic and copies ran while one was open for 0% of the time, Pallas kernels for 6%

profile of v2, /device:TPU:32, one launch (start us, length us, event | category | flops | bytes accessed | tf_op | source)
XLA Modules:
  0.0 136.9 jit_solution(3504777989791843732)
XLA Ops:
  0.0 0.0 collective-permute-start
  0.7 1.4 shard_map.55
  2.0 11.9 %all-to-all-start.9 = ((s32[64,1,128]{2,1,0:T(1,128)}), s32[64,1,128]{2,1,0:T(1,128)S(1)}, u32[]{:S(2)}, u32[]{:S(2)}) async-start(s32[64,1,128]{2,1,0:T(1,128)} %shard_map.55), calls=%async_computation.9 | async-start | bytes 65536 | tf_op jit(solution)/shard_map/all_to_all | solution.py:265
  13.9 8.6 %all-to-all-done.9.asked = s32[64,1,128]{2,1,0:T(1,128)S(1)} async-done(((s32[64,1,128]{2,1,0:T(1,128)}), s32[64,1,128]{2,1,0:T(1,128)S(1)}, u32[]{:S(2)}, u32[]{:S(2)}) %all-to-all-start.9) | async-done | bytes 32800 | tf_op jit(solution)/shard_map/all_to_all | solution.py:265
  22.5 0.0 copy-start
  22.5 0.6 copy-done
  23.1 2.6 %shard_map.56 = (s32[64,128]{1,0:T(8,128)S(1)}, s32[32,128]{1,0:T(8,128)S(1)}, s32[1]{0:T(128)}) custom-call(s32[1]{0:T(128)} %bitcast.11.chip, s32[64,1,128]{2,1,0:T(1,128)} %copy-done), custom_call_target="tpu_custom_call" | custom-call | tf_op jit(solution)/shard_map/pallas_call | solution.py:89
  26.4 0.0 collective-permute-done
  26.4 40.8 %conditional.1 = (bf16[64,4,8,256]{3,2,1,0:T(8,128)(2,1)S(1)}) conditional(s32[]{:T(128)} %bitcast.12, (s32[]{:T(128)}, s32[32,128]{1,0:T(8,128)S(1)}, bf16[16,2,32,8,256]{4,3,2,1,0:T(8,128)(2,1)}, bf16[16,2,32,8,256]{4,3,2,1,0:T(8,128)(2,1)}, s32[64,128]{1,0:T(8,128)S(1)}) %tuple.53, (s32[]{:T(128)}, ...), branch_computations={%region_0.0_spmd, %region_1.0_spmd, %region_2.0_spmd, %region_3.0_... | conditional | bytes 8388616 | solution.py:281
  26.4 2.4 %branch_3_fun.2 = bf16[32,9,8,256]{3,2,1,0:T(8,128)(2,1)S(1)} custom-call(s32[1]{0:T(128)} %bitcast.3.core, s32[32,128]{1,0:T(8,128)S(1)} %get-tuple-element.122.rows, bf16[16,2,32,8,256]{4,3,2,1,0:T(8,128)(2,1)} %get-tuple-element.123.own, bf16[16,2,32,8,256]{4,3,2,1,0:T(8,128)(2,1)} %get-tuple-element.124.other), custom_call_target="tpu_custom_call" | custom-call | tf_op jit(solution)/shard_map/cond/branch_3_fun/pallas_call | solution.py:129
  28.8 36.6 %all_to_all.49.spread = bf16[32,9,8,256]{3,2,1,0:T(8,128)(2,1)S(1)} all-to-all(bf16[32,9,8,256]{3,2,1,0:T(8,128)(2,1)S(1)} %branch_3_fun.2), channel_id=1, replica_groups=mesh['chip'=32,'core'=2,'quad'=4] {'chip'}, dimensions={0} | all-to-all | bytes 2359296 | tf_op jit(solution)/shard_map/cond/branch_3_fun/all_to_all | solution.py:278
  65.4 1.7 %branch_3_fun.3 = bf16[64,4,8,256]{3,2,1,0:T(8,128)(2,1)S(1)} custom-call(s32[64,128]{1,0:T(8,128)S(1)} %get-tuple-element.120.index, bf16[32,9,8,256]{3,2,1,0:T(8,128)(2,1)S(1)} %all_to_all.49.spread), custom_call_target="tpu_custom_call" | custom-call | tf_op jit(solution)/shard_map/cond/branch_3_fun/pallas_call | solution.py:152
  67.1 32.6 %all_to_all.55 = bf16[64,4,8,256]{3,2,1,0:T(8,128)(2,1)S(1)} all-to-all(bf16[64,4,8,256]{3,2,1,0:T(8,128)(2,1)S(1)} %get-tuple-element.188), channel_id=1, replica_groups=mesh['chip'=32,'core'=2,'quad'=4] {'chip','core'}, dimensions={0} | all-to-all | bytes 2097152 | tf_op jit(solution)/shard_map/all_to_all | solution.py:265
  99.8 2.8 %collective-permute-start.7 = (bf16[32,2,1,8,256]{4,3,2,1,0:T(8,128)(2,1)S(1)}, bf16[32,2,1,8,256]{4,3,2,1,0:T(8,128)(2,1)S(1)}, u32[]{:S(2)}, u32[]{:S(2)}) collective-permute-start(bf16[32,2,1,8,256]{4,3,2,1,0:T(8,128)(2,1)S(1)} %get-tuple-element.178), channel_id=1, source_target_pairs={{0,3},{1,0},{2,1},{3,2},{4,7},{5,4},{6,5},{7,6},{8,11},{9,8},{10,9... | collective-permute-start | bytes 786440 | tf_op jit(solution)/shard_map/ppermute | solution.py:289
  102.6 0.0 collective-permute-start.5
  102.6 3.2 %collective-permute-start.3 = (bf16[32,2,1,8,256]{4,3,2,1,0:T(8,128)(2,1)S(1)}, bf16[32,2,1,8,256]{4,3,2,1,0:T(8,128)(2,1)S(1)}, u32[]{:S(2)}, u32[]{:S(2)}) collective-permute-start(bf16[32,2,1,8,256]{4,3,2,1,0:T(8,128)(2,1)S(1)} %get-tuple-element.179), channel_id=1, source_target_pairs={{0,3},{1,0},{2,1},{3,2},{4,7},{5,4},{6,5},{7,6},{8,11},{9,8},{10,9... | collective-permute-start | bytes 786440 | tf_op jit(solution)/shard_map/ppermute | solution.py:289
  105.9 0.0 collective-permute-start.1
  105.9 3.4 %collective-permute-done.7.q3 = bf16[32,2,1,8,256]{4,3,2,1,0:T(8,128)(2,1)S(1)} collective-permute-done((bf16[32,2,1,8,256]{4,3,2,1,0:T(8,128)(2,1)S(1)}, bf16[32,2,1,8,256]{4,3,2,1,0:T(8,128)(2,1)S(1)}, u32[]{:S(2)}, u32[]{:S(2)}) %collective-permute-start.7) | collective-permute-done | bytes 262176 | tf_op jit(solution)/shard_map/ppermute | solution.py:289
  109.3 3.8 %collective-permute-start.8 = (bf16[16,2,1,8,256]{4,3,2,1,0:T(8,128)(2,1)S(1)}, bf16[16,2,1,8,256]{4,3,2,1,0:T(8,128)(2,1)S(1)}, u32[]{:S(2)}, u32[]{:S(2)}) collective-permute-start(bf16[16,2,1,8,256]{4,3,2,1,0:T(8,128)(2,1)S(1)} %slice.49), channel_id=1, source_target_pairs={{0,3},{1,0},{2,1},{3,2},{4,7},{5,4},{6,5},{7,6},{8,11},{9,8},{10,9... | collective-permute-start | bytes 393224 | tf_op jit(solution)/shard_map/ppermute | solution.py:289
  113.1 0.0 collective-permute-done.5.q1
  113.1 0.1 collective-permute-start.6
  113.2 1.7 %collective-permute-done.3.q3 = bf16[32,2,1,8,256]{4,3,2,1,0:T(8,128)(2,1)S(1)} collective-permute-done((bf16[32,2,1,8,256]{4,3,2,1,0:T(8,128)(2,1)S(1)}, bf16[32,2,1,8,256]{4,3,2,1,0:T(8,128)(2,1)S(1)}, u32[]{:S(2)}, u32[]{:S(2)}) %collective-permute-start.3) | collective-permute-done | bytes 262176 | tf_op jit(solution)/shard_map/ppermute | solution.py:289
  114.9 3.8 %collective-permute-start.4 = (bf16[16,2,1,8,256]{4,3,2,1,0:T(8,128)(2,1)S(1)}, bf16[16,2,1,8,256]{4,3,2,1,0:T(8,128)(2,1)S(1)}, u32[]{:S(2)}, u32[]{:S(2)}) collective-permute-start(bf16[16,2,1,8,256]{4,3,2,1,0:T(8,128)(2,1)S(1)} %slice.46), channel_id=1, source_target_pairs={{0,3},{1,0},{2,1},{3,2},{4,7},{5,4},{6,5},{7,6},{8,11},{9,8},{10,9... | collective-permute-start | bytes 393224 | tf_op jit(solution)/shard_map/ppermute | solution.py:289
  118.7 0.0 collective-permute-done.1.q1
  118.7 0.1 collective-permute-start.2
  118.8 0.1 pad_add_fusion.meta
  118.9 0.0 collective-permute-done.8.q2b
  118.9 1.6 %collective-permute-done.6.q2a = bf16[16,2,1,8,256]{4,3,2,1,0:T(8,128)(2,1)S(1)} collective-permute-done((bf16[16,2,1,8,256]{4,3,2,1,0:T(8,128)(2,1)S(1)}, bf16[16,2,1,8,256]{4,3,2,1,0:T(8,128)(2,1)S(1)}, u32[]{:S(2)}, u32[]{:S(2)}) %collective-permute-start.6) | collective-permute-done | bytes 131104 | tf_op jit(solution)/shard_map/ppermute | solution.py:289
  120.5 4.1 %shard_map.57 = (f32[1,8,512]{2,1,0:T(8,128)S(1)}, f32[1,8,512]{2,1,0:T(8,128)S(1)}, f32[1,8,512]{2,1,0:T(8,128)S(1)}, f32[1,8,512]{2,1,0:T(8,128)S(1)}) custom-call(s32[2]{0:T(128)S(1)} %pad_add_fusion.meta, bf16[32,2,4,8,256]{4,3,2,1,0:T(8,128)(2,1)S(1)} %bitcast.68, bf16[32,2,1,8,256]{4,3,2,1,0:T(8,128)(2,1)S(1)} %collective-permute-done.5.q1, ...), custom_call_target="tpu_custom_call" | custom-call | flops 536870912 | bytes 2097152 | tf_op jit(solution)/shard_map/pallas_call | solution.py:237
  124.6 0.0 collective-permute-done.4.q2b
  124.6 0.4 collective-permute-done.2.q2a
  125.0 4.1 %shard_map.58 = (f32[2,8,512]{2,1,0:T(8,128)S(1)}, f32[2,8,512]{2,1,0:T(8,128)S(1)}, f32[2,8,512]{2,1,0:T(8,128)S(1)}, f32[2,8,512]{2,1,0:T(8,128)S(1)}) custom-call(s32[2]{0:T(128)S(1)} %pad_add_fusion.meta, bf16[32,2,4,8,256]{4,3,2,1,0:T(8,128)(2,1)S(1)} %bitcast.69, bf16[32,2,1,8,256]{4,3,2,1,0:T(8,128)(2,1)S(1)} %collective-permute-done.1.q1, ...), custom_call_target="tpu_custom_call" | custom-call | flops 536870912 | bytes 2097152 | tf_op jit(solution)/shard_map/pallas_call | solution.py:237
  129.1 1.3 collective-permute-start.9
  130.4 0.0 collective-permute-start.10
  130.4 1.0 collective-permute-start.11
  131.4 1.7 %collective-permute-done.9 = f32[2,8,512]{2,1,0:T(8,128)S(1)} collective-permute-done((f32[2,8,512]{2,1,0:T(8,128)S(1)}, f32[2,8,512]{2,1,0:T(8,128)S(1)}, u32[]{:S(2)}, u32[]{:S(2)}) %collective-permute-start.9) | collective-permute-done | bytes 32800 | tf_op jit(solution)/shard_map/ppermute | solution.py:289
  133.1 2.9 %collective-permute-done.10 = f32[2,8,512]{2,1,0:T(8,128)S(1)} collective-permute-done((f32[2,8,512]{2,1,0:T(8,128)S(1)}, f32[2,8,512]{2,1,0:T(8,128)S(1)}, u32[]{:S(2)}, u32[]{:S(2)}) %collective-permute-start.10) | collective-permute-done | bytes 32800 | tf_op jit(solution)/shard_map/ppermute | solution.py:289
  135.9 0.1 collective-permute-done.11
  136.1 0.1 pad_maximum_fusion
  136.2 0.1 fusion.8
  136.3 0.7 fusion.10
  (8 shorter events, 0.1 us)
Async XLA Ops:
  0.0 26.4 %collective-permute-start = (bf16[16,512,256]{2,1,0:T(8,128)(2,1)}, bf16[16,512,256]{2,1,0:T(8,128)(2,1)}, u32[]{:S(2)}, u32[]{:S(2)}) collective-permute-start(bf16[16,512,256]{2,1,0:T(8,128)(2,1)} %param.14), channel_id=1, source_target_pairs={{0,4},{4,0},{1,5},{5,1},{2,6},{6,2},{3,7},{7,3},{8,12},{12,8},{9,1... | collective-permute-start | bytes 12582920 | tf_op jit(solution)/shard_map/ppermute | solution.py:267
  2.0 20.5 %all-to-all-start.9 = ((s32[64,1,128]{2,1,0:T(1,128)}), s32[64,1,128]{2,1,0:T(1,128)S(1)}, u32[]{:S(2)}, u32[]{:S(2)}) async-start(s32[64,1,128]{2,1,0:T(1,128)} %shard_map.55), calls=%async_computation.9 | async-start | bytes 65536 | tf_op jit(solution)/shard_map/all_to_all | solution.py:265
  22.5 0.6 copy-start
  99.8 9.5 %collective-permute-start.7 = (bf16[32,2,1,8,256]{4,3,2,1,0:T(8,128)(2,1)S(1)}, bf16[32,2,1,8,256]{4,3,2,1,0:T(8,128)(2,1)S(1)}, u32[]{:S(2)}, u32[]{:S(2)}) collective-permute-start(bf16[32,2,1,8,256]{4,3,2,1,0:T(8,128)(2,1)S(1)} %get-tuple-element.178), channel_id=1, source_target_pairs={{0,3},{1,0},{2,1},{3,2},{4,7},{5,4},{6,5},{7,6},{8,11},{9,8},{10,9... | collective-permute-start | bytes 786440 | tf_op jit(solution)/shard_map/ppermute | solution.py:289
  102.6 10.4 %collective-permute-start.5 = (bf16[32,2,1,8,256]{4,3,2,1,0:T(8,128)(2,1)S(1)}, bf16[32,2,1,8,256]{4,3,2,1,0:T(8,128)(2,1)S(1)}, u32[]{:S(2)}, u32[]{:S(2)}) collective-permute-start(bf16[32,2,1,8,256]{4,3,2,1,0:T(8,128)(2,1)S(1)} %get-tuple-element.178), channel_id=1, source_target_pairs={{0,1},{1,2},{2,3},{3,0},{4,5},{5,6},{6,7},{7,4},{8,9},{9,10},{10,1... | collective-permute-start | bytes 786440 | tf_op jit(solution)/shard_map/ppermute | solution.py:289
  102.6 12.3 %collective-permute-start.3 = (bf16[32,2,1,8,256]{4,3,2,1,0:T(8,128)(2,1)S(1)}, bf16[32,2,1,8,256]{4,3,2,1,0:T(8,128)(2,1)S(1)}, u32[]{:S(2)}, u32[]{:S(2)}) collective-permute-start(bf16[32,2,1,8,256]{4,3,2,1,0:T(8,128)(2,1)S(1)} %get-tuple-element.179), channel_id=1, source_target_pairs={{0,3},{1,0},{2,1},{3,2},{4,7},{5,4},{6,5},{7,6},{8,11},{9,8},{10,9... | collective-permute-start | bytes 786440 | tf_op jit(solution)/shard_map/ppermute | solution.py:289
  105.9 12.8 %collective-permute-start.1 = (bf16[32,2,1,8,256]{4,3,2,1,0:T(8,128)(2,1)S(1)}, bf16[32,2,1,8,256]{4,3,2,1,0:T(8,128)(2,1)S(1)}, u32[]{:S(2)}, u32[]{:S(2)}) collective-permute-start(bf16[32,2,1,8,256]{4,3,2,1,0:T(8,128)(2,1)S(1)} %get-tuple-element.179), channel_id=1, source_target_pairs={{0,1},{1,2},{2,3},{3,0},{4,5},{5,6},{6,7},{7,4},{8,9},{9,10},{10,1... | collective-permute-start | bytes 786440 | tf_op jit(solution)/shard_map/ppermute | solution.py:289
  109.3 9.6 %collective-permute-start.8 = (bf16[16,2,1,8,256]{4,3,2,1,0:T(8,128)(2,1)S(1)}, bf16[16,2,1,8,256]{4,3,2,1,0:T(8,128)(2,1)S(1)}, u32[]{:S(2)}, u32[]{:S(2)}) collective-permute-start(bf16[16,2,1,8,256]{4,3,2,1,0:T(8,128)(2,1)S(1)} %slice.49), channel_id=1, source_target_pairs={{0,3},{1,0},{2,1},{3,2},{4,7},{5,4},{6,5},{7,6},{8,11},{9,8},{10,9... | collective-permute-start | bytes 393224 | tf_op jit(solution)/shard_map/ppermute | solution.py:289
  113.1 7.4 %collective-permute-start.6 = (bf16[16,2,1,8,256]{4,3,2,1,0:T(8,128)(2,1)S(1)}, bf16[16,2,1,8,256]{4,3,2,1,0:T(8,128)(2,1)S(1)}, u32[]{:S(2)}, u32[]{:S(2)}) collective-permute-start(bf16[16,2,1,8,256]{4,3,2,1,0:T(8,128)(2,1)S(1)} %slice.48), channel_id=1, source_target_pairs={{0,1},{1,2},{2,3},{3,0},{4,5},{5,6},{6,7},{7,4},{8,9},{9,10},{10,1... | collective-permute-start | bytes 393224 | tf_op jit(solution)/shard_map/ppermute | solution.py:289
  114.9 9.6 %collective-permute-start.4 = (bf16[16,2,1,8,256]{4,3,2,1,0:T(8,128)(2,1)S(1)}, bf16[16,2,1,8,256]{4,3,2,1,0:T(8,128)(2,1)S(1)}, u32[]{:S(2)}, u32[]{:S(2)}) collective-permute-start(bf16[16,2,1,8,256]{4,3,2,1,0:T(8,128)(2,1)S(1)} %slice.46), channel_id=1, source_target_pairs={{0,3},{1,0},{2,1},{3,2},{4,7},{5,4},{6,5},{7,6},{8,11},{9,8},{10,9... | collective-permute-start | bytes 393224 | tf_op jit(solution)/shard_map/ppermute | solution.py:289
  118.7 6.3 %collective-permute-start.2 = (bf16[16,2,1,8,256]{4,3,2,1,0:T(8,128)(2,1)S(1)}, bf16[16,2,1,8,256]{4,3,2,1,0:T(8,128)(2,1)S(1)}, u32[]{:S(2)}, u32[]{:S(2)}) collective-permute-start(bf16[16,2,1,8,256]{4,3,2,1,0:T(8,128)(2,1)S(1)} %slice.45), channel_id=1, source_target_pairs={{0,1},{1,2},{2,3},{3,0},{4,5},{5,6},{6,7},{7,4},{8,9},{9,10},{10,1... | collective-permute-start | bytes 393224 | tf_op jit(solution)/shard_map/ppermute | solution.py:289
  129.1 4.0 %collective-permute-start.9 = (f32[2,8,512]{2,1,0:T(8,128)S(1)}, f32[2,8,512]{2,1,0:T(8,128)S(1)}, u32[]{:S(2)}, u32[]{:S(2)}) collective-permute-start(f32[2,8,512]{2,1,0:T(8,128)S(1)} %get-tuple-element.169), channel_id=1, source_target_pairs={{0,3},{1,0},{2,1},{3,2},{4,7},{5,4},{6,5},{7,6},{8,11},{9,8},{10,9... | collective-permute-start | bytes 98312 | tf_op jit(solution)/shard_map/ppermute | solution.py:289
  130.4 5.5 %collective-permute-start.10 = (f32[2,8,512]{2,1,0:T(8,128)S(1)}, f32[2,8,512]{2,1,0:T(8,128)S(1)}, u32[]{:S(2)}, u32[]{:S(2)}) collective-permute-start(f32[2,8,512]{2,1,0:T(8,128)S(1)} %get-tuple-element.170), channel_id=1, source_target_pairs={{0,2},{1,3},{2,0},{3,1},{4,6},{5,7},{6,4},{7,5},{8,10},{9,11},{10,... | collective-permute-start | bytes 98312 | tf_op jit(solution)/shard_map/ppermute | solution.py:289
  130.4 5.7 %collective-permute-start.11 = (f32[2,8,512]{2,1,0:T(8,128)S(1)}, f32[2,8,512]{2,1,0:T(8,128)S(1)}, u32[]{:S(2)}, u32[]{:S(2)}) collective-permute-start(f32[2,8,512]{2,1,0:T(8,128)S(1)} %get-tuple-element.171), channel_id=1, source_target_pairs={{0,1},{1,2},{2,3},{3,0},{4,5},{5,6},{6,7},{7,4},{8,9},{9,10},{10,1... | collective-permute-start | bytes 98312 | tf_op jit(solution)/shard_map/ppermute | solution.py:289

commit v3 on v2

--- a/solution.py
+++ b/solution.py
@@ -1,5 +1,4 @@
 import functools
-import math
 
 import jax
 import jax.numpy as jnp
@@ -12,7 +11,6 @@
 IMG_W = 64
 TGT_G = 8
 SHARPNESS_DIVISOR = 0.1
-LOG2E = math.log2(math.e)
 LANES = 128
 CORES = 2
 PLACE_BITS = 6
@@ -158,93 +156,131 @@
     )(index, spread)
 
 
-def match_kernel(image_rows, multiplier, pair, meta, maps, q1, q2a, q2b, q3, *refs):
-    *earlier, out0, out1, out2, out3, scores, column = refs
-    outs = (out0, out1, out2, out3)
-    quad = meta[0]
+def score_kernel(image_rows, multiplier, pair, meta, maps, near_query, near_target, products, rows, columns, scores, stats):
     chips, cores, entries, piece, width = maps.shape
-    target_entry = entries // 2 + pair
     part = chips * piece
     slab = cores * part
-    quads = len(outs)
-    for old, new in zip(earlier, outs):
-        new[0:pair] = old[...]
+    targets = ((maps, entries // 2 + pair), (near_target, 0))
+    queries = ((maps, pair), (near_query, 0))
 
     @pl.when(pair < meta[1])
     def _():
-        for row in range(cores):
-            rows = maps[:, row, target_entry].reshape(part, width)
-            blocks = ((0, 0, maps, pair), (1, 0, q1, 0), (2, 0, q2a, 0), (2, q2a.shape[0], q2b, 0), (3, 0, q3, 0))
-            for step, skip, query, entry in blocks:
-                tokens = query.shape[0] * piece
-                for core in range(cores):
-                    start = step * slab + core * part + skip * piece
-                    scores[row * part : (row + 1) * part, start : start + tokens] = (
-                        lax.dot_general(
-                            rows, query[:, core, entry].reshape(tokens, width), (((1,), (1,)), ((), ())),
-                            preferred_element_type=jnp.float32,
-                        )
-                        * multiplier
+        for row in range(2 * cores):
+            target, entry = targets[row // cores]
+            tokens = target[:, row % cores, entry].reshape(part, width)
+            for column in range(2 * cores):
+                query, entry = queries[column // cores]
+                scores[row * part : (row + 1) * part, column * part : (column + 1) * part] = (
+                    lax.dot_general(
+                        tokens, query[:, column % cores, entry].reshape(part, width), (((1,), (1,)), ((), ())),
+                        preferred_element_type=jnp.float32,
                     )
+                    * multiplier
+                )
+
+        first_lane = lax.broadcasted_iota(jnp.int32, (64, LANES), 1) == 0
 
         def rows_step(index, carry):
-            block = pl.ds(pl.multiple_of(index * 32, 32), 32)
+            block = pl.ds(pl.multiple_of(index * 64, 64), 64)
             top = jnp.max(scores[block, :], axis=1, keepdims=True)
-            powers = jnp.exp2(scores[block, :] - top)
-            column[block, :] = powers * (1.0 / jnp.sum(powers, axis=1, keepdims=True))
+            powers = jnp.exp(scores[block, :] - top)
+            products[block, :] = powers
+            stats[block, :] = jnp.where(first_lane, top, jnp.sum(powers, axis=1, keepdims=True))
             return carry
 
-        lax.fori_loop(0, slab // 32, rows_step, 0, unroll=4)
+        lax.fori_loop(0, 2 * slab // 64, rows_step, 0, unroll=4)
+        for start in range(0, 2 * slab, LANES):
+            columns[:, start : start + LANES] = stats[start : start + LANES, :].T[0:8, :]
 
         bands = slab // IMG_W
         along = lax.broadcasted_iota(jnp.int32, (IMG_W, LANES), 0).astype(jnp.float32)
         coord_x = (2.0 * along + 1.0) / IMG_W - 1.0
-        first_row = quad * bands
-        for step in range(quads):
-            out = outs[step]
-
-            def lanes_step(index, carry, step=step, out=out):
-                lanes = pl.ds(pl.multiple_of(step * slab + index * LANES, LANES), LANES)
-                top = jnp.max(scores[:, lanes], axis=0, keepdims=True)
-                total = jnp.zeros((8, LANES), jnp.float32)
-                weighted_y = jnp.zeros((8, LANES), jnp.float32)
-                mutual = jnp.zeros((8, LANES), jnp.float32)
-                folded = jnp.zeros((IMG_W, LANES), jnp.float32)
-                for band in range(bands):
-                    piece = slice(band * IMG_W, (band + 1) * IMG_W)
-                    powers = jnp.exp2(scores[piece, lanes] - top)
-                    folded += powers
-                    part = jnp.sum(powers.reshape(IMG_W // 8, 8, LANES), axis=0)
-                    total += part
-                    coord_y = (2.0 * (first_row + band).astype(jnp.float32) + 1.0) / image_rows - 1.0
-                    weighted_y += part * coord_y
-                    mutual += jnp.sum((powers * column[piece, lanes]).reshape(IMG_W // 8, 8, LANES), axis=0)
-                place = pl.ds(pl.multiple_of(index * LANES, LANES), LANES)
-                out[pair, 0:1, place] = top
-                out[pair, 1:2, place] = jnp.sum(total, axis=0, keepdims=True)
-                out[pair, 2:3, place] = jnp.sum(folded * coord_x, axis=0, keepdims=True)
-                out[pair, 3:4, place] = jnp.sum(weighted_y, axis=0, keepdims=True)
-                out[pair, 4:5, place] = jnp.sum(mutual, axis=0, keepdims=True)
-                return carry
-
-            lax.fori_loop(0, slab // LANES, lanes_step, 0, unroll=4)
-
-
-def match(image_rows, multiplier, pair, meta, queries, maps, earlier):
+
+        def lanes_step(index, carry):
+            lanes = pl.ds(pl.multiple_of(index * LANES, LANES), LANES)
+            top = jnp.max(scores[:, lanes], axis=0, keepdims=True)
+            total = jnp.zeros((8, LANES), jnp.float32)
+            weighted_y = jnp.zeros((8, LANES), jnp.float32)
+            folded = jnp.zeros((IMG_W, LANES), jnp.float32)
+            for band in range(2 * bands):
+                block = slice(band * IMG_W, (band + 1) * IMG_W)
+                powers = jnp.exp(scores[block, lanes] - top)
+                products[block, lanes] *= powers
+                folded += powers
+                sums = jnp.sum(powers.reshape(IMG_W // 8, 8, LANES), axis=0)
+                total += sums
+                image_row = meta[2 + band // bands] * bands + band % bands
+                weighted_y += sums * ((2.0 * image_row.astype(jnp.float32) + 1.0) / image_rows - 1.0)
+            rows[0:1, lanes] = top
+            rows[1:2, lanes] = jnp.sum(total, axis=0, keepdims=True)
+            rows[2:3, lanes] = jnp.sum(folded * coord_x, axis=0, keepdims=True)
+            rows[3:4, lanes] = jnp.sum(weighted_y, axis=0, keepdims=True)
+            return carry
+
+        lax.fori_loop(0, 2 * slab // LANES, lanes_step, 0, unroll=4)
+
+
+def score(image_rows, multiplier, pair, meta, maps, near_query, near_target):
     chips, cores, _, piece, width = maps.shape
-    quads = len(queries)
-    slab = chips * cores * piece
-    return pl.pallas_call(
-        functools.partial(match_kernel, image_rows, multiplier, pair),
-        in_specs=[SMEM] + [VMEM] * (1 + len(queries) + len(earlier)),
-        out_specs=[VMEM] * quads,
-        out_shape=[jax.ShapeDtypeStruct((pair + 1, 8, slab), jnp.float32)] * quads,
-        scratch_shapes=[pltpu.VMEM((slab, quads * slab), jnp.float32)] * 2,
-        compiler_params=pltpu.CompilerParams(vmem_limit_bytes=32 * 1024 * 1024),
+    tokens = 2 * chips * cores * piece
+    return pl.pallas_call(
+        functools.partial(score_kernel, image_rows, multiplier, pair),
+        in_specs=[SMEM] + [VMEM] * 3,
+        out_specs=[VMEM] * 3,
+        out_shape=[
+            jax.ShapeDtypeStruct((tokens, tokens), jnp.float32),
+            jax.ShapeDtypeStruct((8, tokens), jnp.float32),
+            jax.ShapeDtypeStruct((8, tokens), jnp.float32),
+        ],
+        scratch_shapes=[pltpu.VMEM((tokens, tokens), jnp.float32), pltpu.VMEM((tokens, LANES), jnp.float32)],
+        compiler_params=pltpu.CompilerParams(vmem_limit_bytes=20 * 1024 * 1024),
         cost_estimate=pl.CostEstimate(
-            flops=2 * slab * slab * quads * width, bytes_accessed=2 << 20, transcendentals=2 << 20
+            flops=2 * tokens * tokens * width, bytes_accessed=2 << 20, transcendentals=2 << 20
         ),
-    )(meta, maps, *queries, *earlier)
+    )(meta, maps, near_query, near_target)
+
+
+def mutual_kernel(pairs, meta, *refs):
+    products, rows, columns, others = (refs[pairs * kind : pairs * (kind + 1)] for kind in range(4))
+    kept, sent, weights = refs[4 * pairs :]
+    tokens = weights.shape[0]
+    slab = tokens // 2
+    for pair in range(pairs):
+
+        @pl.when(pair < meta[1])
+        def _():
+            for start in range(0, tokens, LANES):
+                here = slice(start, start + LANES)
+                there = slice((start + slab) % tokens, (start + slab) % tokens + LANES)
+                top = columns[pair][0:1, here]
+                other_top = others[pair][0:1, there]
+                highest = jnp.maximum(top, other_top)
+                scale = jnp.exp(top - highest)
+                total = columns[pair][1:2, here] * scale + others[pair][1:2, there] * jnp.exp(other_top - highest)
+                weights[here, :] = jnp.broadcast_to(scale / total, (LANES, LANES)).T
+
+            for half, out in enumerate((kept, sent)):
+                out[pair, 0:4, :] = rows[pair][0:4, half * slab : (half + 1) * slab]
+                for start in range(0, slab, LANES):
+                    lanes = slice(half * slab + start, half * slab + start + LANES)
+                    mutual = jnp.zeros((64, LANES), jnp.float32)
+                    for row in range(0, tokens, 64):
+                        mutual += products[pair][row : row + 64, lanes] * weights[row : row + 64, :]
+                    out[pair, 4:5, start : start + LANES] = jnp.sum(mutual, axis=0, keepdims=True)
+
+
+def mutual(meta, products, rows, columns, others):
+    pairs = len(products)
+    tokens = products[0].shape[0]
+    shape = jax.ShapeDtypeStruct((pairs, 8, tokens // 2), jnp.float32)
+    return pl.pallas_call(
+        functools.partial(mutual_kernel, pairs),
+        in_specs=[SMEM] + [VMEM] * (4 * pairs),
+        out_specs=[VMEM] * 2,
+        out_shape=[shape] * 2,
+        scratch_shapes=[pltpu.VMEM((tokens, LANES), jnp.float32)],
+        compiler_params=pltpu.CompilerParams(vmem_limit_bytes=20 * 1024 * 1024),
+    )(meta, *products, *rows, *columns, *others)
 
 
 def shards(picture_descriptors, image_slot, group_images, pair_target, pair_count):
@@ -259,7 +295,7 @@
     pairs = pair_target.shape[0]
     chip_rows = images_dev * cores
     image_rows = slab * quads // IMG_W
-    multiplier = LOG2E / (width * SHARPNESS_DIVISOR)
+    multiplier = 1.0 / (width * SHARPNESS_DIVISOR)
 
     def all_pairs(array):
         return lax.all_to_all(array, ("chip", "core"), split_axis=0, concat_axis=0, tiled=True)
@@ -269,7 +305,7 @@
     asked = all_pairs(announce(groups, image_slot, group_images, pair_target, pair_count))
 
     capacities = [size for size in CAPACITIES if size < chip_rows] + [chip_rows]
-    index, rows, branch = plan(chip_rows, 2 * pairs, capacities, chip[None], asked)
+    index, listed, branch = plan(chip_rows, 2 * pairs, capacities, chip[None], asked)
     halves = (images_dev, cores, chips, slab // groups, width)
 
     def exchange(capacity, operands):
@@ -281,24 +317,27 @@
     pieces = lax.switch(
         branch[0],
         [functools.partial(exchange, size) for size in capacities],
-        (picture_descriptors.reshape(halves), traded.reshape(halves), rows, index),
+        (picture_descriptors.reshape(halves), traded.reshape(halves), listed, index),
     )
     maps = all_pairs(pieces).reshape(chips, cores, *pieces.shape[1:])
 
-    def move(array, step):
-        return lax.ppermute(array, "quad", [(i, (i + step) % quads) for i in range(quads)])
-
-    meta = jnp.stack([quad, pair_count[0]])
-    partials = []
+    def trade(array, flip):
+        return lax.ppermute(array, "quad", [(i, i ^ flip) for i in range(quads)])
+
+    query_flip, target_flip = 1, quads - 1
+    meta = jnp.stack([quad, pair_count[0], quad, quad ^ target_flip])
+    products, rows, columns = [], [], []
     for pair in range(pairs):
-        query = maps[:, :, pair : pair + 1]
-        before = move(query, 1)
-        after = move(query, quads - 1)
-        across = (move(before[: chips // 2], 1), move(after[chips // 2 :], quads - 1))
-        partials = match(image_rows, multiplier, pair, meta, (before, *across, after), maps, partials)
-    partial = jnp.stack([partials[0]] + [move(partials[step], quads - step) for step in range(1, quads)])
+        near_query = trade(maps[:, :, pair : pair + 1], query_flip)
+        near_target = trade(maps[:, :, pairs + pair : pairs + pair + 1], target_flip)
+        parts = score(image_rows, multiplier, pair, meta, maps, near_query, near_target)
+        for kept, part in zip((products, rows, columns), parts):
+            kept.append(part)
+    others = [trade(column, target_flip) for column in columns]
+    kept, sent = mutual(meta, products, rows, columns, others)
+    partial = jnp.stack([kept, trade(sent, query_flip)])
     top = partial[:, :, 0]
-    weight = jnp.exp2(top - jnp.max(top, axis=0, keepdims=True))
+    weight = jnp.exp(top - jnp.max(top, axis=0, keepdims=True))
     total = jnp.sum(partial[:, :, 1] * weight, axis=0)
     fields = [jnp.sum(partial[:, :, 2 + field] * weight, axis=0) / total for field in range(3)]
     in_use = jnp.arange(pairs, dtype=jnp.int32) < pair_count[0]

time: 136 us -> 132 us (0.971)
  the two profiles are of different devices: /device:TPU:32 before, /device:TPU:40 now
where the time goes in v3:
time: 132 us; the launch traced here: 134 us
  blocking collectives  70 us (53%)
  waiting for transfers between devices  21.9 us (17%)
  starting transfers between devices  20.1 us (15%)
  Pallas kernels  19.1 us (14%)
  between operations  1.38 us (1%)
    all_to_all x1, blocking collectives, exchange(): lax.all_to_all(pieces, 'chip', split_axis=0, concat_axis=0, tiled=True)  36.7 us
    all_to_all x1, blocking collectives, all_pairs(): lax.all_to_all(array, ('chip', 'core'), split_axis=0, concat_axis=0, tile...  33.3 us
    ppermute x7, waiting for transfers between devices, trade(): return lax.ppermute(array, 'quad', [(i, i ^ flip) for i in range(quads)])  14.1 us
    all_to_all x1, starting transfers between devices, all_pairs(): lax.all_to_all(array, ('chip', 'core'), split_axis=0, concat_axis=0, tile...  11.8 us
    pallas_call x2, Pallas kernels, score(): pl.pallas_call(functools.partial(score_kernel, image_rows, multiplier, pa...  9.55 us
    ppermute x7, starting transfers between devices, trade(): return lax.ppermute(array, 'quad', [(i, i ^ flip) for i in range(quads)])  8.38 us
    all_to_all x1, waiting for transfers between devices, all_pairs(): lax.all_to_all(array, ('chip', 'core'), split_axis=0, concat_axis=0, tile...  7.72 us
  transfers between devices with their start and end apart: 9, of which 5 were waited for; matrix products, arithmetic and copies ran while one was open for 0% of the time, Pallas kernels for 10%

profile of v3, /device:TPU:40, one launch (start us, length us, event | category | flops | bytes accessed | tf_op | source)
XLA Modules:
  0.0 134.1 jit_solution(5864739393968770627)
XLA Ops:
  0.0 0.0 collective-permute-start
  0.7 1.4 %shard_map.55 = s32[64,1,128]{2,1,0:T(1,128)} custom-call(s32[1024]{0:T(1024)} %image_slot.1, s32[10]{0:T(128)} %group_images.1, s32[2]{0:T(128)} %pair_target.1, s32[1]{0:T(128)} %copy.54.pair_count), custom_call_target="tpu_custom_call" | custom-call | tf_op jit(solution)/shard_map/pallas_call | solution.py:36
  2.0 11.8 %all-to-all-start.9 = ((s32[64,1,128]{2,1,0:T(1,128)}), s32[64,1,128]{2,1,0:T(1,128)S(1)}, u32[]{:S(2)}, u32[]{:S(2)}) async-start(s32[64,1,128]{2,1,0:T(1,128)} %shard_map.55), calls=%async_computation.9 | async-start | bytes 65536 | tf_op jit(solution)/shard_map/all_to_all | solution.py:301
  13.8 7.7 %all-to-all-done.9.asked = s32[64,1,128]{2,1,0:T(1,128)S(1)} async-done(((s32[64,1,128]{2,1,0:T(1,128)}), s32[64,1,128]{2,1,0:T(1,128)S(1)}, u32[]{:S(2)}, u32[]{:S(2)}) %all-to-all-start.9) | async-done | bytes 32800 | tf_op jit(solution)/shard_map/all_to_all | solution.py:301
  21.5 0.0 copy-start
  21.5 0.6 copy-done
  22.1 2.6 %shard_map.56 = (s32[64,128]{1,0:T(8,128)S(1)}, s32[32,128]{1,0:T(8,128)S(1)}, s32[1]{0:T(128)}) custom-call(s32[1]{0:T(128)} %bitcast.12.chip, s32[64,1,128]{2,1,0:T(1,128)} %copy-done), custom_call_target="tpu_custom_call" | custom-call | tf_op jit(solution)/shard_map/pallas_call | solution.py:87
  25.3 0.0 collective-permute-done
  25.4 41.0 %conditional.1 = (bf16[64,4,8,256]{3,2,1,0:T(8,128)(2,1)S(1)}) conditional(s32[]{:T(128)} %bitcast.13, (s32[]{:T(128)}, s32[32,128]{1,0:T(8,128)S(1)}, bf16[16,2,32,8,256]{4,3,2,1,0:T(8,128)(2,1)}, bf16[16,2,32,8,256]{4,3,2,1,0:T(8,128)(2,1)}, s32[64,128]{1,0:T(8,128)S(1)}) %tuple.56, (s32[]{:T(128)}, ...), branch_computations={%region_0.0_spmd, %region_1.0_spmd, %region_2.0_spmd, %region_3.0_... | conditional | bytes 8388616 | solution.py:317
  25.4 2.5 %branch_3_fun.2 = bf16[32,9,8,256]{3,2,1,0:T(8,128)(2,1)S(1)} custom-call(s32[1]{0:T(128)} %bitcast.3.core, s32[32,128]{1,0:T(8,128)S(1)} %get-tuple-element.122.rows, bf16[16,2,32,8,256]{4,3,2,1,0:T(8,128)(2,1)} %get-tuple-element.123.own, bf16[16,2,32,8,256]{4,3,2,1,0:T(8,128)(2,1)} %get-tuple-element.124.other), custom_call_target="tpu_custom_call" | custom-call | tf_op jit(solution)/shard_map/cond/branch_3_fun/pallas_call | solution.py:127
  27.9 36.7 %all_to_all.49.spread = bf16[32,9,8,256]{3,2,1,0:T(8,128)(2,1)S(1)} all-to-all(bf16[32,9,8,256]{3,2,1,0:T(8,128)(2,1)S(1)} %branch_3_fun.2), channel_id=1, replica_groups=mesh['chip'=32,'core'=2,'quad'=4] {'chip'}, dimensions={0} | all-to-all | bytes 2359296 | tf_op jit(solution)/shard_map/cond/branch_3_fun/all_to_all | solution.py:314
  64.6 1.7 %branch_3_fun.3 = bf16[64,4,8,256]{3,2,1,0:T(8,128)(2,1)S(1)} custom-call(s32[64,128]{1,0:T(8,128)S(1)} %get-tuple-element.120.index, bf16[32,9,8,256]{3,2,1,0:T(8,128)(2,1)S(1)} %all_to_all.49.spread), custom_call_target="tpu_custom_call" | custom-call | tf_op jit(solution)/shard_map/cond/branch_3_fun/pallas_call | solution.py:150
  66.3 33.3 %all_to_all.55 = bf16[64,4,8,256]{3,2,1,0:T(8,128)(2,1)S(1)} all-to-all(bf16[64,4,8,256]{3,2,1,0:T(8,128)(2,1)S(1)} %get-tuple-element.191), channel_id=1, replica_groups=mesh['chip'=32,'core'=2,'quad'=4] {'chip','core'}, dimensions={0} | all-to-all | bytes 2097152 | tf_op jit(solution)/shard_map/all_to_all | solution.py:301
  99.7 0.1 fusion.11
  99.8 2.8 %collective-permute-start.2 = (bf16[32,2,1,8,256]{4,3,2,1,0:T(8,128)(2,1)S(1)}, bf16[32,2,1,8,256]{4,3,2,1,0:T(8,128)(2,1)S(1)}, u32[]{:S(2)}, u32[]{:S(2)}) collective-permute-start(bf16[32,2,1,8,256]{4,3,2,1,0:T(8,128)(2,1)S(1)} %get-tuple-element.180), channel_id=1, source_target_pairs={{0,3},{1,2},{2,1},{3,0},{4,7},{5,6},{6,5},{7,4},{8,11},{9,10},{10,... | collective-permute-start | bytes 786440 | tf_op jit(solution)/shard_map/ppermute | solution.py:325
  102.6 0.2 collective-permute-start.1
  102.8 1.1 collective-permute-start.4
  104.0 0.7 collective-permute-start.3
  104.6 0.1 pad_add_fusion.meta
  104.7 5.6 %collective-permute-done.2.near_target = bf16[32,2,1,8,256]{4,3,2,1,0:T(8,128)(2,1)S(1)} collective-permute-done((bf16[32,2,1,8,256]{4,3,2,1,0:T(8,128)(2,1)S(1)}, bf16[32,2,1,8,256]{4,3,2,1,0:T(8,128)(2,1)S(1)}, u32[]{:S(2)}, u32[]{:S(2)}) %collective-permute-start.2) | collective-permute-done | bytes 262176 | tf_op jit(solution)/shard_map/ppermute | solution.py:325
  110.3 1.6 %collective-permute-done.1.near_query = bf16[32,2,1,8,256]{4,3,2,1,0:T(8,128)(2,1)S(1)} collective-permute-done((bf16[32,2,1,8,256]{4,3,2,1,0:T(8,128)(2,1)S(1)}, bf16[32,2,1,8,256]{4,3,2,1,0:T(8,128)(2,1)S(1)}, u32[]{:S(2)}, u32[]{:S(2)}) %collective-permute-start.1) | collective-permute-done | bytes 262176 | tf_op jit(solution)/shard_map/ppermute | solution.py:325
  111.8 4.8 %shard_map.57 = (f32[1024,1024]{1,0:T(8,128)S(1)}, f32[8,1024]{1,0:T(8,128)S(1)}, f32[8,1024]{1,0:T(8,128)S(1)}) custom-call(s32[4]{0:T(128)S(1)} %pad_add_fusion.meta, bf16[32,2,4,8,256]{4,3,2,1,0:T(8,128)(2,1)S(1)} %bitcast.65, bf16[32,2,1,8,256]{4,3,2,1,0:T(8,128)(2,1)S(1)} %collective-permute-done.1.near_query, ...), custom_call_target="tpu_custom_call" | custom-call | flops 536870912 | bytes 2097152 | tf_op jit(solution)/shard_map/pallas_call | solution.py:226
  116.6 1.3 collective-permute-start.5
  117.9 0.0 collective-permute-done.4.near_target
  117.9 0.0 collective-permute-done.3.near_query
  117.9 4.8 %shard_map.58 = (f32[1024,1024]{1,0:T(8,128)S(1)}, f32[8,1024]{1,0:T(8,128)S(1)}, f32[8,1024]{1,0:T(8,128)S(1)}) custom-call(s32[4]{0:T(128)S(1)} %pad_add_fusion.meta, bf16[32,2,4,8,256]{4,3,2,1,0:T(8,128)(2,1)S(1)} %bitcast.66, bf16[32,2,1,8,256]{4,3,2,1,0:T(8,128)(2,1)S(1)} %collective-permute-done.3.near_query, ...), custom_call_target="tpu_custom_call" | custom-call | flops 536870912 | bytes 2097152 | tf_op jit(solution)/shard_map/pallas_call | solution.py:226
  122.7 2.1 %collective-permute-start.6 = (f32[8,1024]{1,0:T(8,128)S(1)}, f32[8,1024]{1,0:T(8,128)S(1)}, u32[]{:S(2)}, u32[]{:S(2)}) collective-permute-start(f32[8,1024]{1,0:T(8,128)S(1)} %get-tuple-element.169.refs_5_), channel_id=1, source_target_pairs={{0,3},{1,2},{2,1},{3,0},{4,7},{5,6},{6,5},{7,4},{8,11},{9,10},{10,... | collective-permute-start | bytes 98312 | tf_op jit(solution)/shard_map/ppermute | solution.py:325
  124.8 0.0 collective-permute-done.5.refs_6_
  124.8 3.1 %collective-permute-done.6.refs_7_ = f32[8,1024]{1,0:T(8,128)S(1)} collective-permute-done((f32[8,1024]{1,0:T(8,128)S(1)}, f32[8,1024]{1,0:T(8,128)S(1)}, u32[]{:S(2)}, u32[]{:S(2)}) %collective-permute-start.6) | collective-permute-done | bytes 32800 | tf_op jit(solution)/shard_map/ppermute | solution.py:325
  127.9 1.4 %shard_map.59 = (f32[2,8,512]{2,1,0:T(8,128)S(1)}, f32[2,8,512]{2,1,0:T(8,128)S(1)}) custom-call(s32[4]{0:T(128)S(1)} %pad_add_fusion.meta, f32[1024,1024]{1,0:T(8,128)S(1)} %get-tuple-element.164.refs_0_, f32[1024,1024]{1,0:T(8,128)S(1)} %get-tuple-element.165.refs_1_, f32[8,1024]{1,0:T(8,128)S(1)} %get-tuple-element.166.refs_2_, ...), custom_call_target="tpu_custom_call" | custom-call | tf_op jit(solution)/shard_map/pallas_call | solution.py:276
  129.3 0.1 collective-permute-start.7
  129.5 3.9 %collective-permute-done.7 = f32[2,8,512]{2,1,0:T(8,128)S(1)} collective-permute-done((f32[2,8,512]{2,1,0:T(8,128)S(1)}, f32[2,8,512]{2,1,0:T(8,128)S(1)}, u32[]{:S(2)}, u32[]{:S(2)}) %collective-permute-start.7) | collective-permute-done | bytes 32800 | tf_op jit(solution)/shard_map/ppermute | solution.py:325
  133.5 0.7 fusion
  (4 shorter events, 0.1 us)
Async XLA Ops:
  0.0 25.4 %collective-permute-start = (bf16[16,512,256]{2,1,0:T(8,128)(2,1)}, bf16[16,512,256]{2,1,0:T(8,128)(2,1)}, u32[]{:S(2)}, u32[]{:S(2)}) collective-permute-start(bf16[16,512,256]{2,1,0:T(8,128)(2,1)} %param.14), channel_id=1, source_target_pairs={{0,4},{4,0},{1,5},{5,1},{2,6},{6,2},{3,7},{7,3},{8,12},{12,8},{9,1... | collective-permute-start | bytes 12582920 | tf_op jit(solution)/shard_map/ppermute | solution.py:303
  2.0 19.5 %all-to-all-start.9 = ((s32[64,1,128]{2,1,0:T(1,128)}), s32[64,1,128]{2,1,0:T(1,128)S(1)}, u32[]{:S(2)}, u32[]{:S(2)}) async-start(s32[64,1,128]{2,1,0:T(1,128)} %shard_map.55), calls=%async_computation.9 | async-start | bytes 65536 | tf_op jit(solution)/shard_map/all_to_all | solution.py:301
  21.5 0.6 copy-start
  99.8 10.5 %collective-permute-start.2 = (bf16[32,2,1,8,256]{4,3,2,1,0:T(8,128)(2,1)S(1)}, bf16[32,2,1,8,256]{4,3,2,1,0:T(8,128)(2,1)S(1)}, u32[]{:S(2)}, u32[]{:S(2)}) collective-permute-start(bf16[32,2,1,8,256]{4,3,2,1,0:T(8,128)(2,1)S(1)} %get-tuple-element.180), channel_id=1, source_target_pairs={{0,3},{1,2},{2,1},{3,0},{4,7},{5,6},{6,5},{7,4},{8,11},{9,10},{10,... | collective-permute-start | bytes 786440 | tf_op jit(solution)/shard_map/ppermute | solution.py:325
  102.6 9.2 %collective-permute-start.1 = (bf16[32,2,1,8,256]{4,3,2,1,0:T(8,128)(2,1)S(1)}, bf16[32,2,1,8,256]{4,3,2,1,0:T(8,128)(2,1)S(1)}, u32[]{:S(2)}, u32[]{:S(2)}) collective-permute-start(bf16[32,2,1,8,256]{4,3,2,1,0:T(8,128)(2,1)S(1)} %get-tuple-element.181), channel_id=1, source_target_pairs={{0,1},{1,0},{2,3},{3,2},{4,5},{5,4},{6,7},{7,6},{8,9},{9,8},{10,11... | collective-permute-start | bytes 786440 | tf_op jit(solution)/shard_map/ppermute | solution.py:325
  102.8 15.1 %collective-permute-start.4 = (bf16[32,2,1,8,256]{4,3,2,1,0:T(8,128)(2,1)S(1)}, bf16[32,2,1,8,256]{4,3,2,1,0:T(8,128)(2,1)S(1)}, u32[]{:S(2)}, u32[]{:S(2)}) collective-permute-start(bf16[32,2,1,8,256]{4,3,2,1,0:T(8,128)(2,1)S(1)} %get-tuple-element.178), channel_id=1, source_target_pairs={{0,3},{1,2},{2,1},{3,0},{4,7},{5,6},{6,5},{7,4},{8,11},{9,10},{10,... | collective-permute-start | bytes 786440 | tf_op jit(solution)/shard_map/ppermute | solution.py:325
  104.0 14.0 %collective-permute-start.3 = (bf16[32,2,1,8,256]{4,3,2,1,0:T(8,128)(2,1)S(1)}, bf16[32,2,1,8,256]{4,3,2,1,0:T(8,128)(2,1)S(1)}, u32[]{:S(2)}, u32[]{:S(2)}) collective-permute-start(bf16[32,2,1,8,256]{4,3,2,1,0:T(8,128)(2,1)S(1)} %get-tuple-element.179), channel_id=1, source_target_pairs={{0,1},{1,0},{2,3},{3,2},{4,5},{5,4},{6,7},{7,6},{8,9},{9,8},{10,11... | collective-permute-start | bytes 786440 | tf_op jit(solution)/shard_map/ppermute | solution.py:325
  116.6 8.2 %collective-permute-start.5 = (f32[8,1024]{1,0:T(8,128)S(1)}, f32[8,1024]{1,0:T(8,128)S(1)}, u32[]{:S(2)}, u32[]{:S(2)}) collective-permute-start(f32[8,1024]{1,0:T(8,128)S(1)} %get-tuple-element.168.refs_4_), channel_id=1, source_target_pairs={{0,3},{1,2},{2,1},{3,0},{4,7},{5,6},{6,5},{7,4},{8,11},{9,10},{10,... | collective-permute-start | bytes 98312 | tf_op jit(solution)/shard_map/ppermute | solution.py:325
  122.7 5.2 %collective-permute-start.6 = (f32[8,1024]{1,0:T(8,128)S(1)}, f32[8,1024]{1,0:T(8,128)S(1)}, u32[]{:S(2)}, u32[]{:S(2)}) collective-permute-start(f32[8,1024]{1,0:T(8,128)S(1)} %get-tuple-element.169.refs_5_), channel_id=1, source_target_pairs={{0,3},{1,2},{2,1},{3,0},{4,7},{5,6},{6,5},{7,4},{8,11},{9,10},{10,... | collective-permute-start | bytes 98312 | tf_op jit(solution)/shard_map/ppermute | solution.py:325
  129.3 4.0 %collective-permute-start.7 = (f32[2,8,512]{2,1,0:T(8,128)S(1)}, f32[2,8,512]{2,1,0:T(8,128)S(1)}, u32[]{:S(2)}, u32[]{:S(2)}) collective-permute-start(f32[2,8,512]{2,1,0:T(8,128)S(1)} %get-tuple-element.171), channel_id=1, source_target_pairs={{0,1},{1,0},{2,3},{3,2},{4,5},{5,4},{6,7},{7,6},{8,9},{9,8},{10,11... | collective-permute-start | bytes 98312 | tf_op jit(solution)/shard_map/ppermute | solution.py:325

commit v4 on v3

--- a/solution.py
+++ b/solution.py
@@ -41,64 +41,56 @@
     )(image_slot, group_images, pair_target, pair_count)
 
 
-def plan_kernel(chip_rows, entries, capacities, chip, asked, index, rows, branch, requested, before):
+def plan_kernel(chip_rows, entries, capacities, chip, asked, index, rows, branch):
     groups = asked.shape[0]
-    table = asked[:, 0, :]
-    lane = lax.broadcasted_iota(jnp.int32, (groups, LANES), 1)
-    chips, locals_ = [], []
-    count = jnp.zeros((LANES, LANES), jnp.float32)
+    table = asked[...].T
+    chips_of, rows_of, stored_of = [], [], []
+    wide = lax.broadcasted_iota(jnp.int32, (chip_rows, groups), 0)
+    count = jnp.zeros((chip_rows, chip_rows), jnp.float32)
     for entry in range(entries):
-        stored = table[:, entry : entry + 1]
-        chips.append(jnp.where(lax.div(stored, chip_rows) == lane, 1.0, 0.0) * jnp.where(stored >= 0, 1.0, 0.0))
-        locals_.append(jnp.where(lax.rem(stored, chip_rows) == lane, 1.0, 0.0))
+        stored = table[entry : entry + 1, :]
+        valid = jnp.where(stored >= 0, 1.0, 0.0)
+        stored_of.append(jnp.maximum(stored, 0))
+        chips_of.append(jnp.where(lax.div(stored_of[-1], chip_rows) == wide, valid, 0.0))
+        rows_of.append(jnp.where(lax.rem(stored_of[-1], chip_rows) == wide, 1.0, 0.0))
         count += lax.dot_general(
-            chips[-1], locals_[-1], (((0,), (0,)), ((), ())), preferred_element_type=jnp.float32
+            rows_of[-1], chips_of[-1], (((1,), (1,)), ((), ())), preferred_element_type=jnp.float32
         )
     flags = jnp.where(count > 0.0, 1.0, 0.0)
-    first = lax.broadcasted_iota(jnp.int32, (LANES, LANES), 0)
-    second = lax.broadcasted_iota(jnp.int32, (LANES, LANES), 1)
-    earlier = jnp.dot(flags, jnp.where(first < second, 1.0, 0.0), preferred_element_type=jnp.float32)
-    requested[...] = flags
-    before[...] = earlier
+    first = lax.broadcasted_iota(jnp.int32, (chip_rows, chip_rows), 0)
+    second = lax.broadcasted_iota(jnp.int32, (chip_rows, chip_rows), 1)
+    earlier = jnp.dot(jnp.where(second < first, 1.0, 0.0), flags, preferred_element_type=jnp.float32)
     most = jnp.max(earlier + flags)
     choice = jnp.int32(0)
     for capacity in capacities[:-1]:
         choice += jnp.where(most > capacity, 1, 0)
     branch[0] = choice
 
-    codes = jnp.zeros((groups, LANES), jnp.int32)
+    here = second == chip[0]
+    my_flag = jnp.max(jnp.where(here, flags, 0.0), axis=1, keepdims=True)
+    my_place = jnp.max(jnp.where(here, earlier, 0.0), axis=1, keepdims=True)
+    slot = lax.broadcasted_iota(jnp.int32, (chip_rows, LANES), 1).astype(jnp.float32)
+    row = lax.broadcasted_iota(jnp.int32, (chip_rows, LANES), 0).astype(jnp.float32)
+    chosen = jnp.where((my_flag > 0.0) & (my_place == slot), row, 0.0)
+    rows[...] = jnp.broadcast_to(jnp.sum(chosen, axis=0, keepdims=True), rows.shape).astype(jnp.int32)
+
     for entry in range(entries):
-        places = jnp.dot(chips[entry], earlier, preferred_element_type=jnp.float32) * locals_[entry]
-        place = jnp.sum(places, axis=1, keepdims=True).astype(jnp.int32)
-        stored = jnp.maximum(table[:, entry : entry + 1], 0)
-        codes = jnp.where(lane == entry, lax.div(stored, chip_rows) * PLACES + place, codes)
-    index[...] = codes
-
-    mine = chip[0]
-    slot = lax.broadcasted_iota(jnp.int32, (chip_rows, LANES), 0).astype(jnp.float32)
-    along = lax.broadcasted_iota(jnp.int32, (chip_rows, LANES), 1).astype(jnp.float32)
-    chosen = (requested[pl.ds(mine, 1), :] > 0.0) & (before[pl.ds(mine, 1), :] == slot)
-    row = jnp.sum(jnp.where(chosen, along, 0.0), axis=1, keepdims=True)
-    rows[...] = jnp.broadcast_to(row.astype(jnp.int32), rows.shape)
+        places = jnp.dot(earlier, chips_of[entry], preferred_element_type=jnp.float32) * rows_of[entry]
+        place = jnp.sum(places, axis=0, keepdims=True).astype(jnp.int32)
+        index[entry : entry + 1, :] = lax.div(stored_of[entry], chip_rows) * PLACES + place
 
 
 def plan(chip_rows, entries, capacities, chip, asked):
     groups = asked.shape[0]
     return pl.pallas_call(
         functools.partial(plan_kernel, chip_rows, entries, capacities),
-        grid=(1,),
-        in_specs=[SMEM, pl.BlockSpec(asked.shape, lambda step: (0, 0, 0))],
-        out_specs=(
-            pl.BlockSpec((groups, LANES), lambda step: (0, 0)),
-            pl.BlockSpec((chip_rows, LANES), lambda step: (0, 0)),
-            SMEM,
-        ),
+        in_specs=[SMEM, VMEM],
+        out_specs=(VMEM, VMEM, SMEM),
         out_shape=(
-            jax.ShapeDtypeStruct((groups, LANES), jnp.int32),
-            jax.ShapeDtypeStruct((chip_rows, LANES), jnp.int32),
+            jax.ShapeDtypeStruct((8, groups), jnp.int32),
+            jax.ShapeDtypeStruct((8, LANES), jnp.int32),
             jax.ShapeDtypeStruct((1,), jnp.int32),
         ),
-        scratch_shapes=[pltpu.VMEM((LANES, LANES), jnp.float32)] * 2,
     )(chip, asked)
 
 
@@ -106,7 +98,7 @@
     images_dev = own.shape[0]
     capacity = out.shape[1]
     for slot in range(capacity):
-        row = rows[slot, 0]
+        row = rows[0, slot]
         local = lax.rem(row, images_dev)
         is_own = lax.div(row, images_dev) == core[0]
 
@@ -139,7 +131,7 @@
 
     def step(group, carry):
         for entry in range(entries):
-            code = index[group, entry]
+            code = index[entry, group]
             out[group, entry] = spread[code >> PLACE_BITS, code & (PLACES - 1)]
         return carry
 
@@ -156,7 +148,10 @@
     )(index, spread)
 
 
-def score_kernel(image_rows, multiplier, pair, meta, maps, near_query, near_target, products, rows, columns, scores, stats):
+def score_kernel(image_rows, multiplier, pair, meta, maps, near_query, near_target, *refs):
+    *earlier, products, rows, columns, scores, stats = refs
+    for previous in earlier:
+        columns[0:pair] = previous[...]
     chips, cores, entries, piece, width = maps.shape
     part = chips * piece
     slab = cores * part
@@ -188,9 +183,9 @@
             stats[block, :] = jnp.where(first_lane, top, jnp.sum(powers, axis=1, keepdims=True))
             return carry
 
-        lax.fori_loop(0, 2 * slab // 64, rows_step, 0, unroll=4)
+        lax.fori_loop(0, 2 * slab // 64, rows_step, 0, unroll=16)
         for start in range(0, 2 * slab, LANES):
-            columns[:, start : start + LANES] = stats[start : start + LANES, :].T[0:8, :]
+            columns[pair, :, start : start + LANES] = stats[start : start + LANES, :].T[0:8, :]
 
         bands = slab // IMG_W
         along = lax.broadcasted_iota(jnp.int32, (IMG_W, LANES), 0).astype(jnp.float32)
@@ -217,32 +212,32 @@
             rows[3:4, lanes] = jnp.sum(weighted_y, axis=0, keepdims=True)
             return carry
 
-        lax.fori_loop(0, 2 * slab // LANES, lanes_step, 0, unroll=4)
-
-
-def score(image_rows, multiplier, pair, meta, maps, near_query, near_target):
+        lax.fori_loop(0, 2 * slab // LANES, lanes_step, 0, unroll=8)
+
+
+def score(image_rows, multiplier, pair, meta, maps, near_query, near_target, earlier):
     chips, cores, _, piece, width = maps.shape
     tokens = 2 * chips * cores * piece
     return pl.pallas_call(
         functools.partial(score_kernel, image_rows, multiplier, pair),
-        in_specs=[SMEM] + [VMEM] * 3,
+        in_specs=[SMEM] + [VMEM] * (3 + len(earlier)),
         out_specs=[VMEM] * 3,
         out_shape=[
             jax.ShapeDtypeStruct((tokens, tokens), jnp.float32),
             jax.ShapeDtypeStruct((8, tokens), jnp.float32),
-            jax.ShapeDtypeStruct((8, tokens), jnp.float32),
+            jax.ShapeDtypeStruct((pair + 1, 8, tokens), jnp.float32),
         ],
         scratch_shapes=[pltpu.VMEM((tokens, tokens), jnp.float32), pltpu.VMEM((tokens, LANES), jnp.float32)],
         compiler_params=pltpu.CompilerParams(vmem_limit_bytes=20 * 1024 * 1024),
         cost_estimate=pl.CostEstimate(
             flops=2 * tokens * tokens * width, bytes_accessed=2 << 20, transcendentals=2 << 20
         ),
-    )(meta, maps, near_query, near_target)
+    )(meta, maps, near_query, near_target, *earlier)
 
 
 def mutual_kernel(pairs, meta, *refs):
-    products, rows, columns, others = (refs[pairs * kind : pairs * (kind + 1)] for kind in range(4))
-    kept, sent, weights = refs[4 * pairs :]
+    products, rows = refs[:pairs], refs[pairs : 2 * pairs]
+    columns, others, kept, sent, weights = refs[2 * pairs :]
     tokens = weights.shape[0]
     slab = tokens // 2
     for pair in range(pairs):
@@ -252,11 +247,11 @@
             for start in range(0, tokens, LANES):
                 here = slice(start, start + LANES)
                 there = slice((start + slab) % tokens, (start + slab) % tokens + LANES)
-                top = columns[pair][0:1, here]
-                other_top = others[pair][0:1, there]
+                top = columns[pair, 0:1, here]
+                other_top = others[pair, 0:1, there]
                 highest = jnp.maximum(top, other_top)
                 scale = jnp.exp(top - highest)
-                total = columns[pair][1:2, here] * scale + others[pair][1:2, there] * jnp.exp(other_top - highest)
+                total = columns[pair, 1:2, here] * scale + others[pair, 1:2, there] * jnp.exp(other_top - highest)
                 weights[here, :] = jnp.broadcast_to(scale / total, (LANES, LANES)).T
 
             for half, out in enumerate((kept, sent)):
@@ -275,12 +270,12 @@
     shape = jax.ShapeDtypeStruct((pairs, 8, tokens // 2), jnp.float32)
     return pl.pallas_call(
         functools.partial(mutual_kernel, pairs),
-        in_specs=[SMEM] + [VMEM] * (4 * pairs),
+        in_specs=[SMEM] + [VMEM] * (2 * pairs + 2),
         out_specs=[VMEM] * 2,
         out_shape=[shape] * 2,
         scratch_shapes=[pltpu.VMEM((tokens, LANES), jnp.float32)],
         compiler_params=pltpu.CompilerParams(vmem_limit_bytes=20 * 1024 * 1024),
-    )(meta, *products, *rows, *columns, *others)
+    )(meta, *products, *rows, columns, others)
 
 
 def shards(picture_descriptors, image_slot, group_images, pair_target, pair_count):
@@ -305,7 +300,7 @@
     asked = all_pairs(announce(groups, image_slot, group_images, pair_target, pair_count))
 
     capacities = [size for size in CAPACITIES if size < chip_rows] + [chip_rows]
-    index, listed, branch = plan(chip_rows, 2 * pairs, capacities, chip[None], asked)
+    index, listed, branch = plan(chip_rows, 2 * pairs, capacities, chip[None], asked.reshape(groups, LANES))
     halves = (images_dev, cores, chips, slab // groups, width)
 
     def exchange(capacity, operands):
@@ -326,15 +321,15 @@
 
     query_flip, target_flip = 1, quads - 1
     meta = jnp.stack([quad, pair_count[0], quad, quad ^ target_flip])
-    products, rows, columns = [], [], []
+    products, rows, columns = [], [], ()
     for pair in range(pairs):
         near_query = trade(maps[:, :, pair : pair + 1], query_flip)
         near_target = trade(maps[:, :, pairs + pair : pairs + pair + 1], target_flip)
-        parts = score(image_rows, multiplier, pair, meta, maps, near_query, near_target)
-        for kept, part in zip((products, rows, columns), parts):
-            kept.append(part)
-    others = [trade(column, target_flip) for column in columns]
-    kept, sent = mutual(meta, products, rows, columns, others)
+        product, row, column = score(image_rows, multiplier, pair, meta, maps, near_query, near_target, columns)
+        products.append(product)
+        rows.append(row)
+        columns = (column,)
+    kept, sent = mutual(meta, products, rows, columns[0], trade(columns[0], target_flip))
     partial = jnp.stack([kept, trade(sent, query_flip)])
     top = partial[:, :, 0]
     weight = jnp.exp(top - jnp.max(top, axis=0, keepdims=True))

time: 132 us -> 126 us (0.955); the launches traced: 134 us -> 127 us
  Pallas kernels: 19.1 us -> 11.6 us
  starting transfers between devices: 20.1 us -> 18.3 us
  waiting for transfers between devices: 21.9 us -> 23.7 us
    pallas_call x2, Pallas kernels: 9.55 us -> 4.06 us  [score(): pl.pallas_call(functools.partial(score_kernel, image_rows, multiplier, pa...]
    ppermute x7 -> x6, starting transfers between devices: 8.38 us -> 6.55 us  [trade(): return lax.ppermute(array, 'quad', [(i, i ^ flip) for i in range(quads)])]
    ppermute x7 -> x6, waiting for transfers between devices: 14.1 us -> 16 us  [trade(): return lax.ppermute(array, 'quad', [(i, i ^ flip) for i in range(quads)])]
  transfers between devices with their start and end apart: 9 -> 8, of which waited for: 5 -> 6; matrix products, arithmetic and copies ran while one was open for 0% -> 0% of each run, Pallas kernels for 10% -> 5%
where the time goes in v4:
time: 126 us; the launch traced here: 127 us
  blocking collectives  70 us (56%)
  waiting for transfers between devices  23.7 us (19%)
  starting transfers between devices  18.3 us (15%)
  Pallas kernels  11.6 us (9%)
  between operations  1.38 us (1%)
    all_to_all x1, blocking collectives, exchange(): lax.all_to_all(pieces, 'chip', split_axis=0, concat_axis=0, tiled=True)  36.6 us
    all_to_all x1, blocking collectives, all_pairs(): lax.all_to_all(array, ('chip', 'core'), split_axis=0, concat_axis=0, tile...  33.3 us
    ppermute x6, waiting for transfers between devices, trade(): return lax.ppermute(array, 'quad', [(i, i ^ flip) for i in range(quads)])  16 us
    all_to_all x1, starting transfers between devices, all_pairs(): lax.all_to_all(array, ('chip', 'core'), split_axis=0, concat_axis=0, tile...  11.8 us
    all_to_all x1, waiting for transfers between devices, all_pairs(): lax.all_to_all(array, ('chip', 'core'), split_axis=0, concat_axis=0, tile...  7.72 us
    ppermute x6, starting transfers between devices, trade(): return lax.ppermute(array, 'quad', [(i, i ^ flip) for i in range(quads)])  6.55 us
    pallas_call x2, Pallas kernels, score(): pl.pallas_call(functools.partial(score_kernel, image_rows, multiplier, pa...  4.06 us
  transfers between devices with their start and end apart: 8, of which 6 were waited for; matrix products, arithmetic and copies ran while one was open for 0% of the time, Pallas kernels for 5%

profile of v4, /device:TPU:40, one launch (start us, length us, event | category | flops | bytes accessed | tf_op | source)
XLA Modules:
  0.0 126.5 jit_solution(11334836082371446021)
XLA Ops:
  0.0 0.0 collective-permute-start
  0.7 1.4 %shard_map.55 = s32[64,1,128]{2,1,0:T(1,128)} custom-call(s32[1024]{0:T(1024)} %image_slot.1, s32[10]{0:T(128)} %group_images.1, s32[2]{0:T(128)} %pair_target.1, s32[1]{0:T(128)} %copy.59.pair_count), custom_call_target="tpu_custom_call" | custom-call | tf_op jit(solution)/shard_map/pallas_call | solution.py:36
  2.0 11.8 %all-to-all-start.9 = ((s32[64,1,128]{2,1,0:T(1,128)}), s32[64,1,128]{2,1,0:T(1,128)S(1)}, u32[]{:S(2)}, u32[]{:S(2)}) async-start(s32[64,1,128]{2,1,0:T(1,128)} %shard_map.55), calls=%async_computation.9 | async-start | bytes 65536 | tf_op jit(solution)/shard_map/all_to_all | solution.py:296
  13.8 7.7 %all-to-all-done.9 = s32[64,1,128]{2,1,0:T(1,128)S(1)} async-done(((s32[64,1,128]{2,1,0:T(1,128)}), s32[64,1,128]{2,1,0:T(1,128)S(1)}, u32[]{:S(2)}, u32[]{:S(2)}) %all-to-all-start.9) | async-done | bytes 32800 | tf_op jit(solution)/shard_map/all_to_all | solution.py:296
  21.5 0.0 copy-start
  21.5 0.6 copy-done
  22.1 1.7 %shard_map.56 = (s32[8,64]{1,0:T(8,128)S(1)}, s32[8,128]{1,0:T(8,128)S(1)}, s32[1]{0:T(128)}) custom-call(s32[1]{0:T(128)} %bitcast.12.chip, s32[64,128]{1,0:T(8,128)} %bitcast.78), custom_call_target="tpu_custom_call" | custom-call | tf_op jit(solution)/shard_map/pallas_call | solution.py:85
  24.5 0.0 collective-permute-done
  24.5 40.1 %conditional.1 = (bf16[64,4,8,256]{3,2,1,0:T(8,128)(2,1)S(1)}) conditional(s32[]{:T(128)} %bitcast.14, (s32[]{:T(128)}, s32[8,128]{1,0:T(8,128)S(1)}, bf16[16,2,32,8,256]{4,3,2,1,0:T(8,128)(2,1)}, bf16[16,2,32,8,256]{4,3,2,1,0:T(8,128)(2,1)}, s32[8,64]{1,0:T(8,128)S(1)}) %tuple.56, (s32[]{:T(128)}, ...), branch_computations={%region_0.0_spmd, %region_1.0_spmd, %region_2.0_spmd, %region_3.0_... | conditional | bytes 8388616 | solution.py:312
  24.6 2.0 %branch_3_fun.2 = bf16[32,9,8,256]{3,2,1,0:T(8,128)(2,1)S(1)} custom-call(s32[1]{0:T(128)} %bitcast.3.core, s32[8,128]{1,0:T(8,128)S(1)} %get-tuple-element.122.rows, bf16[16,2,32,8,256]{4,3,2,1,0:T(8,128)(2,1)} %get-tuple-element.123.own, bf16[16,2,32,8,256]{4,3,2,1,0:T(8,128)(2,1)} %get-tuple-element.124.other), custom_call_target="tpu_custom_call" | custom-call | tf_op jit(solution)/shard_map/cond/branch_3_fun/pallas_call | solution.py:119
  26.6 36.6 %all_to_all.49.spread = bf16[32,9,8,256]{3,2,1,0:T(8,128)(2,1)S(1)} all-to-all(bf16[32,9,8,256]{3,2,1,0:T(8,128)(2,1)S(1)} %branch_3_fun.2), channel_id=1, replica_groups=mesh['chip'=32,'core'=2,'quad'=4] {'chip'}, dimensions={0} | all-to-all | bytes 2359296 | tf_op jit(solution)/shard_map/cond/branch_3_fun/all_to_all | solution.py:309
  63.2 1.3 %branch_3_fun.3 = bf16[64,4,8,256]{3,2,1,0:T(8,128)(2,1)S(1)} custom-call(s32[8,64]{1,0:T(8,128)S(1)} %get-tuple-element.120.index, bf16[32,9,8,256]{3,2,1,0:T(8,128)(2,1)S(1)} %all_to_all.49.spread), custom_call_target="tpu_custom_call" | custom-call | tf_op jit(solution)/shard_map/cond/branch_3_fun/pallas_call | solution.py:142
  64.6 33.3 %all_to_all.55 = bf16[64,4,8,256]{3,2,1,0:T(8,128)(2,1)S(1)} all-to-all(bf16[64,4,8,256]{3,2,1,0:T(8,128)(2,1)S(1)} %get-tuple-element.191), channel_id=1, replica_groups=mesh['chip'=32,'core'=2,'quad'=4] {'chip','core'}, dimensions={0} | all-to-all | bytes 2097152 | tf_op jit(solution)/shard_map/all_to_all | solution.py:296
  97.9 0.1 fusion.11
  98.0 2.8 %collective-permute-start.2 = (bf16[32,2,1,8,256]{4,3,2,1,0:T(8,128)(2,1)S(1)}, bf16[32,2,1,8,256]{4,3,2,1,0:T(8,128)(2,1)S(1)}, u32[]{:S(2)}, u32[]{:S(2)}) collective-permute-start(bf16[32,2,1,8,256]{4,3,2,1,0:T(8,128)(2,1)S(1)} %get-tuple-element.180), channel_id=1, source_target_pairs={{0,3},{1,2},{2,1},{3,0},{4,7},{5,6},{6,5},{7,4},{8,11},{9,10},{10,... | collective-permute-start | bytes 786440 | tf_op jit(solution)/shard_map/ppermute | solution.py:320
  100.8 0.2 collective-permute-start.1
  101.1 1.1 collective-permute-start.4
  102.2 0.7 collective-permute-start.3
  102.9 0.1 pad_add_fusion.meta
  103.0 5.6 %collective-permute-done.2.near_target = bf16[32,2,1,8,256]{4,3,2,1,0:T(8,128)(2,1)S(1)} collective-permute-done((bf16[32,2,1,8,256]{4,3,2,1,0:T(8,128)(2,1)S(1)}, bf16[32,2,1,8,256]{4,3,2,1,0:T(8,128)(2,1)S(1)}, u32[]{:S(2)}, u32[]{:S(2)}) %collective-permute-start.2) | collective-permute-done | bytes 262176 | tf_op jit(solution)/shard_map/ppermute | solution.py:320
  108.5 1.6 %collective-permute-done.1.near_query = bf16[32,2,1,8,256]{4,3,2,1,0:T(8,128)(2,1)S(1)} collective-permute-done((bf16[32,2,1,8,256]{4,3,2,1,0:T(8,128)(2,1)S(1)}, bf16[32,2,1,8,256]{4,3,2,1,0:T(8,128)(2,1)S(1)}, u32[]{:S(2)}, u32[]{:S(2)}) %collective-permute-start.1) | collective-permute-done | bytes 262176 | tf_op jit(solution)/shard_map/ppermute | solution.py:320
  110.1 3.5 %shard_map.57 = (f32[1024,1024]{1,0:T(8,128)S(1)}, f32[8,1024]{1,0:T(8,128)S(1)}, f32[1,8,1024]{2,1,0:T(8,128)S(1)}) custom-call(s32[4]{0:T(128)S(1)} %pad_add_fusion.meta, bf16[32,2,4,8,256]{4,3,2,1,0:T(8,128)(2,1)S(1)} %bitcast.66, bf16[32,2,1,8,256]{4,3,2,1,0:T(8,128)(2,1)S(1)} %collective-permute-done.1.near_query, ...), custom_call_target="tpu_custom_call" | custom-call | flops 536870912 | bytes 2097152 | tf_op jit(solution)/shard_map/pallas_call | solution.py:221
  113.6 0.0 collective-permute-done.4.near_target
  113.6 0.3 collective-permute-done.3.near_query
  113.9 0.5 shard_map.58
  114.5 1.6 %collective-permute-start.5 = (f32[2,8,1024]{2,1,0:T(8,128)S(1)}, f32[2,8,1024]{2,1,0:T(8,128)S(1)}, u32[]{:S(2)}, u32[]{:S(2)}) collective-permute-start(f32[2,8,1024]{2,1,0:T(8,128)S(1)} %get-tuple-element.169.refs_4_), channel_id=1, source_target_pairs={{0,3},{1,2},{2,1},{3,0},{4,7},{5,6},{6,5},{7,4},{8,11},{9,10},{10,... | collective-permute-start | bytes 196616 | tf_op jit(solution)/shard_map/ppermute | solution.py:320
  116.1 4.6 %collective-permute-done.5.refs_5_ = f32[2,8,1024]{2,1,0:T(8,128)S(1)} collective-permute-done((f32[2,8,1024]{2,1,0:T(8,128)S(1)}, f32[2,8,1024]{2,1,0:T(8,128)S(1)}, u32[]{:S(2)}, u32[]{:S(2)}) %collective-permute-start.5) | collective-permute-done | bytes 65568 | tf_op jit(solution)/shard_map/ppermute | solution.py:320
  120.7 1.1 shard_map.59
  121.7 0.1 collective-permute-start.6
  121.9 3.9 %collective-permute-done.6 = f32[2,8,512]{2,1,0:T(8,128)S(1)} collective-permute-done((f32[2,8,512]{2,1,0:T(8,128)S(1)}, f32[2,8,512]{2,1,0:T(8,128)S(1)}, u32[]{:S(2)}, u32[]{:S(2)}) %collective-permute-start.6) | collective-permute-done | bytes 32800 | tf_op jit(solution)/shard_map/ppermute | solution.py:320
  125.9 0.7 fusion
  (4 shorter events, 0.1 us)
Async XLA Ops:
  0.0 24.5 %collective-permute-start = (bf16[16,512,256]{2,1,0:T(8,128)(2,1)}, bf16[16,512,256]{2,1,0:T(8,128)(2,1)}, u32[]{:S(2)}, u32[]{:S(2)}) collective-permute-start(bf16[16,512,256]{2,1,0:T(8,128)(2,1)} %param.14), channel_id=1, source_target_pairs={{0,4},{4,0},{1,5},{5,1},{2,6},{6,2},{3,7},{7,3},{8,12},{12,8},{9,1... | collective-permute-start | bytes 12582920 | tf_op jit(solution)/shard_map/ppermute | solution.py:298
  2.0 19.5 %all-to-all-start.9 = ((s32[64,1,128]{2,1,0:T(1,128)}), s32[64,1,128]{2,1,0:T(1,128)S(1)}, u32[]{:S(2)}, u32[]{:S(2)}) async-start(s32[64,1,128]{2,1,0:T(1,128)} %shard_map.55), calls=%async_computation.9 | async-start | bytes 65536 | tf_op jit(solution)/shard_map/all_to_all | solution.py:296
  21.5 0.6 copy-start
  98.0 10.5 %collective-permute-start.2 = (bf16[32,2,1,8,256]{4,3,2,1,0:T(8,128)(2,1)S(1)}, bf16[32,2,1,8,256]{4,3,2,1,0:T(8,128)(2,1)S(1)}, u32[]{:S(2)}, u32[]{:S(2)}) collective-permute-start(bf16[32,2,1,8,256]{4,3,2,1,0:T(8,128)(2,1)S(1)} %get-tuple-element.180), channel_id=1, source_target_pairs={{0,3},{1,2},{2,1},{3,0},{4,7},{5,6},{6,5},{7,4},{8,11},{9,10},{10,... | collective-permute-start | bytes 786440 | tf_op jit(solution)/shard_map/ppermute | solution.py:320
  100.8 9.2 %collective-permute-start.1 = (bf16[32,2,1,8,256]{4,3,2,1,0:T(8,128)(2,1)S(1)}, bf16[32,2,1,8,256]{4,3,2,1,0:T(8,128)(2,1)S(1)}, u32[]{:S(2)}, u32[]{:S(2)}) collective-permute-start(bf16[32,2,1,8,256]{4,3,2,1,0:T(8,128)(2,1)S(1)} %get-tuple-element.181), channel_id=1, source_target_pairs={{0,1},{1,0},{2,3},{3,2},{4,5},{5,4},{6,7},{7,6},{8,9},{9,8},{10,11... | collective-permute-start | bytes 786440 | tf_op jit(solution)/shard_map/ppermute | solution.py:320
  101.1 12.5 %collective-permute-start.4 = (bf16[32,2,1,8,256]{4,3,2,1,0:T(8,128)(2,1)S(1)}, bf16[32,2,1,8,256]{4,3,2,1,0:T(8,128)(2,1)S(1)}, u32[]{:S(2)}, u32[]{:S(2)}) collective-permute-start(bf16[32,2,1,8,256]{4,3,2,1,0:T(8,128)(2,1)S(1)} %get-tuple-element.178), channel_id=1, source_target_pairs={{0,3},{1,2},{2,1},{3,0},{4,7},{5,6},{6,5},{7,4},{8,11},{9,10},{10,... | collective-permute-start | bytes 786440 | tf_op jit(solution)/shard_map/ppermute | solution.py:320
  102.2 11.7 %collective-permute-start.3 = (bf16[32,2,1,8,256]{4,3,2,1,0:T(8,128)(2,1)S(1)}, bf16[32,2,1,8,256]{4,3,2,1,0:T(8,128)(2,1)S(1)}, u32[]{:S(2)}, u32[]{:S(2)}) collective-permute-start(bf16[32,2,1,8,256]{4,3,2,1,0:T(8,128)(2,1)S(1)} %get-tuple-element.179), channel_id=1, source_target_pairs={{0,1},{1,0},{2,3},{3,2},{4,5},{5,4},{6,7},{7,6},{8,9},{9,8},{10,11... | collective-permute-start | bytes 786440 | tf_op jit(solution)/shard_map/ppermute | solution.py:320
  114.5 6.2 %collective-permute-start.5 = (f32[2,8,1024]{2,1,0:T(8,128)S(1)}, f32[2,8,1024]{2,1,0:T(8,128)S(1)}, u32[]{:S(2)}, u32[]{:S(2)}) collective-permute-start(f32[2,8,1024]{2,1,0:T(8,128)S(1)} %get-tuple-element.169.refs_4_), channel_id=1, source_target_pairs={{0,3},{1,2},{2,1},{3,0},{4,7},{5,6},{6,5},{7,4},{8,11},{9,10},{10,... | collective-permute-start | bytes 196616 | tf_op jit(solution)/shard_map/ppermute | solution.py:320
  121.7 4.0 %collective-permute-start.6 = (f32[2,8,512]{2,1,0:T(8,128)S(1)}, f32[2,8,512]{2,1,0:T(8,128)S(1)}, u32[]{:S(2)}, u32[]{:S(2)}) collective-permute-start(f32[2,8,512]{2,1,0:T(8,128)S(1)} %get-tuple-element.171), channel_id=1, source_target_pairs={{0,1},{1,0},{2,3},{3,2},{4,5},{5,4},{6,7},{7,6},{8,9},{9,8},{10,11... | collective-permute-start | bytes 98312 | tf_op jit(solution)/shard_map/ppermute | solution.py:320

commit v5 on v4

--- a/solution.py
+++ b/solution.py
@@ -148,8 +148,8 @@
     )(index, spread)
 
 
-def score_kernel(image_rows, multiplier, pair, meta, maps, near_query, near_target, *refs):
-    *earlier, products, rows, columns, scores, stats = refs
+def columns_kernel(multiplier, pair, meta, maps, near_query, near_target, *refs):
+    *earlier, scores, powers, columns, stats = refs
     for previous in earlier:
         columns[0:pair] = previous[...]
     chips, cores, entries, piece, width = maps.shape
@@ -174,35 +174,53 @@
                 )
 
         first_lane = lax.broadcasted_iota(jnp.int32, (64, LANES), 1) == 0
-
-        def rows_step(index, carry):
-            block = pl.ds(pl.multiple_of(index * 64, 64), 64)
+        for start in range(0, 2 * slab, 64):
+            block = slice(start, start + 64)
             top = jnp.max(scores[block, :], axis=1, keepdims=True)
-            powers = jnp.exp(scores[block, :] - top)
-            products[block, :] = powers
-            stats[block, :] = jnp.where(first_lane, top, jnp.sum(powers, axis=1, keepdims=True))
-            return carry
-
-        lax.fori_loop(0, 2 * slab // 64, rows_step, 0, unroll=16)
+            exponentials = jnp.exp(scores[block, :] - top)
+            powers[block, :] = exponentials
+            stats[block, :] = jnp.where(first_lane, top, jnp.sum(exponentials, axis=1, keepdims=True))
         for start in range(0, 2 * slab, LANES):
             columns[pair, :, start : start + LANES] = stats[start : start + LANES, :].T[0:8, :]
 
-        bands = slab // IMG_W
+
+def score_columns(multiplier, pair, meta, maps, near_query, near_target, earlier):
+    chips, cores, _, piece, width = maps.shape
+    tokens = 2 * chips * cores * piece
+    square = jax.ShapeDtypeStruct((tokens, tokens), jnp.float32)
+    return pl.pallas_call(
+        functools.partial(columns_kernel, multiplier, pair),
+        in_specs=[SMEM] + [VMEM] * (3 + len(earlier)),
+        out_specs=[VMEM] * 3,
+        out_shape=[square, square, jax.ShapeDtypeStruct((pair + 1, 8, tokens), jnp.float32)],
+        scratch_shapes=[pltpu.VMEM((tokens, LANES), jnp.float32)],
+        compiler_params=pltpu.CompilerParams(vmem_limit_bytes=16 * 1024 * 1024),
+        cost_estimate=pl.CostEstimate(
+            flops=2 * tokens * tokens * width, bytes_accessed=2 << 20, transcendentals=1 << 20
+        ),
+    )(meta, maps, near_query, near_target, *earlier)
+
+
+def rows_kernel(image_rows, pair, meta, scores, powers, products, rows):
+    tokens = scores.shape[0]
+    bands = tokens // (2 * IMG_W)
+
+    @pl.when(pair < meta[1])
+    def _():
         along = lax.broadcasted_iota(jnp.int32, (IMG_W, LANES), 0).astype(jnp.float32)
         coord_x = (2.0 * along + 1.0) / IMG_W - 1.0
-
-        def lanes_step(index, carry):
-            lanes = pl.ds(pl.multiple_of(index * LANES, LANES), LANES)
+        for start in range(0, tokens, LANES):
+            lanes = slice(start, start + LANES)
             top = jnp.max(scores[:, lanes], axis=0, keepdims=True)
             total = jnp.zeros((8, LANES), jnp.float32)
             weighted_y = jnp.zeros((8, LANES), jnp.float32)
             folded = jnp.zeros((IMG_W, LANES), jnp.float32)
             for band in range(2 * bands):
                 block = slice(band * IMG_W, (band + 1) * IMG_W)
-                powers = jnp.exp(scores[block, lanes] - top)
-                products[block, lanes] *= powers
-                folded += powers
-                sums = jnp.sum(powers.reshape(IMG_W // 8, 8, LANES), axis=0)
+                exponentials = jnp.exp(scores[block, lanes] - top)
+                products[block, lanes] = powers[block, lanes] * exponentials
+                folded += exponentials
+                sums = jnp.sum(exponentials.reshape(IMG_W // 8, 8, LANES), axis=0)
                 total += sums
                 image_row = meta[2 + band // bands] * bands + band % bands
                 weighted_y += sums * ((2.0 * image_row.astype(jnp.float32) + 1.0) / image_rows - 1.0)
@@ -210,29 +228,22 @@
             rows[1:2, lanes] = jnp.sum(total, axis=0, keepdims=True)
             rows[2:3, lanes] = jnp.sum(folded * coord_x, axis=0, keepdims=True)
             rows[3:4, lanes] = jnp.sum(weighted_y, axis=0, keepdims=True)
-            return carry
-
-        lax.fori_loop(0, 2 * slab // LANES, lanes_step, 0, unroll=8)
-
-
-def score(image_rows, multiplier, pair, meta, maps, near_query, near_target, earlier):
-    chips, cores, _, piece, width = maps.shape
-    tokens = 2 * chips * cores * piece
-    return pl.pallas_call(
-        functools.partial(score_kernel, image_rows, multiplier, pair),
-        in_specs=[SMEM] + [VMEM] * (3 + len(earlier)),
-        out_specs=[VMEM] * 3,
+
+
+def score_rows(image_rows, pair, meta, scores, powers):
+    tokens = scores.shape[0]
+    return pl.pallas_call(
+        functools.partial(rows_kernel, image_rows, pair),
+        in_specs=[SMEM] + [VMEM] * 2,
+        out_specs=[VMEM] * 2,
         out_shape=[
             jax.ShapeDtypeStruct((tokens, tokens), jnp.float32),
             jax.ShapeDtypeStruct((8, tokens), jnp.float32),
-            jax.ShapeDtypeStruct((pair + 1, 8, tokens), jnp.float32),
         ],
-        scratch_shapes=[pltpu.VMEM((tokens, tokens), jnp.float32), pltpu.VMEM((tokens, LANES), jnp.float32)],
+        input_output_aliases={2: 0},
         compiler_params=pltpu.CompilerParams(vmem_limit_bytes=20 * 1024 * 1024),
-        cost_estimate=pl.CostEstimate(
-            flops=2 * tokens * tokens * width, bytes_accessed=2 << 20, transcendentals=2 << 20
-        ),
-    )(meta, maps, near_query, near_target, *earlier)
+        cost_estimate=pl.CostEstimate(flops=10 << 20, bytes_accessed=8 << 20, transcendentals=1 << 20),
+    )(meta, scores, powers)
 
 
 def mutual_kernel(pairs, meta, *refs):
@@ -321,15 +332,16 @@
 
     query_flip, target_flip = 1, quads - 1
     meta = jnp.stack([quad, pair_count[0], quad, quad ^ target_flip])
-    products, rows, columns = [], [], ()
+    columns, squares = (), []
     for pair in range(pairs):
         near_query = trade(maps[:, :, pair : pair + 1], query_flip)
         near_target = trade(maps[:, :, pairs + pair : pairs + pair + 1], target_flip)
-        product, row, column = score(image_rows, multiplier, pair, meta, maps, near_query, near_target, columns)
-        products.append(product)
-        rows.append(row)
+        scores, powers, column = score_columns(multiplier, pair, meta, maps, near_query, near_target, columns)
+        squares.append((scores, powers))
         columns = (column,)
-    kept, sent = mutual(meta, products, rows, columns[0], trade(columns[0], target_flip))
+    others = trade(columns[0], target_flip)
+    products, rows = zip(*(score_rows(image_rows, pair, meta, *square) for pair, square in enumerate(squares)))
+    kept, sent = mutual(meta, products, rows, columns[0], others)
     partial = jnp.stack([kept, trade(sent, query_flip)])
     top = partial[:, :, 0]
     weight = jnp.exp(top - jnp.max(top, axis=0, keepdims=True))

time: 126 us -> 132 us (1.048)
  Pallas kernels: 11.6 us -> 19.2 us
  waiting for transfers between devices: 23.7 us -> 20.4 us
  blocking collectives: 70 us -> 72.9 us
    pallas_call x2 -> x4, Pallas kernels: 4.06 us -> 11 us  [the longest x2 6.84 us: score_rows(): pl.pallas_call(functools.partial(rows_kernel, image_rows, pair), in_specs...]
    ppermute x6, waiting for transfers between devices: 16 us -> 12.7 us  [trade(): return lax.ppermute(array, 'quad', [(i, i ^ flip) for i in range(quads)])]
    all_to_all x1, blocking collectives: 36.6 us -> 39.2 us  [exchange(): lax.all_to_all(pieces, 'chip', split_axis=0, concat_axis=0, tiled=True)]
  transfers between devices with their start and end apart: 8 -> 8, of which waited for: 6 -> 6; matrix products, arithmetic and copies ran while one was open for 0% -> 0% of each run, Pallas kernels for 5% -> 9%
where the time goes in v5:
time: 132 us; the launch traced here: 134 us
  blocking collectives  72.9 us (55%)
  waiting for transfers between devices  20.4 us (15%)
  Pallas kernels  19.2 us (15%)
  starting transfers between devices  18.3 us (14%)
  between operations  1.38 us (1%)
    all_to_all x1, blocking collectives, exchange(): lax.all_to_all(pieces, 'chip', split_axis=0, concat_axis=0, tiled=True)  39.2 us
    all_to_all x1, blocking collectives, all_pairs(): lax.all_to_all(array, ('chip', 'core'), split_axis=0, concat_axis=0, tile...  33.7 us
    ppermute x6, waiting for transfers between devices, trade(): return lax.ppermute(array, 'quad', [(i, i ^ flip) for i in range(quads)])  12.7 us
    all_to_all x1, starting transfers between devices, all_pairs(): lax.all_to_all(array, ('chip', 'core'), split_axis=0, concat_axis=0, tile...  11.8 us
    all_to_all x1, waiting for transfers between devices, all_pairs(): lax.all_to_all(array, ('chip', 'core'), split_axis=0, concat_axis=0, tile...  7.72 us
    pallas_call x2, Pallas kernels, score_rows(): pl.pallas_call(functools.partial(rows_kernel, image_rows, pair), in_specs...  6.84 us
    ppermute x6, starting transfers between devices, trade(): return lax.ppermute(array, 'quad', [(i, i ^ flip) for i in range(quads)])  6.51 us
    pallas_call x2, Pallas kernels, score_columns(): pl.pallas_call(functools.partial(columns_kernel, multiplier, pair), in_sp...  4.13 us
  transfers between devices with their start and end apart: 8, of which 6 were waited for; matrix products, arithmetic and copies ran while one was open for 0% of the time, Pallas kernels for 9%

profile of v5, /device:TPU:40, one launch (start us, length us, event | category | flops | bytes accessed | tf_op | source)
XLA Modules:
  0.0 133.8 jit_solution(5340646013850010732)
XLA Ops:
  0.0 0.0 collective-permute-start
  0.7 1.4 %shard_map.55 = s32[64,1,128]{2,1,0:T(1,128)} custom-call(s32[1024]{0:T(1024)} %image_slot.1, s32[10]{0:T(128)} %group_images.1, s32[2]{0:T(128)} %pair_target.1, s32[1]{0:T(128)} %copy.63.pair_count), custom_call_target="tpu_custom_call" | custom-call | tf_op jit(solution)/shard_map/pallas_call | solution.py:36
  2.0 11.8 %all-to-all-start.9 = ((s32[64,1,128]{2,1,0:T(1,128)}), s32[64,1,128]{2,1,0:T(1,128)S(1)}, u32[]{:S(2)}, u32[]{:S(2)}) async-start(s32[64,1,128]{2,1,0:T(1,128)} %shard_map.55), calls=%async_computation.9 | async-start | bytes 65536 | tf_op jit(solution)/shard_map/all_to_all | solution.py:307
  13.8 7.7 %all-to-all-done.9 = s32[64,1,128]{2,1,0:T(1,128)S(1)} async-done(((s32[64,1,128]{2,1,0:T(1,128)}), s32[64,1,128]{2,1,0:T(1,128)S(1)}, u32[]{:S(2)}, u32[]{:S(2)}) %all-to-all-start.9) | async-done | bytes 32800 | tf_op jit(solution)/shard_map/all_to_all | solution.py:307
  21.5 0.0 copy-start
  21.5 0.6 copy-done
  22.1 1.7 %shard_map.56 = (s32[8,64]{1,0:T(8,128)S(1)}, s32[8,128]{1,0:T(8,128)S(1)}, s32[1]{0:T(128)}) custom-call(s32[1]{0:T(128)} %bitcast.12.chip, s32[64,128]{1,0:T(8,128)} %bitcast.78), custom_call_target="tpu_custom_call" | custom-call | tf_op jit(solution)/shard_map/pallas_call | solution.py:85
  24.5 0.0 collective-permute-done
  24.5 42.8 %conditional.1 = (bf16[64,4,8,256]{3,2,1,0:T(8,128)(2,1)S(1)}) conditional(s32[]{:T(128)} %bitcast.14, (s32[]{:T(128)}, s32[8,128]{1,0:T(8,128)S(1)}, bf16[16,2,32,8,256]{4,3,2,1,0:T(8,128)(2,1)}, bf16[16,2,32,8,256]{4,3,2,1,0:T(8,128)(2,1)}, s32[8,64]{1,0:T(8,128)S(1)}) %tuple.56, (s32[]{:T(128)}, ...), branch_computations={%region_0.0_spmd, %region_1.0_spmd, %region_2.0_spmd, %region_3.0_... | conditional | bytes 8388616 | solution.py:323
  24.5 2.2 %branch_4_fun.2 = bf16[32,10,8,256]{3,2,1,0:T(8,128)(2,1)S(1)} custom-call(s32[1]{0:T(128)} %bitcast.4.core, s32[8,128]{1,0:T(8,128)S(1)} %get-tuple-element.127.rows, bf16[16,2,32,8,256]{4,3,2,1,0:T(8,128)(2,1)} %get-tuple-element.128.own, bf16[16,2,32,8,256]{4,3,2,1,0:T(8,128)(2,1)} %get-tuple-element.129.other), custom_call_target="tpu_custom_call" | custom-call | tf_op jit(solution)/shard_map/cond/branch_4_fun/pallas_call | solution.py:119
  26.8 39.2 %all_to_all.50.spread = bf16[32,10,8,256]{3,2,1,0:T(8,128)(2,1)S(1)} all-to-all(bf16[32,10,8,256]{3,2,1,0:T(8,128)(2,1)S(1)} %branch_4_fun.2), channel_id=1, replica_groups=mesh['chip'=32,'core'=2,'quad'=4] {'chip'}, dimensions={0} | all-to-all | bytes 2621440 | tf_op jit(solution)/shard_map/cond/branch_4_fun/all_to_all | solution.py:320
  66.0 1.3 %branch_4_fun.3 = bf16[64,4,8,256]{3,2,1,0:T(8,128)(2,1)S(1)} custom-call(s32[8,64]{1,0:T(8,128)S(1)} %get-tuple-element.125.index, bf16[32,10,8,256]{3,2,1,0:T(8,128)(2,1)S(1)} %all_to_all.50.spread), custom_call_target="tpu_custom_call" | custom-call | tf_op jit(solution)/shard_map/cond/branch_4_fun/pallas_call | solution.py:142
  67.4 33.7 %all_to_all.55 = bf16[64,4,8,256]{3,2,1,0:T(8,128)(2,1)S(1)} all-to-all(bf16[64,4,8,256]{3,2,1,0:T(8,128)(2,1)S(1)} %get-tuple-element.199), channel_id=1, replica_groups=mesh['chip'=32,'core'=2,'quad'=4] {'chip','core'}, dimensions={0} | all-to-all | bytes 2097152 | tf_op jit(solution)/shard_map/all_to_all | solution.py:307
  101.0 0.1 fusion.11
  101.1 2.8 %collective-permute-start.2 = (bf16[32,2,1,8,256]{4,3,2,1,0:T(8,128)(2,1)S(1)}, bf16[32,2,1,8,256]{4,3,2,1,0:T(8,128)(2,1)S(1)}, u32[]{:S(2)}, u32[]{:S(2)}) collective-permute-start(bf16[32,2,1,8,256]{4,3,2,1,0:T(8,128)(2,1)S(1)} %get-tuple-element.188), channel_id=1, source_target_pairs={{0,3},{1,2},{2,1},{3,0},{4,7},{5,6},{6,5},{7,4},{8,11},{9,10},{10,... | collective-permute-start | bytes 786440 | tf_op jit(solution)/shard_map/ppermute | solution.py:331
  104.0 0.2 collective-permute-start.1
  104.2 1.1 collective-permute-start.4
  105.3 0.7 collective-permute-start.3
  106.0 0.1 pad_add_fusion.meta
  106.1 5.6 %collective-permute-done.2.near_target = bf16[32,2,1,8,256]{4,3,2,1,0:T(8,128)(2,1)S(1)} collective-permute-done((bf16[32,2,1,8,256]{4,3,2,1,0:T(8,128)(2,1)S(1)}, bf16[32,2,1,8,256]{4,3,2,1,0:T(8,128)(2,1)S(1)}, u32[]{:S(2)}, u32[]{:S(2)}) %collective-permute-start.2) | collective-permute-done | bytes 262176 | tf_op jit(solution)/shard_map/ppermute | solution.py:331
  111.7 1.6 %collective-permute-done.1.near_query = bf16[32,2,1,8,256]{4,3,2,1,0:T(8,128)(2,1)S(1)} collective-permute-done((bf16[32,2,1,8,256]{4,3,2,1,0:T(8,128)(2,1)S(1)}, bf16[32,2,1,8,256]{4,3,2,1,0:T(8,128)(2,1)S(1)}, u32[]{:S(2)}, u32[]{:S(2)}) %collective-permute-start.1) | collective-permute-done | bytes 262176 | tf_op jit(solution)/shard_map/ppermute | solution.py:331
  113.2 2.2 %shard_map.57 = (f32[1024,1024]{1,0:T(8,128)S(1)}, f32[1024,1024]{1,0:T(8,128)S(1)}, f32[1,8,1024]{2,1,0:T(8,128)S(1)}) custom-call(s32[4]{0:T(128)S(1)} %pad_add_fusion.meta, bf16[32,2,4,8,256]{4,3,2,1,0:T(8,128)(2,1)S(1)} %bitcast.66, bf16[32,2,1,8,256]{4,3,2,1,0:T(8,128)(2,1)S(1)} %collective-permute-done.1.near_query, ...), custom_call_target="tpu_custom_call" | custom-call | flops 536870912 | bytes 2097152 | tf_op jit(solution)/shard_map/pallas_call | solution.py:191
  115.4 0.4 collective-permute-done.4.near_target
  115.8 1.3 collective-permute-done.3.near_query
  117.0 2.0 %shard_map.59 = (f32[1024,1024]{1,0:T(8,128)S(1)}, f32[1024,1024]{1,0:T(8,128)S(1)}, f32[2,8,1024]{2,1,0:T(8,128)S(1)}) custom-call(s32[4]{0:T(128)S(1)} %pad_add_fusion.meta, bf16[32,2,4,8,256]{4,3,2,1,0:T(8,128)(2,1)S(1)} %bitcast.67, bf16[32,2,1,8,256]{4,3,2,1,0:T(8,128)(2,1)S(1)} %collective-permute-done.3.near_query, ...), custom_call_target="tpu_custom_call" | custom-call | flops 536870912 | bytes 2097152 | tf_op jit(solution)/shard_map/pallas_call | solution.py:191
  119.0 1.5 %collective-permute-start.5 = (f32[2,8,1024]{2,1,0:T(8,128)S(1)}, f32[2,8,1024]{2,1,0:T(8,128)S(1)}, u32[]{:S(2)}, u32[]{:S(2)}) collective-permute-start(f32[2,8,1024]{2,1,0:T(8,128)S(1)} %get-tuple-element.177.refs_4_), channel_id=1, source_target_pairs={{0,3},{1,2},{2,1},{3,0},{4,7},{5,6},{6,5},{7,4},{8,11},{9,10},{10,... | collective-permute-start | bytes 196616 | tf_op jit(solution)/shard_map/ppermute | solution.py:331
  120.6 3.4 %shard_map.58 = (f32[1024,1024]{1,0:T(8,128)S(1)}, f32[8,1024]{1,0:T(8,128)S(1)}) custom-call(s32[4]{0:T(128)S(1)} %pad_add_fusion.meta, f32[1024,1024]{1,0:T(8,128)S(1)} %get-tuple-element.168.scores, f32[1024,1024]{1,0:T(8,128)S(1)} %get-tuple-element.169.powers), custom_call_target="tpu_custom_call", output_to_operand_aliasing={{0}: (2, {})} | custom-call | flops 10485760 | bytes 8388608 | tf_op jit(solution)/shard_map/pallas_call | solution.py:235
  124.0 3.4 %shard_map.60 = (f32[1024,1024]{1,0:T(8,128)S(1)}, f32[8,1024]{1,0:T(8,128)S(1)}) custom-call(s32[4]{0:T(128)S(1)} %pad_add_fusion.meta, f32[1024,1024]{1,0:T(8,128)S(1)} %get-tuple-element.172.scores, f32[1024,1024]{1,0:T(8,128)S(1)} %get-tuple-element.173.powers), custom_call_target="tpu_custom_call", output_to_operand_aliasing={{0}: (2, {})} | custom-call | flops 10485760 | bytes 8388608 | tf_op jit(solution)/shard_map/pallas_call | solution.py:235
  127.4 0.0 collective-permute-done.5.refs_5_
  127.4 1.6 %shard_map.61 = (f32[2,8,512]{2,1,0:T(8,128)S(1)}, f32[2,8,512]{2,1,0:T(8,128)S(1)}) custom-call(s32[4]{0:T(128)S(1)} %pad_add_fusion.meta, f32[1024,1024]{1,0:T(8,128)S(1)} %get-tuple-element.170.refs_0_, f32[1024,1024]{1,0:T(8,128)S(1)} %get-tuple-element.174.refs_1_, f32[8,1024]{1,0:T(8,128)S(1)} %get-tuple-element.175.refs_2_, ...), custom_call_target="tpu_custom_call" | custom-call | tf_op jit(solution)/shard_map/pallas_call | solution.py:282
  129.0 0.1 collective-permute-start.6
  129.1 3.9 %collective-permute-done.6 = f32[2,8,512]{2,1,0:T(8,128)S(1)} collective-permute-done((f32[2,8,512]{2,1,0:T(8,128)S(1)}, f32[2,8,512]{2,1,0:T(8,128)S(1)}, u32[]{:S(2)}, u32[]{:S(2)}) %collective-permute-start.6) | collective-permute-done | bytes 32800 | tf_op jit(solution)/shard_map/ppermute | solution.py:331
  133.1 0.7 fusion
  (4 shorter events, 0.1 us)
Async XLA Ops:
  0.0 24.5 %collective-permute-start = (bf16[16,512,256]{2,1,0:T(8,128)(2,1)}, bf16[16,512,256]{2,1,0:T(8,128)(2,1)}, u32[]{:S(2)}, u32[]{:S(2)}) collective-permute-start(bf16[16,512,256]{2,1,0:T(8,128)(2,1)} %param.14), channel_id=1, source_target_pairs={{0,4},{4,0},{1,5},{5,1},{2,6},{6,2},{3,7},{7,3},{8,12},{12,8},{9,1... | collective-permute-start | bytes 12582920 | tf_op jit(solution)/shard_map/ppermute | solution.py:309
  2.0 19.5 %all-to-all-start.9 = ((s32[64,1,128]{2,1,0:T(1,128)}), s32[64,1,128]{2,1,0:T(1,128)S(1)}, u32[]{:S(2)}, u32[]{:S(2)}) async-start(s32[64,1,128]{2,1,0:T(1,128)} %shard_map.55), calls=%async_computation.9 | async-start | bytes 65536 | tf_op jit(solution)/shard_map/all_to_all | solution.py:307
  21.5 0.6 copy-start
  101.1 10.5 %collective-permute-start.2 = (bf16[32,2,1,8,256]{4,3,2,1,0:T(8,128)(2,1)S(1)}, bf16[32,2,1,8,256]{4,3,2,1,0:T(8,128)(2,1)S(1)}, u32[]{:S(2)}, u32[]{:S(2)}) collective-permute-start(bf16[32,2,1,8,256]{4,3,2,1,0:T(8,128)(2,1)S(1)} %get-tuple-element.188), channel_id=1, source_target_pairs={{0,3},{1,2},{2,1},{3,0},{4,7},{5,6},{6,5},{7,4},{8,11},{9,10},{10,... | collective-permute-start | bytes 786440 | tf_op jit(solution)/shard_map/ppermute | solution.py:331
  104.0 9.2 %collective-permute-start.1 = (bf16[32,2,1,8,256]{4,3,2,1,0:T(8,128)(2,1)S(1)}, bf16[32,2,1,8,256]{4,3,2,1,0:T(8,128)(2,1)S(1)}, u32[]{:S(2)}, u32[]{:S(2)}) collective-permute-start(bf16[32,2,1,8,256]{4,3,2,1,0:T(8,128)(2,1)S(1)} %get-tuple-element.189), channel_id=1, source_target_pairs={{0,1},{1,0},{2,3},{3,2},{4,5},{5,4},{6,7},{7,6},{8,9},{9,8},{10,11... | collective-permute-start | bytes 786440 | tf_op jit(solution)/shard_map/ppermute | solution.py:331
  104.2 11.6 %collective-permute-start.4 = (bf16[32,2,1,8,256]{4,3,2,1,0:T(8,128)(2,1)S(1)}, bf16[32,2,1,8,256]{4,3,2,1,0:T(8,128)(2,1)S(1)}, u32[]{:S(2)}, u32[]{:S(2)}) collective-permute-start(bf16[32,2,1,8,256]{4,3,2,1,0:T(8,128)(2,1)S(1)} %get-tuple-element.186), channel_id=1, source_target_pairs={{0,3},{1,2},{2,1},{3,0},{4,7},{5,6},{6,5},{7,4},{8,11},{9,10},{10,... | collective-permute-start | bytes 786440 | tf_op jit(solution)/shard_map/ppermute | solution.py:331
  105.3 11.7 %collective-permute-start.3 = (bf16[32,2,1,8,256]{4,3,2,1,0:T(8,128)(2,1)S(1)}, bf16[32,2,1,8,256]{4,3,2,1,0:T(8,128)(2,1)S(1)}, u32[]{:S(2)}, u32[]{:S(2)}) collective-permute-start(bf16[32,2,1,8,256]{4,3,2,1,0:T(8,128)(2,1)S(1)} %get-tuple-element.187), channel_id=1, source_target_pairs={{0,1},{1,0},{2,3},{3,2},{4,5},{5,4},{6,7},{7,6},{8,9},{9,8},{10,11... | collective-permute-start | bytes 786440 | tf_op jit(solution)/shard_map/ppermute | solution.py:331
  119.0 8.4 %collective-permute-start.5 = (f32[2,8,1024]{2,1,0:T(8,128)S(1)}, f32[2,8,1024]{2,1,0:T(8,128)S(1)}, u32[]{:S(2)}, u32[]{:S(2)}) collective-permute-start(f32[2,8,1024]{2,1,0:T(8,128)S(1)} %get-tuple-element.177.refs_4_), channel_id=1, source_target_pairs={{0,3},{1,2},{2,1},{3,0},{4,7},{5,6},{6,5},{7,4},{8,11},{9,10},{10,... | collective-permute-start | bytes 196616 | tf_op jit(solution)/shard_map/ppermute | solution.py:331
  129.0 4.0 %collective-permute-start.6 = (f32[2,8,512]{2,1,0:T(8,128)S(1)}, f32[2,8,512]{2,1,0:T(8,128)S(1)}, u32[]{:S(2)}, u32[]{:S(2)}) collective-permute-start(f32[2,8,512]{2,1,0:T(8,128)S(1)} %get-tuple-element.179), channel_id=1, source_target_pairs={{0,1},{1,0},{2,3},{3,2},{4,5},{5,4},{6,7},{7,6},{8,9},{9,8},{10,11... | collective-permute-start | bytes 98312 | tf_op jit(solution)/shard_map/ppermute | solution.py:331

commit v6 on v5

--- a/solution.py
+++ b/solution.py
@@ -240,8 +240,7 @@
             jax.ShapeDtypeStruct((tokens, tokens), jnp.float32),
             jax.ShapeDtypeStruct((8, tokens), jnp.float32),
         ],
-        input_output_aliases={2: 0},
-        compiler_params=pltpu.CompilerParams(vmem_limit_bytes=20 * 1024 * 1024),
+        compiler_params=pltpu.CompilerParams(vmem_limit_bytes=16 * 1024 * 1024),
         cost_estimate=pl.CostEstimate(flops=10 << 20, bytes_accessed=8 << 20, transcendentals=1 << 20),
     )(meta, scores, powers)
 

time: 132 us -> 133 us (level); the launches traced: 134 us -> 133 us
  transfers between devices with their start and end apart: 8 -> 8, of which waited for: 6 -> 6; matrix products, arithmetic and copies ran while one was open for 0% -> 0% of each run, Pallas kernels for 9% -> 8%
where the time goes in v6:
time: 133 us
  blocking collectives  72.4 us (54%)
  waiting for transfers between devices  20.4 us (15%)
  Pallas kernels  18.6 us (14%)
  starting transfers between devices  18.3 us (14%)
  between operations  1.38 us (1%)
    all_to_all x1, blocking collectives, exchange(): lax.all_to_all(pieces, 'chip', split_axis=0, concat_axis=0, tiled=True)  38.8 us
    all_to_all x1, blocking collectives, all_pairs(): lax.all_to_all(array, ('chip', 'core'), split_axis=0, concat_axis=0, tile...  33.7 us
    ppermute x6, waiting for transfers between devices, trade(): return lax.ppermute(array, 'quad', [(i, i ^ flip) for i in range(quads)])  12.7 us
    all_to_all x1, starting transfers between devices, all_pairs(): lax.all_to_all(array, ('chip', 'core'), split_axis=0, concat_axis=0, tile...  11.8 us
    all_to_all x1, waiting for transfers between devices, all_pairs(): lax.all_to_all(array, ('chip', 'core'), split_axis=0, concat_axis=0, tile...  7.72 us
    ppermute x6, starting transfers between devices, trade(): return lax.ppermute(array, 'quad', [(i, i ^ flip) for i in range(quads)])  6.52 us
    pallas_call x2, Pallas kernels, score_rows(): pl.pallas_call(functools.partial(rows_kernel, image_rows, pair), in_specs...  5.99 us
    pallas_call x2, Pallas kernels, score_columns(): pl.pallas_call(functools.partial(columns_kernel, multiplier, pair), in_sp...  4.14 us
  transfers between devices with their start and end apart: 8, of which 6 were waited for; matrix products, arithmetic and copies ran while one was open for 0% of the time, Pallas kernels for 8%

profile of v6, /device:TPU:40, one launch (start us, length us, event | category | flops | bytes accessed | tf_op | source)
XLA Modules:
  0.0 132.7 jit_solution(4084268475743319468)
XLA Ops:
  0.0 0.0 collective-permute-start
  0.7 1.4 %shard_map.55 = s32[64,1,128]{2,1,0:T(1,128)} custom-call(s32[1024]{0:T(1024)} %image_slot.1, s32[10]{0:T(128)} %group_images.1, s32[2]{0:T(128)} %pair_target.1, s32[1]{0:T(128)} %copy.59.pair_count), custom_call_target="tpu_custom_call" | custom-call | tf_op jit(solution)/shard_map/pallas_call | solution.py:36
  2.0 11.8 %all-to-all-start.9 = ((s32[64,1,128]{2,1,0:T(1,128)}), s32[64,1,128]{2,1,0:T(1,128)S(1)}, u32[]{:S(2)}, u32[]{:S(2)}) async-start(s32[64,1,128]{2,1,0:T(1,128)} %shard_map.55), calls=%async_computation.9 | async-start | bytes 65536 | tf_op jit(solution)/shard_map/all_to_all | solution.py:306
  13.8 7.7 %all-to-all-done.9 = s32[64,1,128]{2,1,0:T(1,128)S(1)} async-done(((s32[64,1,128]{2,1,0:T(1,128)}), s32[64,1,128]{2,1,0:T(1,128)S(1)}, u32[]{:S(2)}, u32[]{:S(2)}) %all-to-all-start.9) | async-done | bytes 32800 | tf_op jit(solution)/shard_map/all_to_all | solution.py:306
  21.5 0.0 copy-start
  21.5 0.6 copy-done
  22.1 1.7 %shard_map.56 = (s32[8,64]{1,0:T(8,128)S(1)}, s32[8,128]{1,0:T(8,128)S(1)}, s32[1]{0:T(128)}) custom-call(s32[1]{0:T(128)} %bitcast.12.chip, s32[64,128]{1,0:T(8,128)} %bitcast.78), custom_call_target="tpu_custom_call" | custom-call | tf_op jit(solution)/shard_map/pallas_call | solution.py:85
  24.5 0.0 collective-permute-done
  24.5 42.6 %conditional.1 = (bf16[64,4,8,256]{3,2,1,0:T(8,128)(2,1)S(1)}) conditional(s32[]{:T(128)} %bitcast.14, (s32[]{:T(128)}, s32[8,128]{1,0:T(8,128)S(1)}, bf16[16,2,32,8,256]{4,3,2,1,0:T(8,128)(2,1)}, bf16[16,2,32,8,256]{4,3,2,1,0:T(8,128)(2,1)}, s32[8,64]{1,0:T(8,128)S(1)}) %tuple.56, (s32[]{:T(128)}, ...), branch_computations={%region_0.0_spmd, %region_1.0_spmd, %region_2.0_spmd, %region_3.0_... | conditional | bytes 8388616 | solution.py:322
  24.5 2.4 %branch_4_fun.2 = bf16[32,10,8,256]{3,2,1,0:T(8,128)(2,1)S(1)} custom-call(s32[1]{0:T(128)} %bitcast.4.core, s32[8,128]{1,0:T(8,128)S(1)} %get-tuple-element.127.rows, bf16[16,2,32,8,256]{4,3,2,1,0:T(8,128)(2,1)} %get-tuple-element.128.own, bf16[16,2,32,8,256]{4,3,2,1,0:T(8,128)(2,1)} %get-tuple-element.129.other), custom_call_target="tpu_custom_call" | custom-call | tf_op jit(solution)/shard_map/cond/branch_4_fun/pallas_call | solution.py:119
  27.0 38.8 %all_to_all.50.spread = bf16[32,10,8,256]{3,2,1,0:T(8,128)(2,1)S(1)} all-to-all(bf16[32,10,8,256]{3,2,1,0:T(8,128)(2,1)S(1)} %branch_4_fun.2), channel_id=1, replica_groups=mesh['chip'=32,'core'=2,'quad'=4] {'chip'}, dimensions={0} | all-to-all | bytes 2621440 | tf_op jit(solution)/shard_map/cond/branch_4_fun/all_to_all | solution.py:319
  65.8 1.3 %branch_4_fun.3 = bf16[64,4,8,256]{3,2,1,0:T(8,128)(2,1)S(1)} custom-call(s32[8,64]{1,0:T(8,128)S(1)} %get-tuple-element.125.index, bf16[32,10,8,256]{3,2,1,0:T(8,128)(2,1)S(1)} %all_to_all.50.spread), custom_call_target="tpu_custom_call" | custom-call | tf_op jit(solution)/shard_map/cond/branch_4_fun/pallas_call | solution.py:142
  67.1 33.7 %all_to_all.55 = bf16[64,4,8,256]{3,2,1,0:T(8,128)(2,1)S(1)} all-to-all(bf16[64,4,8,256]{3,2,1,0:T(8,128)(2,1)S(1)} %get-tuple-element.199), channel_id=1, replica_groups=mesh['chip'=32,'core'=2,'quad'=4] {'chip','core'}, dimensions={0} | all-to-all | bytes 2097152 | tf_op jit(solution)/shard_map/all_to_all | solution.py:306
  100.8 0.1 fusion.11
  100.9 2.8 %collective-permute-start.2 = (bf16[32,2,1,8,256]{4,3,2,1,0:T(8,128)(2,1)S(1)}, bf16[32,2,1,8,256]{4,3,2,1,0:T(8,128)(2,1)S(1)}, u32[]{:S(2)}, u32[]{:S(2)}) collective-permute-start(bf16[32,2,1,8,256]{4,3,2,1,0:T(8,128)(2,1)S(1)} %get-tuple-element.188), channel_id=1, source_target_pairs={{0,3},{1,2},{2,1},{3,0},{4,7},{5,6},{6,5},{7,4},{8,11},{9,10},{10,... | collective-permute-start | bytes 786440 | tf_op jit(solution)/shard_map/ppermute | solution.py:330
  103.7 0.2 collective-permute-start.1
  104.0 1.1 collective-permute-start.4
  105.1 0.7 collective-permute-start.3
  105.8 0.1 pad_add_fusion.meta
  105.8 5.6 %collective-permute-done.2.near_target = bf16[32,2,1,8,256]{4,3,2,1,0:T(8,128)(2,1)S(1)} collective-permute-done((bf16[32,2,1,8,256]{4,3,2,1,0:T(8,128)(2,1)S(1)}, bf16[32,2,1,8,256]{4,3,2,1,0:T(8,128)(2,1)S(1)}, u32[]{:S(2)}, u32[]{:S(2)}) %collective-permute-start.2) | collective-permute-done | bytes 262176 | tf_op jit(solution)/shard_map/ppermute | solution.py:330
  111.4 1.6 %collective-permute-done.1.near_query = bf16[32,2,1,8,256]{4,3,2,1,0:T(8,128)(2,1)S(1)} collective-permute-done((bf16[32,2,1,8,256]{4,3,2,1,0:T(8,128)(2,1)S(1)}, bf16[32,2,1,8,256]{4,3,2,1,0:T(8,128)(2,1)S(1)}, u32[]{:S(2)}, u32[]{:S(2)}) %collective-permute-start.1) | collective-permute-done | bytes 262176 | tf_op jit(solution)/shard_map/ppermute | solution.py:330
  113.0 2.2 %shard_map.57 = (f32[1024,1024]{1,0:T(8,128)S(1)}, f32[1024,1024]{1,0:T(8,128)S(1)}, f32[1,8,1024]{2,1,0:T(8,128)S(1)}) custom-call(s32[4]{0:T(128)S(1)} %pad_add_fusion.meta, bf16[32,2,4,8,256]{4,3,2,1,0:T(8,128)(2,1)S(1)} %bitcast.66, bf16[32,2,1,8,256]{4,3,2,1,0:T(8,128)(2,1)S(1)} %collective-permute-done.1.near_query, ...), custom_call_target="tpu_custom_call" | custom-call | flops 536870912 | bytes 2097152 | tf_op jit(solution)/shard_map/pallas_call | solution.py:191
  115.1 0.4 collective-permute-done.4.near_target
  115.5 1.3 collective-permute-done.3.near_query
  116.8 2.0 %shard_map.59 = (f32[1024,1024]{1,0:T(8,128)S(1)}, f32[1024,1024]{1,0:T(8,128)S(1)}, f32[2,8,1024]{2,1,0:T(8,128)S(1)}) custom-call(s32[4]{0:T(128)S(1)} %pad_add_fusion.meta, bf16[32,2,4,8,256]{4,3,2,1,0:T(8,128)(2,1)S(1)} %bitcast.67, bf16[32,2,1,8,256]{4,3,2,1,0:T(8,128)(2,1)S(1)} %collective-permute-done.3.near_query, ...), custom_call_target="tpu_custom_call" | custom-call | flops 536870912 | bytes 2097152 | tf_op jit(solution)/shard_map/pallas_call | solution.py:191
  118.8 1.6 %collective-permute-start.5 = (f32[2,8,1024]{2,1,0:T(8,128)S(1)}, f32[2,8,1024]{2,1,0:T(8,128)S(1)}, u32[]{:S(2)}, u32[]{:S(2)}) collective-permute-start(f32[2,8,1024]{2,1,0:T(8,128)S(1)} %get-tuple-element.177.refs_4_), channel_id=1, source_target_pairs={{0,3},{1,2},{2,1},{3,0},{4,7},{5,6},{6,5},{7,4},{8,11},{9,10},{10,... | collective-permute-start | bytes 196616 | tf_op jit(solution)/shard_map/ppermute | solution.py:330
  120.3 3.0 %shard_map.58 = (f32[1024,1024]{1,0:T(8,128)S(1)}, f32[8,1024]{1,0:T(8,128)S(1)}) custom-call(s32[4]{0:T(128)S(1)} %pad_add_fusion.meta, f32[1024,1024]{1,0:T(8,128)S(1)} %get-tuple-element.168.scores, f32[1024,1024]{1,0:T(8,128)S(1)} %get-tuple-element.169.powers), custom_call_target="tpu_custom_call" | custom-call | flops 10485760 | bytes 8388608 | tf_op jit(solution)/shard_map/pallas_call | solution.py:235
  123.3 3.0 %shard_map.60 = (f32[1024,1024]{1,0:T(8,128)S(1)}, f32[8,1024]{1,0:T(8,128)S(1)}) custom-call(s32[4]{0:T(128)S(1)} %pad_add_fusion.meta, f32[1024,1024]{1,0:T(8,128)S(1)} %get-tuple-element.172.scores, f32[1024,1024]{1,0:T(8,128)S(1)} %get-tuple-element.173.powers), custom_call_target="tpu_custom_call" | custom-call | flops 10485760 | bytes 8388608 | tf_op jit(solution)/shard_map/pallas_call | solution.py:235
  126.3 0.0 collective-permute-done.5.refs_5_
  126.3 1.6 %shard_map.61 = (f32[2,8,512]{2,1,0:T(8,128)S(1)}, f32[2,8,512]{2,1,0:T(8,128)S(1)}) custom-call(s32[4]{0:T(128)S(1)} %pad_add_fusion.meta, f32[1024,1024]{1,0:T(8,128)S(1)} %get-tuple-element.170.refs_0_, f32[1024,1024]{1,0:T(8,128)S(1)} %get-tuple-element.174.refs_1_, f32[8,1024]{1,0:T(8,128)S(1)} %get-tuple-element.175.refs_2_, ...), custom_call_target="tpu_custom_call" | custom-call | tf_op jit(solution)/shard_map/pallas_call | solution.py:281
  127.9 0.1 collective-permute-start.6
  128.0 3.9 %collective-permute-done.6 = f32[2,8,512]{2,1,0:T(8,128)S(1)} collective-permute-done((f32[2,8,512]{2,1,0:T(8,128)S(1)}, f32[2,8,512]{2,1,0:T(8,128)S(1)}, u32[]{:S(2)}, u32[]{:S(2)}) %collective-permute-start.6) | collective-permute-done | bytes 32800 | tf_op jit(solution)/shard_map/ppermute | solution.py:330
  132.0 0.7 fusion
  (4 shorter events, 0.1 us)
Async XLA Ops:
  0.0 24.5 %collective-permute-start = (bf16[16,512,256]{2,1,0:T(8,128)(2,1)}, bf16[16,512,256]{2,1,0:T(8,128)(2,1)}, u32[]{:S(2)}, u32[]{:S(2)}) collective-permute-start(bf16[16,512,256]{2,1,0:T(8,128)(2,1)} %param.14), channel_id=1, source_target_pairs={{0,4},{4,0},{1,5},{5,1},{2,6},{6,2},{3,7},{7,3},{8,12},{12,8},{9,1... | collective-permute-start | bytes 12582920 | tf_op jit(solution)/shard_map/ppermute | solution.py:308
  2.0 19.5 %all-to-all-start.9 = ((s32[64,1,128]{2,1,0:T(1,128)}), s32[64,1,128]{2,1,0:T(1,128)S(1)}, u32[]{:S(2)}, u32[]{:S(2)}) async-start(s32[64,1,128]{2,1,0:T(1,128)} %shard_map.55), calls=%async_computation.9 | async-start | bytes 65536 | tf_op jit(solution)/shard_map/all_to_all | solution.py:306
  21.5 0.6 copy-start
  100.9 10.5 %collective-permute-start.2 = (bf16[32,2,1,8,256]{4,3,2,1,0:T(8,128)(2,1)S(1)}, bf16[32,2,1,8,256]{4,3,2,1,0:T(8,128)(2,1)S(1)}, u32[]{:S(2)}, u32[]{:S(2)}) collective-permute-start(bf16[32,2,1,8,256]{4,3,2,1,0:T(8,128)(2,1)S(1)} %get-tuple-element.188), channel_id=1, source_target_pairs={{0,3},{1,2},{2,1},{3,0},{4,7},{5,6},{6,5},{7,4},{8,11},{9,10},{10,... | collective-permute-start | bytes 786440 | tf_op jit(solution)/shard_map/ppermute | solution.py:330
  103.7 9.2 %collective-permute-start.1 = (bf16[32,2,1,8,256]{4,3,2,1,0:T(8,128)(2,1)S(1)}, bf16[32,2,1,8,256]{4,3,2,1,0:T(8,128)(2,1)S(1)}, u32[]{:S(2)}, u32[]{:S(2)}) collective-permute-start(bf16[32,2,1,8,256]{4,3,2,1,0:T(8,128)(2,1)S(1)} %get-tuple-element.189), channel_id=1, source_target_pairs={{0,1},{1,0},{2,3},{3,2},{4,5},{5,4},{6,7},{7,6},{8,9},{9,8},{10,11... | collective-permute-start | bytes 786440 | tf_op jit(solution)/shard_map/ppermute | solution.py:330
  104.0 11.6 %collective-permute-start.4 = (bf16[32,2,1,8,256]{4,3,2,1,0:T(8,128)(2,1)S(1)}, bf16[32,2,1,8,256]{4,3,2,1,0:T(8,128)(2,1)S(1)}, u32[]{:S(2)}, u32[]{:S(2)}) collective-permute-start(bf16[32,2,1,8,256]{4,3,2,1,0:T(8,128)(2,1)S(1)} %get-tuple-element.186), channel_id=1, source_target_pairs={{0,3},{1,2},{2,1},{3,0},{4,7},{5,6},{6,5},{7,4},{8,11},{9,10},{10,... | collective-permute-start | bytes 786440 | tf_op jit(solution)/shard_map/ppermute | solution.py:330
  105.1 11.7 %collective-permute-start.3 = (bf16[32,2,1,8,256]{4,3,2,1,0:T(8,128)(2,1)S(1)}, bf16[32,2,1,8,256]{4,3,2,1,0:T(8,128)(2,1)S(1)}, u32[]{:S(2)}, u32[]{:S(2)}) collective-permute-start(bf16[32,2,1,8,256]{4,3,2,1,0:T(8,128)(2,1)S(1)} %get-tuple-element.187), channel_id=1, source_target_pairs={{0,1},{1,0},{2,3},{3,2},{4,5},{5,4},{6,7},{7,6},{8,9},{9,8},{10,11... | collective-permute-start | bytes 786440 | tf_op jit(solution)/shard_map/ppermute | solution.py:330
  118.8 7.5 %collective-permute-start.5 = (f32[2,8,1024]{2,1,0:T(8,128)S(1)}, f32[2,8,1024]{2,1,0:T(8,128)S(1)}, u32[]{:S(2)}, u32[]{:S(2)}) collective-permute-start(f32[2,8,1024]{2,1,0:T(8,128)S(1)} %get-tuple-element.177.refs_4_), channel_id=1, source_target_pairs={{0,3},{1,2},{2,1},{3,0},{4,7},{5,6},{6,5},{7,4},{8,11},{9,10},{10,... | collective-permute-start | bytes 196616 | tf_op jit(solution)/shard_map/ppermute | solution.py:330
  127.9 4.0 %collective-permute-start.6 = (f32[2,8,512]{2,1,0:T(8,128)S(1)}, f32[2,8,512]{2,1,0:T(8,128)S(1)}, u32[]{:S(2)}, u32[]{:S(2)}) collective-permute-start(f32[2,8,512]{2,1,0:T(8,128)S(1)} %get-tuple-element.179), channel_id=1, source_target_pairs={{0,1},{1,0},{2,3},{3,2},{4,5},{5,4},{6,7},{7,6},{8,9},{9,8},{10,11... | collective-permute-start | bytes 98312 | tf_op jit(solution)/shard_map/ppermute | solution.py:330
